TPU v7x, 512 devices: a whole 4x4x16 slice. The times are simulated.
512 devices in a mesh: mem: 8 (over z_hi, y), lat: 4 (over x), lon: 16 (over z_lo, core).
Axes of the slice: x: 4, y: 4, z: 16 (z_hi: 2, z_lo: 8; z = z_hi * 8 + z_lo), core: 2. Of those that a mesh axis runs over, the one named last changes fastest.
Arguments:
- members: bfloat16 [128, 8, 1440, 512], P('mem', None, 'lon', 'lat'), may hold values from -6 to 6
- grad_field: float32 [8, 1440, 512], P('mem', 'lon', 'lat'), may hold values from -6 to 6
- static_std: float32 [8, 1440, 512], P(None, 'lon', 'lat'), may hold values from 0.3 to 3
- vert_mix: float32 [8, 8], replicated, may hold values from -2 to 2
- loc_weights: float32 [512, 128], P('lat'), may hold values from 0.25 to 4
Outputs:
- alpha_grad: float32 [1024, 512, 128], P(('mem', 'lon'), 'lat')
- static_grad: float32 [8, 1440, 512], P('mem', 'lon', 'lat')
All inputs are finite; a program needn't handle non-finite values.
Results may differ from a plain program's by a relative error of at most 0.0057.
Values may be sent and summed in bfloat16 or wider, within the bound.
No kernel may reach another device: no remote copies, remote signals or barrier semaphores. Data moves between devices by JAX's collectives and lax.ppermute only.
A program may use at most 64 MiB of HBM per device.

v0:
```python
import jax
import jax.numpy as jnp
from jax import lax
from jax.sharding import PartitionSpec as P

NLON = 1440
NLAT = 512
KLON = 512
KLAT = 128


def lon_table_make(n_lon, k_lon):
    cells = jnp.arange(n_lon, dtype=jnp.int32)[:, None]
    waves = jnp.arange(k_lon // 2, dtype=jnp.int32)[None, :]
    cos_phase = (cells * waves % n_lon).astype(jnp.float32)
    sin_phase = (cells * (waves + 1) % n_lon).astype(jnp.float32)
    factor = jnp.sqrt(jnp.float32(2.0) / n_lon)
    angle_cos = jnp.float32(2.0 * jnp.pi) * cos_phase / n_lon
    angle_sin = jnp.float32(2.0 * jnp.pi) * sin_phase / n_lon
    table = jnp.concatenate([jnp.cos(angle_cos), jnp.sin(angle_sin)], axis=1) * factor
    return table.astype(jnp.bfloat16)


def lat_table_make(first, count, n_lat, k_lat):
    cells = first + jnp.arange(count, dtype=jnp.int32)[:, None]
    waves = jnp.arange(k_lat, dtype=jnp.int32)[None, :]
    phase = ((2 * cells + 1) * waves % (4 * n_lat)).astype(jnp.float32)
    angle = jnp.float32(jnp.pi) * phase / (2 * n_lat)
    return (jnp.cos(angle) * jnp.sqrt(jnp.float32(2.0) / n_lat)).astype(jnp.bfloat16)


def local(members, grad_field, static_std, vert_mix, loc_weights):
    mem_local, levels, lon_local, lat_local = members.shape
    levels_own = grad_field.shape[0]
    whole_grad = lax.all_gather(grad_field, "mem", axis=0, tiled=True)
    product = (members.astype(jnp.float32) * whole_grad[None]).astype(jnp.bfloat16)
    member_rows = product.reshape(mem_local * levels, lon_local, lat_local)
    lon_table = lon_table_make(NLON, KLON)
    zonal = jnp.einsum(
        "rnc,nk->rkc",
        lax.all_to_all(member_rows, "lon", split_axis=0, concat_axis=1, tiled=True),
        lon_table,
        preferred_element_type=jnp.float32,
    ).astype(jnp.bfloat16)
    lat_first = lax.axis_index("lat") * lat_local
    lat_table = lat_table_make(lat_first, lat_local, NLAT, KLAT)
    partial_sums = jnp.einsum("rkc,cq->rkq", zonal, lat_table, preferred_element_type=jnp.float32)
    summed = lax.psum_scatter(partial_sums, "lat", scatter_dimension=1, tiled=True)
    alpha_grad = summed * loc_weights[None]
    level_first = lax.axis_index("mem") * levels_own
    own_mix = lax.dynamic_slice_in_dim(vert_mix, level_first, levels_own, 0)
    own_std = lax.dynamic_slice_in_dim(static_std, level_first, levels_own, 0)
    terms = jnp.einsum(
        "lj,lxy->jxy", own_mix, own_std * grad_field, precision=lax.Precision.HIGHEST
    )
    static_grad = lax.psum_scatter(terms, "mem", scatter_dimension=0, tiled=True)
    return (alpha_grad, static_grad)


def solution(mesh):
    in_specs = (
        P("mem", None, "lon", "lat"),
        P("mem", "lon", "lat"),
        P(None, "lon", "lat"),
        P(),
        P("lat", None),
    )
    out_specs = (P(("mem", "lon"), "lat", None), P("mem", "lon", "lat"))
    return jax.shard_map(local, mesh=mesh, in_specs=in_specs, out_specs=out_specs, check_vma=False)
```

profile of v0, /device:TPU:1, one launch (start us, length us, event | category | flops | bytes accessed | tf_op | source)
XLA Modules:
  0.0 300.7 jit_solution(1129494648810352419)
XLA Ops:
  7.2 0.0 copy-start
  7.2 1.0 copy-done
  8.2 1.4 fusion.41
  9.6 62.3 %all_gather.3 = f32[8,90,128]{2,1,0:T(8,128)S(1)} all-gather(f32[1,90,128]{2,1,0:T(8,128)S(1)} %get-tuple-element.7), channel_id=1, replica_groups=mesh['mem'=8,'lat'=4,'lon'=16] {'mem'}, dimensions={0}, use_global_device_ids=true | all-gather | bytes 414720 | tf_op jit(solution)/shard_map/all_gather | solution.py:35
  71.9 0.2 copy.21
  72.1 2.8 fusion
  74.9 3.6 %copy.22 = bf16[128,90,128]{2,1,0:T(8,128)(2,1)} copy(bf16[128,90,128]{2,0,1:T(8,128)(2,1)S(1)} %fusion) | data formatting | bytes 5898240 | tf_op jit(solution)/shard_map/reshape | solution.py:37
  78.5 15.5 %all-to-all-start = ((bf16[128,90,128]{2,1,0:T(8,128)(2,1)}), bf16[128,90,128]{2,1,0:T(8,128)(2,1)S(1)}, u32[]{:S(2)}, u32[]{:S(2)}) async-start(bf16[128,90,128]{2,1,0:T(8,128)(2,1)} %copy.22), calls=%async_computation | async-start | bytes 6291456 | tf_op jit(solution)/shard_map/all_to_all | solution.py:41
  94.0 0.0 reduce-scatter.5.cloned.1.call-start
  94.0 0.7 dynamic-slice_bitcast_fusion
  94.7 1.6 broadcast_multiply_fusion.1
  96.4 0.0 reduce-scatter.5.cloned.1.call-update
  96.4 0.0 reduce-scatter.3.cloned.1.call-start
  96.5 6.6 %fusion.12 = f32[1440,256]{1,0:T(8,128)} fusion(s32[256]{0:T(256)S(1)} %iota_add_fusion), kind=kLoop, calls=%fused_computation.14 | loop fusion | flops 3317760 | bytes 1475584 | tf_op jit(solution)/shard_map/sin | solution.py:20
  103.1 6.5 %fusion.9 = f32[1440,256]{1,0:T(8,128)} fusion(), kind=kLoop, calls=%fused_computation.11 | loop fusion | flops 3317760 | bytes 1474560 | tf_op jit(solution)/shard_map/cos | solution.py:20
  109.6 110.0 %all-to-all-done = bf16[128,90,128]{2,1,0:T(8,128)(2,1)S(1)} async-done(((bf16[128,90,128]{2,1,0:T(8,128)(2,1)}), bf16[128,90,128]{2,1,0:T(8,128)(2,1)S(1)}, u32[]{:S(2)}, u32[]{:S(2)}) %all-to-all-start) | async-done | bytes 2949152 | tf_op jit(solution)/shard_map/all_to_all | solution.py:41
  219.5 2.8 copy.24
  222.4 6.3 %fusion.29 = f32[8,512,128]{2,1,0:T(8,128)} fusion(bf16[8,1440,128]{2,0,1:T(8,128)(2,1)} %bitcast.25, f32[1440,256]{1,0:T(8,128)} %fusion.12, f32[1440,256]{1,0:T(8,128)} %fusion.9, s32[128]{0:T(128)S(1)} %multiply_add_fusion), kind=kOutput, calls=%fused_computation.26 | convolution fusion | flops 1647165440 | bytes 7995904 | tf_op jit(solution)/shard_map/rkc,cq->rkq/dot_general | solution.py:47
  228.6 0.0 copy-start.1
  228.6 0.0 reduce-scatter.3.cloned.1.call-update
  228.7 31.1 %reduce-scatter.5.cloned.1.call-done = f32[1,90,128]{2,1,0:T(8,128)} async-done(((f32[8,90,128]{2,1,0:T(8,128)}), f32[1,90,128]{2,1,0:T(8,128)}) %reduce-scatter.5.cloned.1.call-update) | async-done | bytes 46096 | tf_op jit(solution)/shard_map/reduce_scatter | solution.py:56
  259.7 1.5 copy.28
  261.2 30.8 %reduce-scatter.3.cloned.1.call-done = f32[8,128,128]{2,1,0:T(8,128)} async-done(((f32[8,512,128]{2,1,0:T(8,128)}), f32[8,128,128]{2,1,0:T(8,128)}) %reduce-scatter.3.cloned.1.call-update) | async-done | bytes 524304 | tf_op jit(solution)/shard_map/reduce_scatter | solution.py:48
  292.0 0.0 copy-done.1
  292.0 1.9 broadcast_multiply_fusion
  (3 shorter events, 0.0 us)
Async XLA Ops:
  7.2 1.0 copy-start
  78.5 141.1 %all-to-all-start = ((bf16[128,90,128]{2,1,0:T(8,128)(2,1)}), bf16[128,90,128]{2,1,0:T(8,128)(2,1)S(1)}, u32[]{:S(2)}, u32[]{:S(2)}) async-start(bf16[128,90,128]{2,1,0:T(8,128)(2,1)} %copy.22), calls=%async_computation | async-start | bytes 6291456 | tf_op jit(solution)/shard_map/all_to_all | solution.py:41
  94.0 165.7 %reduce-scatter.5.cloned.1.call-start = ((), (), s32[]{:S(2)}) async-start(), calls=%async_computation.4 | async-start | bytes 442368 | tf_op jit(solution)/shard_map/reduce_scatter | solution.py:56
  96.4 195.6 %reduce-scatter.3.cloned.1.call-start = ((), (), s32[]{:S(2)}) async-start(), calls=%async_computation.3 | async-start | bytes 2621440 | tf_op jit(solution)/shard_map/reduce_scatter | solution.py:48
  228.6 63.4 %copy-start.1 = (f32[128,128]{1,0:T(8,128)S(1)}, f32[128,128]{1,0:T(8,128)}, u32[]{:S(2)}) copy-start(f32[128,128]{1,0:T(8,128)} %param.9) | copy-start | bytes 196612
Sparse Core Ops, SparseCore 0:
  99.9 159.8 reduce-scatter.4
  262.6 29.3 reduce-scatter.2
where the time goes:
time: 301 us
  waiting for transfers between devices  172 us (57%)
  blocking collectives  62.3 us (21%)
  other arithmetic  20.8 us (7%)
  starting transfers between devices  15.6 us (5%)
  between operations  14.1 us (5%)
  local copies, waits for them, and re-layouts  9.8 us (3%)
  matrix products  6.27 us (2%)
    all_to_all x1, waiting for transfers between devices, local(): lax.all_to_all(member_rows, 'lon', split_axis=0, concat_axis=1, tiled=True)  110 us
    all_gather x1, blocking collectives, local(): whole_grad = lax.all_gather(grad_field, 'mem', axis=0, tiled=True)  62.3 us
    reduce_scatter x1, waiting for transfers between devices, local(): lax.psum_scatter(terms, 'mem', scatter_dimension=0, tiled=True)  31.1 us
    reduce_scatter x1, waiting for transfers between devices, local(): lax.psum_scatter(partial_sums, 'lat', scatter_dimension=1, tiled=True)  30.8 us
    all_to_all x1, starting transfers between devices, local(): lax.all_to_all(member_rows, 'lon', split_axis=0, concat_axis=1, tiled=True)  15.5 us
    sin x1, other arithmetic, lon_table_make(): jnp.sin(angle_sin)  6.61 us
    cos x1, other arithmetic, lon_table_make(): jnp.cos(angle_cos)  6.47 us
    dot_general x1, matrix products, local(): jnp.einsum('rkc,cq->rkq', zonal, lat_table, preferred_element_type=jnp.fl...  6.27 us
  transfers between devices with their start and end apart: 3, of which 3 were waited for; matrix products, arithmetic and copies ran while one was open for 9% of the time, Pallas kernels for 0%

commit v1 on v0

v1 whole, which is shorter than its diff:
```python
import jax
import jax.numpy as jnp
from jax import lax
from jax.experimental import pallas as pl
from jax.experimental.pallas import tpu as pltpu
from jax.sharding import PartitionSpec as P

NLON = 1440
NLAT = 512
KLON = 512
KLAT = 128
PAIR = 2
TILE = 8


def cosine(phase, period):
    return jnp.cos(jnp.float32(2.0 * jnp.pi) * (phase % period).astype(jnp.float32) / period)


def lon_table_make(n_lon, k_lon, blocks, rows, waves):
    band = n_lon // blocks
    column = waves
    level = column // (k_lon // 4) % PAIR
    number = column // (k_lon // 4 * PAIR) * (k_lon // 4) + column % (k_lon // 4)
    sine = number >= k_lon // 2
    wave = jnp.where(sine, number - k_lon // 2 + 1, number)[None, :]
    shift = jnp.where(sine, n_lon // 4, 0)[None, :]
    row = jnp.arange(rows, dtype=jnp.int32)[:, None]
    starts = jnp.arange(blocks, dtype=jnp.int32)[:, None] * band * wave - shift
    places = row % band * wave
    factor = jnp.sqrt(jnp.float32(2.0) / n_lon)
    cos_start, sin_start = cosine(starts, n_lon) * factor, cosine(starts - n_lon // 4, n_lon) * factor
    own = row // band == level[None, :]
    cos_place = jnp.where(own, cosine(places, n_lon), 0.0)
    sin_place = jnp.where(own, cosine(places - n_lon // 4, n_lon), 0.0)
    table = cos_start[:, None] * cos_place[None] - sin_start[:, None] * sin_place[None]
    return table.astype(jnp.bfloat16).reshape(blocks * rows, PAIR * k_lon)


def lat_table_make(cells, n_lat, k_lat):
    waves = jnp.arange(k_lat, dtype=jnp.int32)[None, :]
    phase = ((2 * cells[:, None] + 1) * waves % (4 * n_lat)).astype(jnp.float32)
    angle = jnp.float32(jnp.pi) * phase / (2 * n_lat)
    return (jnp.cos(angle) * jnp.sqrt(jnp.float32(2.0) / n_lat)).astype(jnp.bfloat16)


def after(value, earlier):
    return lax.optimization_barrier((value, earlier))[0]


def ring(size, step, groups=1):
    return [(g * size + i, g * size + (i + step) % size) for g in range(groups) for i in range(size)]


def from_ahead(field, axis, groups):
    return [lax.ppermute(field, axis, ring(4, -step, groups)) for step in (1, 2, 3)]


def by_position(mine, ahead, me):
    turned = jnp.stack([mine, *ahead, mine, *ahead[:2]])
    return lax.dynamic_slice_in_dim(turned, (4 - me) % 4, 4, 0)


def spread_kernel(members_ref, out_ref, wide, both):
    count, lon, levels, _ = members_ref.shape
    both[...] = jnp.zeros_like(both)
    for m in range(count):
        wide[m % 2, : lon * levels] = members_ref[m].astype(jnp.float32).reshape(lon * levels, -1)
        for part in range(levels // PAIR):
            for place in range(PAIR):
                both[part, place * lon : (place + 1) * lon] = wide[
                    m % 2, pl.ds(part * PAIR + place, lon, stride=levels), :
                ]
            out_ref[part, m] = both[part].astype(jnp.bfloat16)


def spread(members, rows):
    count, lon, levels, lat = members.shape
    step = min(2, count)
    return pl.pallas_call(
        spread_kernel,
        out_shape=jax.ShapeDtypeStruct((levels // PAIR, count, rows, lat), members.dtype),
        grid=(count // step,),
        in_specs=[pl.BlockSpec((step, lon, levels, lat), lambda i: (i, 0, 0, 0))],
        out_specs=pl.BlockSpec((levels // PAIR, step, rows, lat), lambda i: (0, i, 0, 0)),
        scratch_shapes=[
            pltpu.VMEM((2, (lon + TILE) * levels, lat), jnp.float32),
            pltpu.VMEM((levels // PAIR, rows, lat), jnp.float32),
        ],
        compiler_params=pltpu.CompilerParams(vmem_limit_bytes=56 * 2**20),
        cost_estimate=pl.CostEstimate(flops=members.size, bytes_accessed=4 * members.size, transcendentals=0),
    )(members)


def lat_sums_kernel(x_ref, parts_ref, grads_ref, table_ref, out_ref):
    x = x_ref[0]
    for m in range(out_ref.shape[0]):
        product = [
            (parts_ref[part, m].astype(jnp.float32) * grads_ref[(part + 4 - x) % 4]).astype(jnp.bfloat16)
            for part in range(4)
        ]
        sums = jnp.dot(
            jnp.concatenate(product, axis=1), table_ref[...], preferred_element_type=jnp.float32
        )
        out_ref[m] = sums.astype(jnp.bfloat16)


def lat_sums(x, parts, grads, table):
    bands, count, rows, lat = parts.shape
    waves = table.shape[1]
    step = min(4, count)
    return pl.pallas_call(
        lat_sums_kernel,
        out_shape=jax.ShapeDtypeStruct((count, rows, waves), jnp.bfloat16),
        grid=(count // step,),
        in_specs=[
            pl.BlockSpec(memory_space=pltpu.SMEM),
            pl.BlockSpec((bands, step, rows, lat), lambda i: (0, i, 0, 0)),
            pl.BlockSpec((bands, rows, lat), lambda i: (0, 0, 0)),
            pl.BlockSpec((bands * lat, waves), lambda i: (0, 0)),
        ],
        out_specs=pl.BlockSpec((step, rows, waves), lambda i: (i, 0, 0)),
        compiler_params=pltpu.CompilerParams(vmem_limit_bytes=24 * 2**20),
        cost_estimate=pl.CostEstimate(
            flops=2 * parts.size * waves, bytes_accessed=2 * parts.size, transcendentals=0
        ),
    )(jnp.reshape(x, (1,)).astype(jnp.int32), parts, grads, table)


def local(members, grad_field, static_std, vert_mix, loc_weights):
    mem_local, levels, lon_local, lat_local = members.shape
    mem = lax.axis_index("mem")
    half_z, y = mem // 4, mem % 4
    x = lax.axis_index("lat")
    rows = -(-PAIR * lon_local // TILE) * TILE

    sent = spread(members.transpose(0, 2, 1, 3), rows)
    parts = lax.all_to_all(sent, "lat", split_axis=0, concat_axis=0, tiled=True)

    lat_table = lat_table_make(after(jnp.arange(NLAT, dtype=jnp.int32), sent), NLAT, KLAT)
    own_grad = after(grad_field[0], lat_table)
    far_grad = lax.ppermute(own_grad, "mem", [(i, (i + 4) % 8) for i in range(8)])
    low = jnp.where(half_z == 0, own_grad, far_grad)
    high = jnp.where(half_z == 0, far_grad, own_grad)
    halves = jnp.stack([low, high])
    grads = by_position(halves, from_ahead(halves, "mem", 2), y)
    grads = grads.transpose(1, 0, 2, 3).reshape(levels, lon_local, lat_local)
    pairs = grads.reshape(4, PAIR * lon_local, lat_local)
    pairs = jnp.pad(pairs, ((0, 0), (0, rows - PAIR * lon_local), (0, 0)))

    def pair(step):
        return lax.dynamic_index_in_dim(pairs, (x + step) % 4, 0, keepdims=False)

    met = jnp.stack(
        [pair(0)] + [lax.ppermute(pair(4 - step), "lat", ring(4, -step)) for step in (1, 2, 3)]
    )

    sums = lat_sums(x, parts, met, lat_table)

    whole = lax.all_to_all(sums, "lon", split_axis=0, concat_axis=0, tiled=True)
    columns = after(jnp.arange(PAIR * KLON, dtype=jnp.int32), sums)
    lon_table = lon_table_make(NLON, KLON, mem_local, rows, columns)
    zonal = jnp.einsum(
        "nk,nq->kq", lon_table, whole.reshape(mem_local * rows, KLAT), preferred_element_type=jnp.float32
    ).astype(jnp.bfloat16)
    zonal = zonal.reshape(4, PAIR, KLON // 4, KLAT)
    alpha = lax.all_to_all(zonal, "lat", split_axis=0, concat_axis=0, tiled=True)
    alpha_grad = alpha.reshape(levels, KLON // 4, KLAT).astype(jnp.float32) * loc_weights[None]

    mix = after(lax.dynamic_index_in_dim(vert_mix, mem, 1, keepdims=False), sums)
    static_grad = jnp.sum(mix[:, None, None] * (static_std * grads), axis=0)
    return (alpha_grad, static_grad[None])


def solution(mesh):
    in_specs = (
        P("mem", None, "lon", "lat"),
        P("mem", "lon", "lat"),
        P(None, "lon", "lat"),
        P(),
        P("lat", None),
    )
    out_specs = (P(("mem", "lon"), "lat", None), P("mem", "lon", "lat"))
    return jax.shard_map(local, mesh=mesh, in_specs=in_specs, out_specs=out_specs, check_vma=False)
```

time: 301 us -> 127 us (0.42)
  waiting for transfers between devices: 172 us -> 41.6 us
  blocking collectives: 62.3 us -> 0 us
  starting transfers between devices: 15.6 us -> 58.3 us
  between operations: 14.1 us -> 1 us
  other arithmetic: 20.8 us -> 8.75 us
  Pallas kernels: 0 us -> 8.61 us
  local copies, waits for them, and re-layouts: 9.8 us -> 4.66 us
  matrix products: 6.27 us -> 2.73 us
    all_to_all x1 -> x3, waiting for transfers between devices: 110 us -> 33.1 us  [the longest x1 27.6 us: local(): whole = lax.all_to_all(sums, 'lon', split_axis=0, concat_axis=0, tiled=True)]
    all_gather x1 -> x0, blocking collectives: 62.3 us -> none  [local(): whole_grad = lax.all_gather(grad_field, 'mem', axis=0, tiled=True)]
    reduce_scatter x2 -> x0, waiting for transfers between devices: 61.9 us -> none  [the longest x1 31.1 us: local(): lax.psum_scatter(terms, 'mem', scatter_dimension=0, tiled=True)]
    ppermute x0 -> x7, starting transfers between devices: none -> 35.5 us  [the longest x1 15.4 us: local(): lax.ppermute(own_grad, 'mem', [(i, (i + 4) % 8) for i in range(8)])]
    pallas_call x0 -> x2, Pallas kernels: none -> 8.61 us  [the longest x1 6.78 us: spread(): pl.pallas_call(spread_kernel, out_shape=jax.ShapeDtypeStruct((levels // P...]
    ppermute x0 -> x7, waiting for transfers between devices: none -> 8.49 us  [the longest x3 4.2 us: from_ahead(): lax.ppermute(field, axis, ring(4, -step, groups))]
    all_to_all x1 -> x3, starting transfers between devices: 15.5 us -> 22.8 us  [the longest x1 14.2 us: local(): whole = lax.all_to_all(sums, 'lon', split_axis=0, concat_axis=0, tiled=True)]
    sin x1 -> x0, other arithmetic: 6.61 us -> none  [lon_table_make(): jnp.sin(angle_sin)]
  transfers between devices with their start and end apart: 3 -> 10, of which waited for: 3 -> 6; matrix products, arithmetic and copies ran while one was open for 9% -> 9% of each run, Pallas kernels for 0% -> 0%
where the time goes in v1:
time: 127 us; the launch traced here: 126 us
  starting transfers between devices  58.3 us (46%)
  waiting for transfers between devices  41.6 us (33%)
  other arithmetic  8.75 us (7%)
  Pallas kernels  8.61 us (7%)
  local copies, waits for them, and re-layouts  4.66 us (4%)
  matrix products  2.73 us (2%)
    all_to_all x1, waiting for transfers between devices, local(): whole = lax.all_to_all(sums, 'lon', split_axis=0, concat_axis=0, tiled=True)  27.6 us
    ppermute x1, starting transfers between devices, local(): lax.ppermute(own_grad, 'mem', [(i, (i + 4) % 8) for i in range(8)])  15.4 us
    all_to_all x1, starting transfers between devices, local(): whole = lax.all_to_all(sums, 'lon', split_axis=0, concat_axis=0, tiled=True)  14.2 us
    ppermute x3, starting transfers between devices, local(): lax.ppermute(pair(4 - step), 'lat', ring(4, -step))  10.5 us
    ppermute x3, starting transfers between devices, from_ahead(): lax.ppermute(field, axis, ring(4, -step, groups))  9.5 us
    pallas_call x1, Pallas kernels, spread(): pl.pallas_call(spread_kernel, out_shape=jax.ShapeDtypeStruct((levels // P...  6.78 us
    select_n x1, other arithmetic, lon_table_make(): cos_place = jnp.where(own, cosine(places, n_lon), 0.0)  5.93 us
    all_to_all x1, waiting for transfers between devices, local(): lax.all_to_all(zonal, 'lat', split_axis=0, concat_axis=0, tiled=True)  5.52 us
  transfers between devices with their start and end apart: 10, of which 6 were waited for; matrix products, arithmetic and copies ran while one was open for 9% of the time, Pallas kernels for 0%

profile of v1, /device:TPU:1, one launch (start us, length us, event | category | flops | bytes accessed | tf_op | source)
XLA Modules:
  0.0 125.6 jit_solution(14170627861130905128)
XLA Ops:
  0.6 0.0 copy-start
  0.6 6.8 %shard_map.68 = bf16[4,16,184,128]{3,2,1,0:T(8,128)(2,1)} custom-call(bf16[16,90,8,128]{3,2,1,0:T(8,128)(2,1)} %bitcast.41), custom_call_target="tpu_custom_call" | custom-call | flops 1474560 | bytes 5898240 | tf_op jit(solution)/shard_map/pallas_call | solution.py:80
  7.4 0.0 copy-start.6
  7.4 5.0 %all-to-all-start = ((bf16[4,16,184,128]{3,2,1,0:T(8,128)(2,1)}), bf16[4,16,184,128]{3,2,1,0:T(8,128)(2,1)S(1)}, u32[]{:S(2)}, u32[]{:S(2)}) async-start(bf16[4,16,184,128]{3,2,1,0:T(8,128)(2,1)} %shard_map.68), calls=%async_computation | async-start | bytes 6029312 | tf_op jit(solution)/shard_map/all_to_all | solution.py:138
  12.4 1.0 fusion.21.table_ref
  13.5 0.0 copy-done.6
  13.5 15.4 %collective-permute-start = (f32[90,128]{1,0:T(8,128)S(1)}, f32[90,128]{1,0:T(8,128)S(1)}, u32[]{:S(2)}, u32[]{:S(2)}) collective-permute-start(f32[90,128]{1,0:T(8,128)S(1)} %bitcast.43), channel_id=1, source_target_pairs={{0,256},{64,320},{128,384},{192,448},{256,0},{320,64},{384,128},{4... | collective-permute-start | bytes 138248 | tf_op jit(solution)/shard_map/ppermute | solution.py:142
  29.0 1.5 %collective-permute-done = f32[90,128]{1,0:T(8,128)S(1)} collective-permute-done((f32[90,128]{1,0:T(8,128)S(1)}, f32[90,128]{1,0:T(8,128)S(1)}, u32[]{:S(2)}, u32[]{:S(2)}) %collective-permute-start) | collective-permute-done | bytes 46112 | tf_op jit(solution)/shard_map/ppermute | solution.py:142
  30.6 4.6 %collective-permute-start.1 = (f32[2,90,128]{2,1,0:T(8,128)S(1)}, f32[2,90,128]{2,1,0:T(8,128)S(1)}, u32[]{:S(2)}, u32[]{:S(2)}) collective-permute-start(f32[2,90,128]{2,1,0:T(8,128)S(1)} %pad_maximum_fusion.1), channel_id=1, source_target_pairs={{0,192},{64,0},{128,64},{192,128},{256,448},{320,256},{384,320},{4... | collective-permute-start | bytes 276488 | tf_op jit(solution)/shard_map/ppermute | solution.py:56
  35.2 2.3 %collective-permute-start.2 = (f32[2,90,128]{2,1,0:T(8,128)S(1)}, f32[2,90,128]{2,1,0:T(8,128)S(1)}, u32[]{:S(2)}, u32[]{:S(2)}) collective-permute-start(f32[2,90,128]{2,1,0:T(8,128)S(1)} %pad_maximum_fusion.1), channel_id=1, source_target_pairs={{0,128},{64,192},{128,0},{192,64},{256,384},{320,448},{384,256},{4... | collective-permute-start | bytes 276488 | tf_op jit(solution)/shard_map/ppermute | solution.py:56
  37.5 2.6 %collective-permute-start.3 = (f32[2,90,128]{2,1,0:T(8,128)S(1)}, f32[2,90,128]{2,1,0:T(8,128)S(1)}, u32[]{:S(2)}, u32[]{:S(2)}) collective-permute-start(f32[2,90,128]{2,1,0:T(8,128)S(1)} %pad_maximum_fusion.1), channel_id=1, source_target_pairs={{0,64},{64,128},{128,192},{192,0},{256,320},{320,384},{384,448},{4... | collective-permute-start | bytes 276488 | tf_op jit(solution)/shard_map/ppermute | solution.py:56
  40.1 0.0 collective-permute-done.1
  40.1 2.2 %collective-permute-done.2 = f32[2,90,128]{2,1,0:T(8,128)S(1)} collective-permute-done((f32[2,90,128]{2,1,0:T(8,128)S(1)}, f32[2,90,128]{2,1,0:T(8,128)S(1)}, u32[]{:S(2)}, u32[]{:S(2)}) %collective-permute-start.2) | collective-permute-done | bytes 92192 | tf_op jit(solution)/shard_map/ppermute | solution.py:56
  42.4 2.0 %collective-permute-done.3 = f32[2,90,128]{2,1,0:T(8,128)S(1)} collective-permute-done((f32[2,90,128]{2,1,0:T(8,128)S(1)}, f32[2,90,128]{2,1,0:T(8,128)S(1)}, u32[]{:S(2)}, u32[]{:S(2)}) %collective-permute-start.3) | collective-permute-done | bytes 92192 | tf_op jit(solution)/shard_map/ppermute | solution.py:56
  44.5 0.0 copy-start.2
  44.5 0.7 copy-done.2
  45.2 0.8 reshape_reshape.3
  46.0 1.1 pad_dynamic-slice_fusion.3
  47.1 3.1 %collective-permute-start.6 = (f32[184,128]{1,0:T(8,128)S(1)}, f32[184,128]{1,0:T(8,128)S(1)}, u32[]{:S(2)}, u32[]{:S(2)}) collective-permute-start(f32[184,128]{1,0:T(8,128)S(1)} %get-tuple-element.13), channel_id=1, source_target_pairs={{0,16},{16,32},{32,48},{48,0},{1,17},{17,33},{33,49},{49,1},{2,18}... | collective-permute-start | bytes 282632 | tf_op jit(solution)/shard_map/ppermute | solution.py:155
  50.2 4.5 %collective-permute-start.5 = (f32[184,128]{1,0:T(8,128)S(1)}, f32[184,128]{1,0:T(8,128)S(1)}, u32[]{:S(2)}, u32[]{:S(2)}) collective-permute-start(f32[184,128]{1,0:T(8,128)S(1)} %get-tuple-element.12), channel_id=1, source_target_pairs={{0,32},{16,48},{32,0},{48,16},{1,33},{17,49},{33,1},{49,17},{2,34}... | collective-permute-start | bytes 282632 | tf_op jit(solution)/shard_map/ppermute | solution.py:155
  54.7 2.9 %collective-permute-start.4 = (f32[184,128]{1,0:T(8,128)S(1)}, f32[184,128]{1,0:T(8,128)S(1)}, u32[]{:S(2)}, u32[]{:S(2)}) collective-permute-start(f32[184,128]{1,0:T(8,128)S(1)} %get-tuple-element.11), channel_id=1, source_target_pairs={{0,48},{16,0},{32,16},{48,32},{1,49},{17,1},{33,17},{49,33},{2,50}... | collective-permute-start | bytes 282632 | tf_op jit(solution)/shard_map/ppermute | solution.py:155
  57.6 0.0 collective-permute-done.6
  57.6 0.0 collective-permute-done.5
  57.6 2.8 %collective-permute-done.4 = f32[184,128]{1,0:T(8,128)S(1)} collective-permute-done((f32[184,128]{1,0:T(8,128)S(1)}, f32[184,128]{1,0:T(8,128)S(1)}, u32[]{:S(2)}, u32[]{:S(2)}) %collective-permute-start.4) | collective-permute-done | bytes 94240 | tf_op jit(solution)/shard_map/ppermute | solution.py:155
  60.4 0.0 all-to-all-done.parts_ref
  60.4 1.8 %shard_map.69 = bf16[16,184,128]{2,1,0:T(8,128)(2,1)S(1)} custom-call(s32[1]{0:T(128)} %bitcast.x_ref, bf16[4,16,184,128]{3,2,1,0:T(8,128)(2,1)S(1)} %all-to-all-done.parts_ref, f32[4,184,128]{2,1,0:T(8,128)S(1)} %pad_maximum_fusion.grads_ref, bf16[512,128]{1,0:T(8,128)(2,1)S(1)} %fusion.21.table_ref), custom_call_target="tpu_custom_call" | custom-call | flops 385875968 | bytes 3014656 | tf_op jit(solution)/shard_map/pallas_call | solution.py:112
  62.3 0.0 copy-start.1
  62.3 0.9 copy-done.1
  63.2 14.2 %all-to-all-start.1 = ((bf16[16,184,128]{2,1,0:T(8,128)(2,1)}), bf16[16,184,128]{2,1,0:T(8,128)(2,1)S(1)}, u32[]{:S(2)}, u32[]{:S(2)}) async-start(bf16[16,184,128]{2,1,0:T(8,128)(2,1)} %copy-done.1), calls=%async_computation.1 | async-start | bytes 1507328 | tf_op jit(solution)/shard_map/all_to_all | solution.py:160
  77.4 0.6 fusion.31
  78.0 5.9 %compare_select_fusion.1 = (f32[184,1024]{1,0:T(8,128)S(1)}, f32[184,1024]{1,0:T(8,128)S(1)}) fusion(s32[1024]{0:T(1024)S(1)} %get-tuple-element.21, s32[184]{0:T(256)S(1)} %get-tuple-element.23, s32[1024]{0:T(1024)S(1)} %get-tuple-element.22, s32[184]{0:T(256)S(1)} %get-tuple-element.24), kind=kLoop, calls=%fused_computation.11 | loop fusion | flops 3956736 | bytes 1516992 | tf_op jit(solution)/shard_map/jit(_where)/select_n | solution.py:34
  84.0 27.6 %all-to-all-done.1 = bf16[16,184,128]{2,1,0:T(8,128)(2,1)S(1)} async-done(((bf16[16,184,128]{2,1,0:T(8,128)(2,1)}), bf16[16,184,128]{2,1,0:T(8,128)(2,1)S(1)}, u32[]{:S(2)}, u32[]{:S(2)}) %all-to-all-start.1) | async-done | bytes 753696 | tf_op jit(solution)/shard_map/all_to_all | solution.py:160
  111.5 0.0 copy-start.3
  111.5 0.0 copy-start.4
  111.5 0.0 copy-start.5
  111.5 2.7 %fusion.2 = bf16[1024,128]{1,0:T(8,128)(2,1)} fusion(bf16[16,184,128]{2,1,0:T(8,128)(2,1)S(1)} %all-to-all-done.1, f32[184,1024]{1,0:T(8,128)S(1)} %get-tuple-element.17, f32[16,1024]{1,0:T(8,128)S(1)} %get-tuple-element.19, f32[184,1024]{1,0:T(8,128)S(1)} %get-tuple-element.16, f32[16,1024]{1,0:T(8,128)S(1)} %get-tuple-element.18), kind=kOutput, calls=%fused_computation.3 | convolution fusion | flops 783941632 | bytes 2654208 | tf_op jit(solution)/shard_map/nk,nq->kq/dot_general | solution.py:163
  114.3 3.7 %all-to-all-start.2 = ((bf16[4,2,128,128]{3,2,1,0:T(8,128)(2,1)}), bf16[4,2,128,128]{3,2,1,0:T(8,128)(2,1)S(1)}, u32[]{:S(2)}, u32[]{:S(2)}) async-start(bf16[4,2,128,128]{3,2,1,0:T(8,128)(2,1)} %bitcast.16), calls=%async_computation.2 | async-start | bytes 524288 | tf_op jit(solution)/shard_map/all_to_all | solution.py:167
  117.9 0.0 copy-done
  117.9 0.2 dynamic-slice_reduce_fusion
  118.1 0.0 copy-done.3
  118.1 0.2 copy.10
  118.4 0.0 copy-done.4
  118.4 0.2 multiply_reduce_fusion
  118.6 0.7 broadcast_in_dim.15
  119.2 5.5 %all-to-all-done.2 = bf16[4,2,128,128]{3,2,1,0:T(8,128)(2,1)S(1)} async-done(((bf16[4,2,128,128]{3,2,1,0:T(8,128)(2,1)}), bf16[4,2,128,128]{3,2,1,0:T(8,128)(2,1)S(1)}, u32[]{:S(2)}, u32[]{:S(2)}) %all-to-all-start.2) | async-done | bytes 262176 | tf_op jit(solution)/shard_map/all_to_all | solution.py:167
  124.8 0.0 copy-done.5
  124.8 0.9 convert_multiply_fusion
  (19 shorter events, 0.2 us)
Async XLA Ops:
  0.6 117.3 %copy-start = (f32[8,8]{1,0:T(8,128)S(1)}, f32[8,8]{1,0:T(8,128)}, u32[]{:S(2)}) copy-start(f32[8,8]{1,0:T(8,128)} %param.8) | copy-start | bytes 772
  7.4 6.0 %copy-start.6 = (f32[1,90,128]{2,0,1:T(1,128)S(1)}, f32[1,90,128]{2,0,1:T(1,128)}, u32[]{:S(2)}) copy-start(f32[1,90,128]{2,0,1:T(1,128)} %param.6) | copy-start | bytes 138244
  7.4 53.0 %all-to-all-start = ((bf16[4,16,184,128]{3,2,1,0:T(8,128)(2,1)}), bf16[4,16,184,128]{3,2,1,0:T(8,128)(2,1)S(1)}, u32[]{:S(2)}, u32[]{:S(2)}) async-start(bf16[4,16,184,128]{3,2,1,0:T(8,128)(2,1)} %shard_map.68), calls=%async_computation | async-start | bytes 6029312 | tf_op jit(solution)/shard_map/all_to_all | solution.py:138
  13.5 17.0 %collective-permute-start = (f32[90,128]{1,0:T(8,128)S(1)}, f32[90,128]{1,0:T(8,128)S(1)}, u32[]{:S(2)}, u32[]{:S(2)}) collective-permute-start(f32[90,128]{1,0:T(8,128)S(1)} %bitcast.43), channel_id=1, source_target_pairs={{0,256},{64,320},{128,384},{192,448},{256,0},{320,64},{384,128},{4... | collective-permute-start | bytes 138248 | tf_op jit(solution)/shard_map/ppermute | solution.py:142
  30.6 9.5 %collective-permute-start.1 = (f32[2,90,128]{2,1,0:T(8,128)S(1)}, f32[2,90,128]{2,1,0:T(8,128)S(1)}, u32[]{:S(2)}, u32[]{:S(2)}) collective-permute-start(f32[2,90,128]{2,1,0:T(8,128)S(1)} %pad_maximum_fusion.1), channel_id=1, source_target_pairs={{0,192},{64,0},{128,64},{192,128},{256,448},{320,256},{384,320},{4... | collective-permute-start | bytes 276488 | tf_op jit(solution)/shard_map/ppermute | solution.py:56
  35.2 7.2 %collective-permute-start.2 = (f32[2,90,128]{2,1,0:T(8,128)S(1)}, f32[2,90,128]{2,1,0:T(8,128)S(1)}, u32[]{:S(2)}, u32[]{:S(2)}) collective-permute-start(f32[2,90,128]{2,1,0:T(8,128)S(1)} %pad_maximum_fusion.1), channel_id=1, source_target_pairs={{0,128},{64,192},{128,0},{192,64},{256,384},{320,448},{384,256},{4... | collective-permute-start | bytes 276488 | tf_op jit(solution)/shard_map/ppermute | solution.py:56
  37.5 6.9 %collective-permute-start.3 = (f32[2,90,128]{2,1,0:T(8,128)S(1)}, f32[2,90,128]{2,1,0:T(8,128)S(1)}, u32[]{:S(2)}, u32[]{:S(2)}) collective-permute-start(f32[2,90,128]{2,1,0:T(8,128)S(1)} %pad_maximum_fusion.1), channel_id=1, source_target_pairs={{0,64},{64,128},{128,192},{192,0},{256,320},{320,384},{384,448},{4... | collective-permute-start | bytes 276488 | tf_op jit(solution)/shard_map/ppermute | solution.py:56
  44.5 0.7 copy-start.2
  47.1 10.5 %collective-permute-start.6 = (f32[184,128]{1,0:T(8,128)S(1)}, f32[184,128]{1,0:T(8,128)S(1)}, u32[]{:S(2)}, u32[]{:S(2)}) collective-permute-start(f32[184,128]{1,0:T(8,128)S(1)} %get-tuple-element.13), channel_id=1, source_target_pairs={{0,16},{16,32},{32,48},{48,0},{1,17},{17,33},{33,49},{49,1},{2,18}... | collective-permute-start | bytes 282632 | tf_op jit(solution)/shard_map/ppermute | solution.py:155
  50.2 7.4 %collective-permute-start.5 = (f32[184,128]{1,0:T(8,128)S(1)}, f32[184,128]{1,0:T(8,128)S(1)}, u32[]{:S(2)}, u32[]{:S(2)}) collective-permute-start(f32[184,128]{1,0:T(8,128)S(1)} %get-tuple-element.12), channel_id=1, source_target_pairs={{0,32},{16,48},{32,0},{48,16},{1,33},{17,49},{33,1},{49,17},{2,34}... | collective-permute-start | bytes 282632 | tf_op jit(solution)/shard_map/ppermute | solution.py:155
  54.7 5.7 %collective-permute-start.4 = (f32[184,128]{1,0:T(8,128)S(1)}, f32[184,128]{1,0:T(8,128)S(1)}, u32[]{:S(2)}, u32[]{:S(2)}) collective-permute-start(f32[184,128]{1,0:T(8,128)S(1)} %get-tuple-element.11), channel_id=1, source_target_pairs={{0,48},{16,0},{32,16},{48,32},{1,49},{17,1},{33,17},{49,33},{2,50}... | collective-permute-start | bytes 282632 | tf_op jit(solution)/shard_map/ppermute | solution.py:155
  62.3 0.9 copy-start.1
  63.2 48.4 %all-to-all-start.1 = ((bf16[16,184,128]{2,1,0:T(8,128)(2,1)}), bf16[16,184,128]{2,1,0:T(8,128)(2,1)S(1)}, u32[]{:S(2)}, u32[]{:S(2)}) async-start(bf16[16,184,128]{2,1,0:T(8,128)(2,1)} %copy-done.1), calls=%async_computation.1 | async-start | bytes 1507328 | tf_op jit(solution)/shard_map/all_to_all | solution.py:160
  111.5 6.6 %copy-start.3 = (f32[2,4,90,128]{3,2,0,1:T(8,128)S(1)}, f32[2,4,90,128]{3,2,0,1:T(8,128)}, u32[]{:S(2)}) copy-start(f32[2,4,90,128]{3,2,0,1:T(8,128)} %copy-done.2) | copy-start | bytes 1105924
  111.5 6.8 %copy-start.4 = (f32[8,90,128]{2,0,1:T(8,128)S(1)}, f32[8,90,128]{2,0,1:T(8,128)}, u32[]{:S(2)}) copy-start(f32[8,90,128]{2,0,1:T(8,128)} %param.7) | copy-start | bytes 1105924
  111.5 13.2 %copy-start.5 = (f32[128,128]{1,0:T(8,128)S(1)}, f32[128,128]{1,0:T(8,128)}, u32[]{:S(2)}) copy-start(f32[128,128]{1,0:T(8,128)} %param.9) | copy-start | bytes 196612
  114.3 10.5 %all-to-all-start.2 = ((bf16[4,2,128,128]{3,2,1,0:T(8,128)(2,1)}), bf16[4,2,128,128]{3,2,1,0:T(8,128)(2,1)S(1)}, u32[]{:S(2)}, u32[]{:S(2)}) async-start(bf16[4,2,128,128]{3,2,1,0:T(8,128)(2,1)} %bitcast.16), calls=%async_computation.2 | async-start | bytes 524288 | tf_op jit(solution)/shard_map/all_to_all | solution.py:167

commit v2 on v1

v2 whole, which is shorter than its diff:
```python
import jax
import jax.numpy as jnp
from jax import lax
from jax.experimental import pallas as pl
from jax.experimental.pallas import tpu as pltpu
from jax.sharding import PartitionSpec as P

NLON = 1440
NLAT = 512
KLON = 512
KLAT = 128
PAIR = 2
TILE = 8


def cosine(phase, period):
    return jnp.cos(jnp.float32(2.0 * jnp.pi) * (phase % period).astype(jnp.float32) / period)


def lon_table_make(n_lon, k_lon, blocks, rows, waves):
    band = n_lon // blocks
    whole = band // TILE * TILE
    column = waves
    level = column // (k_lon // 4) % PAIR
    number = column // (k_lon // 4 * PAIR) * (k_lon // 4) + column % (k_lon // 4)
    sine = number >= k_lon // 2
    wave = jnp.where(sine, number - k_lon // 2 + 1, number)[None, :]
    shift = jnp.where(sine, n_lon // 4, 0)[None, :]
    row = jnp.arange(rows, dtype=jnp.int32)[:, None]
    starts = jnp.arange(blocks, dtype=jnp.int32)[:, None] * band * wave - shift
    last = row - PAIR * whole
    place = jnp.where(last < 0, row % whole, whole + last % (band - whole))
    row_level = jnp.where(last < 0, row // whole, last // (band - whole))
    places = place * wave
    factor = jnp.sqrt(jnp.float32(2.0) / n_lon)
    cos_start, sin_start = cosine(starts, n_lon) * factor, cosine(starts - n_lon // 4, n_lon) * factor
    own = row_level == level[None, :]
    cos_place = jnp.where(own, cosine(places, n_lon), 0.0)
    sin_place = jnp.where(own, cosine(places - n_lon // 4, n_lon), 0.0)
    table = cos_start[:, None] * cos_place[None] - sin_start[:, None] * sin_place[None]
    return table.astype(jnp.bfloat16).reshape(blocks * rows, PAIR * k_lon)


def lat_table_make(cells, n_lat, k_lat):
    waves = jnp.arange(k_lat, dtype=jnp.int32)[None, :]
    phase = ((2 * cells[:, None] + 1) * waves % (4 * n_lat)).astype(jnp.float32)
    angle = jnp.float32(jnp.pi) * phase / (2 * n_lat)
    return (jnp.cos(angle) * jnp.sqrt(jnp.float32(2.0) / n_lat)).astype(jnp.bfloat16)


def after(value, earlier):
    return lax.optimization_barrier((value, earlier))[0]


def partners(size, flip):
    return [(i, i ^ flip) for i in range(size)]


def from_ahead(field):
    rings = [[(i, i // 4 * 4 + (i - step) % 4) for i in range(8)] for step in (1, 2, 3)]
    return [lax.ppermute(field, "mem", pairs) for pairs in rings]


def by_position(mine, ahead, me):
    turned = jnp.stack([mine, *ahead, mine, *ahead[:2]])
    return lax.dynamic_slice_in_dim(turned, (4 - me) % 4, 4, 0)


def pack_rows(fields, rows):
    lon = fields[0].shape[0]
    whole = lon // TILE * TILE
    empty = jnp.zeros((rows - len(fields) * lon, fields[0].shape[1]), fields[0].dtype)
    return jnp.concatenate([*[f[:whole] for f in fields], *[f[whole:] for f in fields], empty])


def spread_kernel(members_ref, out_ref, wide):
    count, lon, levels, lat = members_ref.shape
    whole = lon // TILE * TILE
    rows = out_ref.shape[2]
    for m in range(count):
        wide[m % 2] = members_ref[m].astype(jnp.float32).reshape(lon * levels, lat)
        for part in range(levels // PAIR):
            firsts = [part * PAIR + place for place in range(PAIR)]
            pieces = [wide[m % 2, pl.ds(first, whole, stride=levels), :] for first in firsts]
            lasts = [
                wide[m % 2, pl.ds(first + n * levels, 1), :] for first in firsts for n in range(whole, lon)
            ]
            empty = jnp.zeros((rows - PAIR * lon, lat), jnp.float32)
            out_ref[part, m] = jnp.concatenate([*pieces, *lasts, empty]).astype(jnp.bfloat16)


def spread(members, rows):
    count, lon, levels, lat = members.shape
    step = min(4, count)
    return pl.pallas_call(
        spread_kernel,
        out_shape=jax.ShapeDtypeStruct((levels // PAIR, count, rows, lat), members.dtype),
        grid=(count // step,),
        in_specs=[pl.BlockSpec((step, lon, levels, lat), lambda i: (i, 0, 0, 0))],
        out_specs=pl.BlockSpec((levels // PAIR, step, rows, lat), lambda i: (0, i, 0, 0)),
        scratch_shapes=[pltpu.VMEM((2, lon * levels, lat), jnp.float32)],
        compiler_params=pltpu.CompilerParams(vmem_limit_bytes=56 * 2**20),
        cost_estimate=pl.CostEstimate(flops=members.size, bytes_accessed=4 * members.size, transcendentals=0),
    )(members)


def lat_sums_kernel(parts_ref, grads_ref, table_ref, out_ref, packed):
    bands, count, rows, _ = parts_ref.shape

    @pl.when(pl.program_id(0) == 0)
    def _():
        for part in range(bands):
            packed[part] = pack_rows([grads_ref[part, place] for place in range(PAIR)], rows)

    for m in range(count):
        product = [
            (parts_ref[part, m].astype(jnp.float32) * packed[part]).astype(jnp.bfloat16)
            for part in range(bands)
        ]
        sums = jnp.dot(
            jnp.concatenate(product, axis=1), table_ref[...], preferred_element_type=jnp.float32
        )
        out_ref[m] = sums.astype(jnp.bfloat16)


def lat_sums(parts, grads, table):
    bands, count, rows, lat = parts.shape
    waves = table.shape[1]
    step = min(4, count)
    return pl.pallas_call(
        lat_sums_kernel,
        out_shape=pltpu.HBM((count, rows, waves), jnp.bfloat16),
        grid=(count // step,),
        in_specs=[
            pl.BlockSpec((bands, step, rows, lat), lambda i: (0, i, 0, 0)),
            pl.BlockSpec(grads.shape, lambda i: (0, 0, 0, 0)),
            pl.BlockSpec((bands * lat, waves), lambda i: (0, 0)),
        ],
        out_specs=pl.BlockSpec((step, rows, waves), lambda i: (i, 0, 0)),
        scratch_shapes=[pltpu.VMEM((bands, rows, lat), jnp.float32)],
        compiler_params=pltpu.CompilerParams(vmem_limit_bytes=24 * 2**20),
        cost_estimate=pl.CostEstimate(
            flops=2 * parts.size * waves, bytes_accessed=2 * parts.size, transcendentals=0
        ),
    )(parts, grads, table)


def local(members, grad_field, static_std, vert_mix, loc_weights):
    mem_local, levels, lon_local, lat_local = members.shape
    mem = lax.axis_index("mem")
    half_z, y = mem // 4, mem % 4
    rows = -(-PAIR * lon_local // TILE) * TILE

    sent = spread(members.transpose(0, 2, 1, 3), rows)
    parts = lax.all_to_all(sent, "lat", split_axis=0, concat_axis=0, tiled=True)

    lat_table = lat_table_make(after(jnp.arange(NLAT, dtype=jnp.int32), sent), NLAT, KLAT)
    own_grad = after(grad_field, lat_table)[0]
    far_grad = lax.ppermute(own_grad, "mem", partners(8, 4))
    mine = jnp.stack([jnp.where(half_z == 0, own_grad, far_grad), jnp.where(half_z == 0, far_grad, own_grad)])
    grads = by_position(mine, from_ahead(mine), y)
    grads = grads.transpose(1, 0, 2, 3).reshape(levels, lon_local, lat_local)
    pairs = after(grads.reshape(4, PAIR, lon_local, lat_local), parts)
    met = lax.all_to_all(pairs, "lat", split_axis=0, concat_axis=0, tiled=True)
    sums = lat_sums(parts, met, lat_table)

    whole = lax.all_to_all(sums, "lon", split_axis=0, concat_axis=0, tiled=True)
    columns = after(jnp.arange(PAIR * KLON, dtype=jnp.int32), sums)
    lon_table = lon_table_make(NLON, KLON, mem_local, rows, columns)
    zonal = jnp.einsum(
        "nk,nq->kq", lon_table, whole.reshape(mem_local * rows, KLAT), preferred_element_type=jnp.float32
    ).astype(jnp.bfloat16)
    zonal = zonal.reshape(4, PAIR, KLON // 4, KLAT)
    alpha = lax.all_to_all(zonal, "lat", split_axis=0, concat_axis=0, tiled=True)
    alpha_grad = alpha.reshape(levels, KLON // 4, KLAT).astype(jnp.float32) * loc_weights[None]

    mix = after(lax.dynamic_index_in_dim(vert_mix, mem, 1, keepdims=False), sums)
    static_grad = jnp.sum(mix[:, None, None] * (static_std * grads), axis=0)
    return (alpha_grad, static_grad[None])


def solution(mesh):
    in_specs = (
        P("mem", None, "lon", "lat"),
        P("mem", "lon", "lat"),
        P(None, "lon", "lat"),
        P(),
        P("lat", None),
    )
    out_specs = (P(("mem", "lon"), "lat", None), P("mem", "lon", "lat"))
    return jax.shard_map(local, mesh=mesh, in_specs=in_specs, out_specs=out_specs, check_vma=False)
```

time: 127 us -> 122 us (0.961)
  blocking collectives: 0 us -> 9.89 us
  starting transfers between devices: 58.3 us -> 50.4 us
  local copies, waits for them, and re-layouts: 4.66 us -> 1.35 us
  waiting for transfers between devices: 41.6 us -> 39.2 us
    ppermute x7 -> x4, starting transfers between devices: 35.5 us -> 24.9 us  [the longest x1 15.4 us: local(): far_grad = lax.ppermute(own_grad, 'mem', partners(8, 4))]
    all_to_all x0 -> x1, blocking collectives: none -> 9.89 us  [local(): met = lax.all_to_all(pairs, 'lat', split_axis=0, concat_axis=0, tiled=True)]
    all_to_all x1, starting transfers between devices: 14.2 us -> 17.1 us  [local(): whole = lax.all_to_all(sums, 'lon', split_axis=0, concat_axis=0, tiled=True)]
    ppermute x7 -> x4, waiting for transfers between devices: 8.49 us -> 5.76 us  [the longest x3 4.2 us: from_ahead(): return [lax.ppermute(field, 'mem', pairs) for pairs in rings]]
    pallas_call x1, Pallas kernels: 6.78 us -> 4.7 us  [spread(): pl.pallas_call(spread_kernel, out_shape=jax.ShapeDtypeStruct((levels // P...]
    unnamed x19 -> x13, local copies, waits for them, and re-layouts: 1.68 us -> 0.06 us
  transfers between devices with their start and end apart: 10 -> 7, of which waited for: 6 -> 5; matrix products, arithmetic and copies ran while one was open for 9% -> 7% of each run, Pallas kernels for 0% -> 0%
where the time goes in v2:
time: 122 us; the launch traced here: 121 us
  starting transfers between devices  50.4 us (41%)
  waiting for transfers between devices  39.2 us (32%)
  blocking collectives  9.89 us (8%)
  other arithmetic  8.71 us (7%)
  Pallas kernels  7.41 us (6%)
  matrix products  2.76 us (2%)
  local copies, waits for them, and re-layouts  1.35 us (1%)
    all_to_all x1, waiting for transfers between devices, local(): whole = lax.all_to_all(sums, 'lon', split_axis=0, concat_axis=0, tiled=True)  27.6 us
    all_to_all x1, starting transfers between devices, local(): whole = lax.all_to_all(sums, 'lon', split_axis=0, concat_axis=0, tiled=True)  17.1 us
    ppermute x1, starting transfers between devices, local(): far_grad = lax.ppermute(own_grad, 'mem', partners(8, 4))  15.4 us
    all_to_all x1, blocking collectives, local(): met = lax.all_to_all(pairs, 'lat', split_axis=0, concat_axis=0, tiled=True)  9.89 us
    ppermute x3, starting transfers between devices, from_ahead(): return [lax.ppermute(field, 'mem', pairs) for pairs in rings]  9.5 us
    select_n x1, other arithmetic, lon_table_make(): cos_place = jnp.where(own, cosine(places, n_lon), 0.0)  5.93 us
    all_to_all x1, waiting for transfers between devices, local(): lax.all_to_all(zonal, 'lat', split_axis=0, concat_axis=0, tiled=True)  5.92 us
    all_to_all x1, starting transfers between devices, local(): parts = lax.all_to_all(sent, 'lat', split_axis=0, concat_axis=0, tiled=True)  4.97 us
  transfers between devices with their start and end apart: 7, of which 5 were waited for; matrix products, arithmetic and copies ran while one was open for 7% of the time, Pallas kernels for 0%

profile of v2, /device:TPU:1, one launch (start us, length us, event | category | flops | bytes accessed | tf_op | source)
XLA Modules:
  0.0 120.6 jit_solution(9799352336759455418)
XLA Ops:
  0.6 0.0 copy-start
  0.6 4.7 %shard_map.68 = bf16[4,16,184,128]{3,2,1,0:T(8,128)(2,1)} custom-call(bf16[16,90,8,128]{3,2,1,0:T(8,128)(2,1)} %bitcast.38), custom_call_target="tpu_custom_call" | custom-call | flops 1474560 | bytes 5898240 | tf_op jit(solution)/shard_map/pallas_call | solution.py:95
  5.3 0.0 copy-start.2
  5.3 5.0 %all-to-all-start = ((bf16[4,16,184,128]{3,2,1,0:T(8,128)(2,1)}), bf16[4,16,184,128]{3,2,1,0:T(8,128)(2,1)S(1)}, u32[]{:S(2)}, u32[]{:S(2)}) async-start(bf16[4,16,184,128]{3,2,1,0:T(8,128)(2,1)} %shard_map.68), calls=%async_computation | async-start | bytes 6029312 | tf_op jit(solution)/shard_map/all_to_all | solution.py:155
  10.3 1.0 fusion.21.table_ref
  11.4 0.0 copy-done.2
  11.4 15.4 %collective-permute-start = (f32[90,128]{1,0:T(8,128)S(1)}, f32[90,128]{1,0:T(8,128)S(1)}, u32[]{:S(2)}, u32[]{:S(2)}) collective-permute-start(f32[90,128]{1,0:T(8,128)S(1)} %bitcast.39), channel_id=1, source_target_pairs={{0,256},{64,320},{128,384},{192,448},{256,0},{320,64},{384,128},{4... | collective-permute-start | bytes 138248 | tf_op jit(solution)/shard_map/ppermute | solution.py:159
  26.9 1.6 %collective-permute-done = f32[90,128]{1,0:T(8,128)S(1)} collective-permute-done((f32[90,128]{1,0:T(8,128)S(1)}, f32[90,128]{1,0:T(8,128)S(1)}, u32[]{:S(2)}, u32[]{:S(2)}) %collective-permute-start) | collective-permute-done | bytes 46112 | tf_op jit(solution)/shard_map/ppermute | solution.py:159
  28.5 4.6 %collective-permute-start.1 = (f32[2,90,128]{2,1,0:T(8,128)S(1)}, f32[2,90,128]{2,1,0:T(8,128)S(1)}, u32[]{:S(2)}, u32[]{:S(2)}) collective-permute-start(f32[2,90,128]{2,1,0:T(8,128)S(1)} %pad_maximum_fusion), channel_id=1, source_target_pairs={{0,192},{64,0},{128,64},{192,128},{256,448},{320,256},{384,320},{4... | collective-permute-start | bytes 276488 | tf_op jit(solution)/shard_map/ppermute | solution.py:61
  33.1 2.3 %collective-permute-start.2 = (f32[2,90,128]{2,1,0:T(8,128)S(1)}, f32[2,90,128]{2,1,0:T(8,128)S(1)}, u32[]{:S(2)}, u32[]{:S(2)}) collective-permute-start(f32[2,90,128]{2,1,0:T(8,128)S(1)} %pad_maximum_fusion), channel_id=1, source_target_pairs={{0,128},{64,192},{128,0},{192,64},{256,384},{320,448},{384,256},{4... | collective-permute-start | bytes 276488 | tf_op jit(solution)/shard_map/ppermute | solution.py:61
  35.4 2.6 %collective-permute-start.3 = (f32[2,90,128]{2,1,0:T(8,128)S(1)}, f32[2,90,128]{2,1,0:T(8,128)S(1)}, u32[]{:S(2)}, u32[]{:S(2)}) collective-permute-start(f32[2,90,128]{2,1,0:T(8,128)S(1)} %pad_maximum_fusion), channel_id=1, source_target_pairs={{0,64},{64,128},{128,192},{192,0},{256,320},{320,384},{384,448},{4... | collective-permute-start | bytes 276488 | tf_op jit(solution)/shard_map/ppermute | solution.py:61
  38.0 0.0 collective-permute-done.1
  38.0 2.2 %collective-permute-done.2 = f32[2,90,128]{2,1,0:T(8,128)S(1)} collective-permute-done((f32[2,90,128]{2,1,0:T(8,128)S(1)}, f32[2,90,128]{2,1,0:T(8,128)S(1)}, u32[]{:S(2)}, u32[]{:S(2)}) %collective-permute-start.2) | collective-permute-done | bytes 92192 | tf_op jit(solution)/shard_map/ppermute | solution.py:61
  40.3 2.0 %collective-permute-done.3 = f32[2,90,128]{2,1,0:T(8,128)S(1)} collective-permute-done((f32[2,90,128]{2,1,0:T(8,128)S(1)}, f32[2,90,128]{2,1,0:T(8,128)S(1)}, u32[]{:S(2)}, u32[]{:S(2)}) %collective-permute-start.3) | collective-permute-done | bytes 92192 | tf_op jit(solution)/shard_map/ppermute | solution.py:61
  42.4 0.2 copy.11
  42.6 0.0 all-to-all-done.parts_ref
  42.6 0.1 copy.12
  42.8 9.9 %all_to_all.20 = f32[4,2,90,128]{3,1,2,0:T(2,128)S(1)} all-to-all(f32[4,2,90,128]{3,1,2,0:T(2,128)S(1)} %copy.12), channel_id=1, replica_groups=mesh['mem'=8,'lat'=4,'lon'=16] {'lat'}, dimensions={0} | all-to-all | bytes 737280 | tf_op jit(solution)/shard_map/all_to_all | solution.py:164
  52.7 2.7 %shard_map.69 = bf16[16,184,128]{2,1,0:T(8,128)(2,1)} custom-call(bf16[4,16,184,128]{3,2,1,0:T(8,128)(2,1)S(1)} %all-to-all-done.parts_ref, f32[4,2,90,128]{3,2,1,0:T(8,128)S(1)} %copy.13.grads_ref, bf16[512,128]{1,0:T(8,128)(2,1)S(1)} %fusion.21.table_ref), custom_call_target="tpu_custom_call" | custom-call | flops 385875968 | bytes 3014656 | tf_op jit(solution)/shard_map/pallas_call | solution.py:130
  55.4 17.1 %all-to-all-start.2 = ((bf16[16,184,128]{2,1,0:T(8,128)(2,1)}), bf16[16,184,128]{2,1,0:T(8,128)(2,1)S(1)}, u32[]{:S(2)}, u32[]{:S(2)}) async-start(bf16[16,184,128]{2,1,0:T(8,128)(2,1)} %shard_map.69), calls=%async_computation.2 | async-start | bytes 1507328 | tf_op jit(solution)/shard_map/all_to_all | solution.py:167
  72.5 0.6 fusion.28
  73.1 5.9 %compare_select_fusion.1 = (f32[184,1024]{1,0:T(8,128)S(1)}, f32[184,1024]{1,0:T(8,128)S(1)}) fusion(s32[1024]{0:T(1024)S(1)} %get-tuple-element.19, s32[184]{0:T(256)S(1)} %get-tuple-element.22, s32[1024]{0:T(1024)S(1)} %get-tuple-element.20, s32[184]{0:T(256)S(1)} %get-tuple-element.21), kind=kLoop, calls=%fused_computation.11 | loop fusion | flops 3956736 | bytes 1516992 | tf_op jit(solution)/shard_map/jit(_where)/select_n | solution.py:38
  79.1 27.6 %all-to-all-done.2 = bf16[16,184,128]{2,1,0:T(8,128)(2,1)S(1)} async-done(((bf16[16,184,128]{2,1,0:T(8,128)(2,1)}), bf16[16,184,128]{2,1,0:T(8,128)(2,1)S(1)}, u32[]{:S(2)}, u32[]{:S(2)}) %all-to-all-start.2) | async-done | bytes 753696 | tf_op jit(solution)/shard_map/all_to_all | solution.py:167
  106.6 0.0 copy-start.1
  106.6 0.0 copy-start.3
  106.6 2.8 %fusion.2 = bf16[1024,128]{1,0:T(8,128)(2,1)} fusion(bf16[16,184,128]{2,1,0:T(8,128)(2,1)S(1)} %all-to-all-done.2, f32[184,1024]{1,0:T(8,128)S(1)} %get-tuple-element.15, f32[16,1024]{1,0:T(8,128)S(1)} %get-tuple-element.17, f32[184,1024]{1,0:T(8,128)S(1)} %get-tuple-element.14, f32[16,1024]{1,0:T(8,128)S(1)} %get-tuple-element.16), kind=kOutput, calls=%fused_computation.3 | convolution fusion | flops 783941632 | bytes 2654208 | tf_op jit(solution)/shard_map/nk,nq->kq/dot_general | solution.py:170
  109.4 3.4 %all-to-all-start.3 = ((bf16[4,2,128,128]{3,2,1,0:T(8,128)(2,1)}), bf16[4,2,128,128]{3,2,1,0:T(8,128)(2,1)S(1)}, u32[]{:S(2)}, u32[]{:S(2)}) async-start(bf16[4,2,128,128]{3,2,1,0:T(8,128)(2,1)} %bitcast.10), calls=%async_computation.3 | async-start | bytes 524288 | tf_op jit(solution)/shard_map/all_to_all | solution.py:174
  112.8 0.0 copy-done
  112.8 0.2 dynamic-slice_reduce_fusion
  113.0 0.0 copy-done.1
  113.0 0.2 multiply_reduce_fusion
  113.2 0.7 broadcast_in_dim.15
  113.9 5.9 %all-to-all-done.3 = bf16[4,2,128,128]{3,2,1,0:T(8,128)(2,1)S(1)} async-done(((bf16[4,2,128,128]{3,2,1,0:T(8,128)(2,1)}), bf16[4,2,128,128]{3,2,1,0:T(8,128)(2,1)S(1)}, u32[]{:S(2)}, u32[]{:S(2)}) %all-to-all-start.3) | async-done | bytes 262176 | tf_op jit(solution)/shard_map/all_to_all | solution.py:174
  119.8 0.0 copy-done.3
  119.8 0.9 convert_multiply_fusion
  (18 shorter events, 0.2 us)
Async XLA Ops:
  0.6 112.2 %copy-start = (f32[8,8]{1,0:T(8,128)S(1)}, f32[8,8]{1,0:T(8,128)}, u32[]{:S(2)}) copy-start(f32[8,8]{1,0:T(8,128)} %param.8) | copy-start | bytes 772
  5.3 6.0 %copy-start.2 = (f32[1,90,128]{2,0,1:T(1,128)S(1)}, f32[1,90,128]{2,0,1:T(1,128)}, u32[]{:S(2)}) copy-start(f32[1,90,128]{2,0,1:T(1,128)} %param.6) | copy-start | bytes 138244
  5.3 37.3 %all-to-all-start = ((bf16[4,16,184,128]{3,2,1,0:T(8,128)(2,1)}), bf16[4,16,184,128]{3,2,1,0:T(8,128)(2,1)S(1)}, u32[]{:S(2)}, u32[]{:S(2)}) async-start(bf16[4,16,184,128]{3,2,1,0:T(8,128)(2,1)} %shard_map.68), calls=%async_computation | async-start | bytes 6029312 | tf_op jit(solution)/shard_map/all_to_all | solution.py:155
  11.4 17.0 %collective-permute-start = (f32[90,128]{1,0:T(8,128)S(1)}, f32[90,128]{1,0:T(8,128)S(1)}, u32[]{:S(2)}, u32[]{:S(2)}) collective-permute-start(f32[90,128]{1,0:T(8,128)S(1)} %bitcast.39), channel_id=1, source_target_pairs={{0,256},{64,320},{128,384},{192,448},{256,0},{320,64},{384,128},{4... | collective-permute-start | bytes 138248 | tf_op jit(solution)/shard_map/ppermute | solution.py:159
  28.5 9.5 %collective-permute-start.1 = (f32[2,90,128]{2,1,0:T(8,128)S(1)}, f32[2,90,128]{2,1,0:T(8,128)S(1)}, u32[]{:S(2)}, u32[]{:S(2)}) collective-permute-start(f32[2,90,128]{2,1,0:T(8,128)S(1)} %pad_maximum_fusion), channel_id=1, source_target_pairs={{0,192},{64,0},{128,64},{192,128},{256,448},{320,256},{384,320},{4... | collective-permute-start | bytes 276488 | tf_op jit(solution)/shard_map/ppermute | solution.py:61
  33.1 7.2 %collective-permute-start.2 = (f32[2,90,128]{2,1,0:T(8,128)S(1)}, f32[2,90,128]{2,1,0:T(8,128)S(1)}, u32[]{:S(2)}, u32[]{:S(2)}) collective-permute-start(f32[2,90,128]{2,1,0:T(8,128)S(1)} %pad_maximum_fusion), channel_id=1, source_target_pairs={{0,128},{64,192},{128,0},{192,64},{256,384},{320,448},{384,256},{4... | collective-permute-start | bytes 276488 | tf_op jit(solution)/shard_map/ppermute | solution.py:61
  35.4 6.9 %collective-permute-start.3 = (f32[2,90,128]{2,1,0:T(8,128)S(1)}, f32[2,90,128]{2,1,0:T(8,128)S(1)}, u32[]{:S(2)}, u32[]{:S(2)}) collective-permute-start(f32[2,90,128]{2,1,0:T(8,128)S(1)} %pad_maximum_fusion), channel_id=1, source_target_pairs={{0,64},{64,128},{128,192},{192,0},{256,320},{320,384},{384,448},{4... | collective-permute-start | bytes 276488 | tf_op jit(solution)/shard_map/ppermute | solution.py:61
  55.4 51.2 %all-to-all-start.2 = ((bf16[16,184,128]{2,1,0:T(8,128)(2,1)}), bf16[16,184,128]{2,1,0:T(8,128)(2,1)S(1)}, u32[]{:S(2)}, u32[]{:S(2)}) async-start(bf16[16,184,128]{2,1,0:T(8,128)(2,1)} %shard_map.69), calls=%async_computation.2 | async-start | bytes 1507328 | tf_op jit(solution)/shard_map/all_to_all | solution.py:167
  106.6 6.4 %copy-start.1 = (f32[8,90,128]{2,0,1:T(8,128)S(1)}, f32[8,90,128]{2,0,1:T(8,128)}, u32[]{:S(2)}) copy-start(f32[8,90,128]{2,0,1:T(8,128)} %param.7) | copy-start | bytes 1105924
  106.6 13.2 %copy-start.3 = (f32[128,128]{1,0:T(8,128)S(1)}, f32[128,128]{1,0:T(8,128)}, u32[]{:S(2)}) copy-start(f32[128,128]{1,0:T(8,128)} %param.9) | copy-start | bytes 196612
  109.4 10.4 %all-to-all-start.3 = ((bf16[4,2,128,128]{3,2,1,0:T(8,128)(2,1)}), bf16[4,2,128,128]{3,2,1,0:T(8,128)(2,1)S(1)}, u32[]{:S(2)}, u32[]{:S(2)}) async-start(bf16[4,2,128,128]{3,2,1,0:T(8,128)(2,1)} %bitcast.10), calls=%async_computation.3 | async-start | bytes 524288 | tf_op jit(solution)/shard_map/all_to_all | solution.py:174

commit v3 on v2

--- a/solution.py
+++ b/solution.py
@@ -17,28 +17,25 @@
     return jnp.cos(jnp.float32(2.0 * jnp.pi) * (phase % period).astype(jnp.float32) / period)
 
 
-def lon_table_make(n_lon, k_lon, blocks, rows, waves):
+def lon_table_make(n_lon, places, waves):
+    half = waves.shape[0] // 2
+    sine = waves >= half
+    number = jnp.where(sine, waves - half + 1, waves)[:, None]
+    phase = number * places[None, :] - jnp.where(sine, n_lon // 4, 0)[:, None]
+    return cosine(phase, n_lon) * jnp.sqrt(jnp.float32(2.0) / n_lon)
+
+
+def lon_tables_make(n_lon, blocks, waves):
     band = n_lon // blocks
     whole = band // TILE * TILE
-    column = waves
-    level = column // (k_lon // 4) % PAIR
-    number = column // (k_lon // 4 * PAIR) * (k_lon // 4) + column % (k_lon // 4)
-    sine = number >= k_lon // 2
-    wave = jnp.where(sine, number - k_lon // 2 + 1, number)[None, :]
-    shift = jnp.where(sine, n_lon // 4, 0)[None, :]
-    row = jnp.arange(rows, dtype=jnp.int32)[:, None]
-    starts = jnp.arange(blocks, dtype=jnp.int32)[:, None] * band * wave - shift
-    last = row - PAIR * whole
-    place = jnp.where(last < 0, row % whole, whole + last % (band - whole))
-    row_level = jnp.where(last < 0, row // whole, last // (band - whole))
-    places = place * wave
-    factor = jnp.sqrt(jnp.float32(2.0) / n_lon)
-    cos_start, sin_start = cosine(starts, n_lon) * factor, cosine(starts - n_lon // 4, n_lon) * factor
-    own = row_level == level[None, :]
-    cos_place = jnp.where(own, cosine(places, n_lon), 0.0)
-    sin_place = jnp.where(own, cosine(places - n_lon // 4, n_lon), 0.0)
-    table = cos_start[:, None] * cos_place[None] - sin_start[:, None] * sin_place[None]
-    return table.astype(jnp.bfloat16).reshape(blocks * rows, PAIR * k_lon)
+    left = band - whole
+    column = jnp.arange(blocks * whole, dtype=jnp.int32)
+    main = lon_table_make(n_lon, column // whole * band + column % whole, waves)
+    column = jnp.arange(blocks * TILE, dtype=jnp.int32)
+    row = column % TILE
+    tail = lon_table_make(n_lon, column // TILE * band + whole + row % left, waves)
+    tails = [jnp.where((row // left == level)[None, :], tail, 0.0) for level in range(PAIR)]
+    return main.astype(jnp.bfloat16), jnp.stack(tails).astype(jnp.bfloat16)
 
 
 def lat_table_make(cells, n_lat, k_lat):
@@ -54,16 +51,6 @@
 
 def partners(size, flip):
     return [(i, i ^ flip) for i in range(size)]
-
-
-def from_ahead(field):
-    rings = [[(i, i // 4 * 4 + (i - step) % 4) for i in range(8)] for step in (1, 2, 3)]
-    return [lax.ppermute(field, "mem", pairs) for pairs in rings]
-
-
-def by_position(mine, ahead, me):
-    turned = jnp.stack([mine, *ahead, mine, *ahead[:2]])
-    return lax.dynamic_slice_in_dim(turned, (4 - me) % 4, 4, 0)
 
 
 def pack_rows(fields, rows):
@@ -104,13 +91,14 @@
     )(members)
 
 
-def lat_sums_kernel(parts_ref, grads_ref, table_ref, out_ref, packed):
+def lat_sums_kernel(x_ref, parts_ref, grads_ref, table_ref, out_ref, packed):
     bands, count, rows, _ = parts_ref.shape
+    x = x_ref[0]
 
     @pl.when(pl.program_id(0) == 0)
     def _():
         for part in range(bands):
-            packed[part] = pack_rows([grads_ref[part, place] for place in range(PAIR)], rows)
+            packed[part] = pack_rows([grads_ref[(part + 4 - x) % 4, place] for place in range(PAIR)], rows)
 
     for m in range(count):
         product = [
@@ -123,7 +111,7 @@
         out_ref[m] = sums.astype(jnp.bfloat16)
 
 
-def lat_sums(parts, grads, table):
+def lat_sums(x, parts, grads, table):
     bands, count, rows, lat = parts.shape
     waves = table.shape[1]
     step = min(4, count)
@@ -132,6 +120,7 @@
         out_shape=pltpu.HBM((count, rows, waves), jnp.bfloat16),
         grid=(count // step,),
         in_specs=[
+            pl.BlockSpec(memory_space=pltpu.SMEM),
             pl.BlockSpec((bands, step, rows, lat), lambda i: (0, i, 0, 0)),
             pl.BlockSpec(grads.shape, lambda i: (0, 0, 0, 0)),
             pl.BlockSpec((bands * lat, waves), lambda i: (0, 0)),
@@ -142,35 +131,71 @@
         cost_estimate=pl.CostEstimate(
             flops=2 * parts.size * waves, bytes_accessed=2 * parts.size, transcendentals=0
         ),
-    )(parts, grads, table)
+    )(jnp.reshape(x, (1,)).astype(jnp.int32), parts, grads, table)
+
+
+def zonal_kernel(rows_ref, main_ref, tails_ref, out_ref):
+    blocks = rows_ref.shape[0]
+    whole = main_ref.shape[1] // blocks
+    bands = [rows_ref[block].astype(jnp.float32) for block in range(blocks)]
+    last = jnp.concatenate([band[PAIR * whole :] for band in bands]).astype(jnp.bfloat16)
+    for level in range(PAIR):
+        first = [band[level * whole : (level + 1) * whole] for band in bands]
+        sums = jnp.dot(
+            main_ref[...], jnp.concatenate(first).astype(jnp.bfloat16), preferred_element_type=jnp.float32
+        ) + jnp.dot(tails_ref[level], last, preferred_element_type=jnp.float32)
+        quarter = sums.shape[0] // 4
+        for part in range(4):
+            out_ref[part, level] = sums[part * quarter : (part + 1) * quarter].astype(jnp.bfloat16)
+
+
+def zonal_sums(rows, main, tails):
+    waves, k_lat = main.shape[0], rows.shape[2]
+    return pl.pallas_call(
+        zonal_kernel,
+        out_shape=pltpu.HBM((4, PAIR, waves // 4, k_lat), jnp.bfloat16),
+        in_specs=[pl.BlockSpec(memory_space=pltpu.VMEM)] * 3,
+        out_specs=pl.BlockSpec(memory_space=pltpu.VMEM),
+        compiler_params=pltpu.CompilerParams(vmem_limit_bytes=24 * 2**20),
+        cost_estimate=pl.CostEstimate(
+            flops=2 * PAIR * main.size * k_lat, bytes_accessed=2 * (main.size + rows.size), transcendentals=0
+        ),
+    )(rows, main, tails)
 
 
 def local(members, grad_field, static_std, vert_mix, loc_weights):
     mem_local, levels, lon_local, lat_local = members.shape
     mem = lax.axis_index("mem")
     half_z, y = mem // 4, mem % 4
+    x = lax.axis_index("lat")
     rows = -(-PAIR * lon_local // TILE) * TILE
 
     sent = spread(members.transpose(0, 2, 1, 3), rows)
     parts = lax.all_to_all(sent, "lat", split_axis=0, concat_axis=0, tiled=True)
 
     lat_table = lat_table_make(after(jnp.arange(NLAT, dtype=jnp.int32), sent), NLAT, KLAT)
-    own_grad = after(grad_field, lat_table)[0]
+    own_grad = grad_field[0]
     far_grad = lax.ppermute(own_grad, "mem", partners(8, 4))
     mine = jnp.stack([jnp.where(half_z == 0, own_grad, far_grad), jnp.where(half_z == 0, far_grad, own_grad)])
-    grads = by_position(mine, from_ahead(mine), y)
+    beside = lax.ppermute(mine, "mem", partners(8, 1))
+    two = jnp.stack([jnp.where(y % 2 == 0, mine, beside), jnp.where(y % 2 == 0, beside, mine)])
+    others = lax.ppermute(two, "mem", partners(8, 3))
+    grads = jnp.concatenate([jnp.where(y < 2, two, others), jnp.where(y < 2, others, two)])
     grads = grads.transpose(1, 0, 2, 3).reshape(levels, lon_local, lat_local)
-    pairs = after(grads.reshape(4, PAIR, lon_local, lat_local), parts)
-    met = lax.all_to_all(pairs, "lat", split_axis=0, concat_axis=0, tiled=True)
-    sums = lat_sums(parts, met, lat_table)
+    pairs = grads.reshape(4, PAIR, lon_local, lat_local)
+
+    def pair(step):
+        return lax.dynamic_index_in_dim(pairs, (x + step) % 4, 0, keepdims=False)
+
+    met = jnp.stack(
+        [pair(0)]
+        + [lax.ppermute(pair(4 - d), "lat", [(i, (i - d) % 4) for i in range(4)]) for d in (1, 2, 3)]
+    )
+    sums = lat_sums(x, parts, met, lat_table)
 
     whole = lax.all_to_all(sums, "lon", split_axis=0, concat_axis=0, tiled=True)
-    columns = after(jnp.arange(PAIR * KLON, dtype=jnp.int32), sums)
-    lon_table = lon_table_make(NLON, KLON, mem_local, rows, columns)
-    zonal = jnp.einsum(
-        "nk,nq->kq", lon_table, whole.reshape(mem_local * rows, KLAT), preferred_element_type=jnp.float32
-    ).astype(jnp.bfloat16)
-    zonal = zonal.reshape(4, PAIR, KLON // 4, KLAT)
+    waves = after(jnp.arange(KLON, dtype=jnp.int32), sums)
+    zonal = zonal_sums(whole, *lon_tables_make(NLON, mem_local, waves))
     alpha = lax.all_to_all(zonal, "lat", split_axis=0, concat_axis=0, tiled=True)
     alpha_grad = alpha.reshape(levels, KLON // 4, KLAT).astype(jnp.float32) * loc_weights[None]
 

time: 122 us -> 120 us (0.984)
  blocking collectives: 9.89 us -> 0 us
  other arithmetic: 8.71 us -> 16.1 us
  starting transfers between devices: 50.4 us -> 57.3 us
  waiting for transfers between devices: 39.2 us -> 34.3 us
  matrix products: 2.76 us -> 0 us
  Pallas kernels: 7.41 us -> 9.11 us
    convert_element_type x0 -> x1, other arithmetic: none -> 12.3 us  [lon_tables_make(): return (main.astype(jnp.bfloat16), jnp.stack(tails).astype(jnp.bfloat16))]
    all_to_all x1 -> x0, blocking collectives: 9.89 us -> none  [local(): met = lax.all_to_all(pairs, 'lat', split_axis=0, concat_axis=0, tiled=True)]
    ppermute x3 -> x5, starting transfers between devices: 9.5 us -> 18.4 us  [the longest x3 10.5 us: local(): lax.ppermute(pair(4 - d), 'lat', [(i, (i - d) % 4) for i in range(4)])]
    all_to_all x1, waiting for transfers between devices: 27.6 us -> 20.2 us  [local(): whole = lax.all_to_all(sums, 'lon', split_axis=0, concat_axis=0, tiled=True)]
    select_n x3 -> x2, other arithmetic: 5.96 us -> 0.03 us  [the longest x1 0.03 us: local(): jnp.where(y < 2, two, others)]
    ppermute x3 -> x5, waiting for transfers between devices: 4.2 us -> 7.01 us  [the longest x1 3.33 us: local(): others = lax.ppermute(two, 'mem', partners(8, 3))]
    dot_general x1 -> x0, matrix products: 2.76 us -> none  [local(): jnp.einsum('nk,nq->kq', lon_table, whole.reshape(mem_local * rows, KLAT),...]
    all_to_all x1, starting transfers between devices: 17.1 us -> 14.9 us  [local(): whole = lax.all_to_all(sums, 'lon', split_axis=0, concat_axis=0, tiled=True)]
  transfers between devices with their start and end apart: 7 -> 9, of which waited for: 5 -> 6; matrix products, arithmetic and copies ran while one was open for 7% -> 14% of each run, Pallas kernels for 0% -> 0%
where the time goes in v3:
time: 120 us; the launch traced here: 119 us
  starting transfers between devices  57.3 us (48%)
  waiting for transfers between devices  34.3 us (29%)
  other arithmetic  16.1 us (13%)
  Pallas kernels  9.11 us (8%)
    all_to_all x1, waiting for transfers between devices, local(): whole = lax.all_to_all(sums, 'lon', split_axis=0, concat_axis=0, tiled=True)  20.2 us
    ppermute x1, starting transfers between devices, local(): far_grad = lax.ppermute(own_grad, 'mem', partners(8, 4))  15.4 us
    all_to_all x1, starting transfers between devices, local(): whole = lax.all_to_all(sums, 'lon', split_axis=0, concat_axis=0, tiled=True)  14.9 us
    convert_element_type x1, other arithmetic, lon_tables_make(): return (main.astype(jnp.bfloat16), jnp.stack(tails).astype(jnp.bfloat16))  12.3 us
    ppermute x3, starting transfers between devices, local(): lax.ppermute(pair(4 - d), 'lat', [(i, (i - d) % 4) for i in range(4)])  10.5 us
    all_to_all x1, waiting for transfers between devices, local(): lax.all_to_all(zonal, 'lat', split_axis=0, concat_axis=0, tiled=True)  5.51 us
    all_to_all x1, starting transfers between devices, local(): parts = lax.all_to_all(sent, 'lat', split_axis=0, concat_axis=0, tiled=True)  4.97 us
    pallas_call x1, Pallas kernels, spread(): pl.pallas_call(spread_kernel, out_shape=jax.ShapeDtypeStruct((levels // P...  4.73 us
  transfers between devices with their start and end apart: 9, of which 6 were waited for; matrix products, arithmetic and copies ran while one was open for 14% of the time, Pallas kernels for 0%

profile of v3, /device:TPU:1, one launch (start us, length us, event | category | flops | bytes accessed | tf_op | source)
XLA Modules:
  0.0 119.0 jit_solution(16096269671206992169)
XLA Ops:
  0.6 0.0 copy-start
  0.6 4.7 %shard_map.68 = bf16[4,16,184,128]{3,2,1,0:T(8,128)(2,1)} custom-call(bf16[16,90,8,128]{3,2,1,0:T(8,128)(2,1)} %bitcast.33), custom_call_target="tpu_custom_call" | custom-call | flops 1474560 | bytes 5898240 | tf_op jit(solution)/shard_map/pallas_call | solution.py:82
  5.4 0.0 copy-start.4
  5.4 5.0 %all-to-all-start = ((bf16[4,16,184,128]{3,2,1,0:T(8,128)(2,1)}), bf16[4,16,184,128]{3,2,1,0:T(8,128)(2,1)S(1)}, u32[]{:S(2)}, u32[]{:S(2)}) async-start(bf16[4,16,184,128]{3,2,1,0:T(8,128)(2,1)} %shard_map.68), calls=%async_computation | async-start | bytes 6029312 | tf_op jit(solution)/shard_map/all_to_all | solution.py:174
  10.4 0.0 copy-done.4
  10.4 15.4 %collective-permute-start = (f32[90,128]{1,0:T(8,128)S(1)}, f32[90,128]{1,0:T(8,128)S(1)}, u32[]{:S(2)}, u32[]{:S(2)}) collective-permute-start(f32[90,128]{1,0:T(8,128)S(1)} %bitcast.39), channel_id=1, source_target_pairs={{0,256},{64,320},{128,384},{192,448},{256,0},{320,64},{384,128},{4... | collective-permute-start | bytes 138248 | tf_op jit(solution)/shard_map/ppermute | solution.py:178
  25.8 1.6 %collective-permute-done = f32[90,128]{1,0:T(8,128)S(1)} collective-permute-done((f32[90,128]{1,0:T(8,128)S(1)}, f32[90,128]{1,0:T(8,128)S(1)}, u32[]{:S(2)}, u32[]{:S(2)}) %collective-permute-start) | collective-permute-done | bytes 46112 | tf_op jit(solution)/shard_map/ppermute | solution.py:178
  27.4 3.2 %collective-permute-start.1 = (f32[2,90,128]{2,1,0:T(8,128)S(1)}, f32[2,90,128]{2,1,0:T(8,128)S(1)}, u32[]{:S(2)}, u32[]{:S(2)}) collective-permute-start(f32[2,90,128]{2,1,0:T(8,128)S(1)} %pad_maximum_fusion.3), channel_id=1, source_target_pairs={{0,64},{64,0},{128,192},{192,128},{256,320},{320,256},{384,448},{4... | collective-permute-start | bytes 276488 | tf_op jit(solution)/shard_map/ppermute | solution.py:180
  30.8 2.3 %collective-permute-done.1 = f32[2,90,128]{2,1,0:T(8,128)S(1)} collective-permute-done((f32[2,90,128]{2,1,0:T(8,128)S(1)}, f32[2,90,128]{2,1,0:T(8,128)S(1)}, u32[]{:S(2)}, u32[]{:S(2)}) %collective-permute-start.1) | collective-permute-done | bytes 92192 | tf_op jit(solution)/shard_map/ppermute | solution.py:180
  33.1 4.6 %collective-permute-start.2 = (f32[2,2,90,128]{3,2,1,0:T(8,128)S(1)}, f32[2,2,90,128]{3,2,1,0:T(8,128)S(1)}, u32[]{:S(2)}, u32[]{:S(2)}) collective-permute-start(f32[2,2,90,128]{3,2,1,0:T(8,128)S(1)} %pad_maximum_fusion.2), channel_id=1, source_target_pairs={{0,192},{64,128},{128,64},{192,0},{256,448},{320,384},{384,320},{4... | collective-permute-start | bytes 552968 | tf_op jit(solution)/shard_map/ppermute | solution.py:182
  37.8 3.3 %collective-permute-done.2 = f32[2,2,90,128]{3,2,1,0:T(8,128)S(1)} collective-permute-done((f32[2,2,90,128]{3,2,1,0:T(8,128)S(1)}, f32[2,2,90,128]{3,2,1,0:T(8,128)S(1)}, u32[]{:S(2)}, u32[]{:S(2)}) %collective-permute-start.2) | collective-permute-done | bytes 184352 | tf_op jit(solution)/shard_map/ppermute | solution.py:182
  41.2 0.0 copy-start.1
  41.3 3.1 %collective-permute-start.5 = (f32[2,90,128]{2,1,0:T(8,128)S(1)}, f32[2,90,128]{2,1,0:T(8,128)S(1)}, u32[]{:S(2)}, u32[]{:S(2)}) collective-permute-start(f32[2,90,128]{2,1,0:T(8,128)S(1)} %get-tuple-element.9), channel_id=1, source_target_pairs={{0,16},{16,32},{32,48},{48,0},{1,17},{17,33},{33,49},{49,1},{2,18}... | collective-permute-start | bytes 276488 | tf_op jit(solution)/shard_map/ppermute | solution.py:192
  44.4 4.5 %collective-permute-start.4 = (f32[2,90,128]{2,1,0:T(8,128)S(1)}, f32[2,90,128]{2,1,0:T(8,128)S(1)}, u32[]{:S(2)}, u32[]{:S(2)}) collective-permute-start(f32[2,90,128]{2,1,0:T(8,128)S(1)} %get-tuple-element.10), channel_id=1, source_target_pairs={{0,32},{16,48},{32,0},{48,16},{1,33},{17,49},{33,1},{49,17},{2,34}... | collective-permute-start | bytes 276488 | tf_op jit(solution)/shard_map/ppermute | solution.py:192
  48.9 2.9 %collective-permute-start.3 = (f32[2,90,128]{2,1,0:T(8,128)S(1)}, f32[2,90,128]{2,1,0:T(8,128)S(1)}, u32[]{:S(2)}, u32[]{:S(2)}) collective-permute-start(f32[2,90,128]{2,1,0:T(8,128)S(1)} %get-tuple-element.11), channel_id=1, source_target_pairs={{0,48},{16,0},{32,16},{48,32},{1,49},{17,1},{33,17},{49,33},{2,50}... | collective-permute-start | bytes 276488 | tf_op jit(solution)/shard_map/ppermute | solution.py:192
  51.8 1.0 fusion.13.table_ref
  52.9 0.0 collective-permute-done.5
  52.9 0.0 collective-permute-done.4
  52.9 1.4 %collective-permute-done.3 = f32[2,90,128]{2,1,0:T(8,128)S(1)} collective-permute-done((f32[2,90,128]{2,1,0:T(8,128)S(1)}, f32[2,90,128]{2,1,0:T(8,128)S(1)}, u32[]{:S(2)}, u32[]{:S(2)}) %collective-permute-start.3) | collective-permute-done | bytes 92192 | tf_op jit(solution)/shard_map/ppermute | solution.py:192
  54.3 0.0 copy-done.1
  54.3 0.0 all-to-all-done.parts_ref
  54.3 2.7 %shard_map.69 = bf16[16,184,128]{2,1,0:T(8,128)(2,1)} custom-call(s32[1]{0:T(128)} %bitcast.x_ref, bf16[4,16,184,128]{3,2,1,0:T(8,128)(2,1)S(1)} %all-to-all-done.parts_ref, f32[4,2,90,128]{3,2,1,0:T(8,128)S(1)} %pad_maximum_fusion.grads_ref, bf16[512,128]{1,0:T(8,128)(2,1)S(1)} %fusion.13.table_ref), custom_call_target="tpu_custom_call" | custom-call | flops 385875968 | bytes 3014656 | tf_op jit(solution)/shard_map/pallas_call | solution.py:118
  57.0 14.9 %all-to-all-start.1 = ((bf16[16,184,128]{2,1,0:T(8,128)(2,1)}), bf16[16,184,128]{2,1,0:T(8,128)(2,1)S(1)}, u32[]{:S(2)}, u32[]{:S(2)}) async-start(bf16[16,184,128]{2,1,0:T(8,128)(2,1)} %shard_map.69), calls=%async_computation.1 | async-start | bytes 1507328 | tf_op jit(solution)/shard_map/all_to_all | solution.py:196
  71.9 0.0 copy-start.2
  72.0 1.5 %select_convert_fusion.1 = (bf16[1,512,128]{2,1,0:T(8,128)(2,1)S(1)}, bf16[1,512,128]{2,1,0:T(8,128)(2,1)S(1)}) fusion(s32[512]{0:T(512)S(1)} %get-tuple-element.21, s32[128]{0:T(128)S(1)} %fusion.33, s32[512]{0:T(512)S(1)} %get-tuple-element.20, pred[128]{0:T(512)(128)(4,1)S(1)} %get-tuple-element.23, pred[128]{0:T(512)(128)(4,1)S(1)} %get-tuple-element.22), kind=kLoop, calls=%fused_computation.30 | loop fusion | flops 983040 | bytes 267008 | tf_op jit(solution)/shard_map/convert.1
  73.5 0.0 copy-start.3
  73.5 0.0 copy-start.5
  73.6 12.3 %fusion.4.main_ref = bf16[512,1408]{1,0:T(8,128)(2,1)S(1)} fusion(s32[512]{0:T(512)S(1)} %get-tuple-element.21, s32[1408]{0:T(1024)S(1)} %fusion.31, s32[512]{0:T(512)S(1)} %get-tuple-element.20), kind=kLoop, calls=%fused_computation.5 | loop fusion | flops 8650752 | bytes 1451520 | tf_op jit(solution)/shard_map/convert_element_type | solution.py:38
  85.9 20.2 %all-to-all-done.1.rows_ref = bf16[16,184,128]{2,1,0:T(8,128)(2,1)S(1)} async-done(((bf16[16,184,128]{2,1,0:T(8,128)(2,1)}), bf16[16,184,128]{2,1,0:T(8,128)(2,1)S(1)}, u32[]{:S(2)}, u32[]{:S(2)}) %all-to-all-start.1) | async-done | bytes 753696 | tf_op jit(solution)/shard_map/all_to_all | solution.py:196
  106.0 1.7 %shard_map.70 = bf16[4,2,128,128]{3,2,1,0:T(8,128)(2,1)} custom-call(bf16[16,184,128]{2,1,0:T(8,128)(2,1)S(1)} %all-to-all-done.1.rows_ref, bf16[512,1408]{1,0:T(8,128)(2,1)S(1)} %fusion.4.main_ref, bf16[2,512,128]{2,1,0:T(8,128)(2,1)S(1)} %pad_maximum_fusion.1.tails_ref), custom_call_target="tpu_custom_call" | custom-call | flops 369098752 | bytes 2195456 | tf_op jit(solution)/shard_map/pallas_call | solution.py:154
  107.7 3.7 %all-to-all-start.2 = ((bf16[4,2,128,128]{3,2,1,0:T(8,128)(2,1)}), bf16[4,2,128,128]{3,2,1,0:T(8,128)(2,1)S(1)}, u32[]{:S(2)}, u32[]{:S(2)}) async-start(bf16[4,2,128,128]{3,2,1,0:T(8,128)(2,1)} %shard_map.70), calls=%async_computation.2 | async-start | bytes 524288 | tf_op jit(solution)/shard_map/all_to_all | solution.py:199
  111.4 0.0 copy-done
  111.4 0.2 dynamic-slice_reduce_fusion
  111.5 0.0 copy-done.2
  111.5 0.2 copy.8
  111.8 0.0 copy-done.3
  111.8 0.2 multiply_reduce_fusion
  112.0 0.7 broadcast_in_dim.48
  112.7 5.5 %all-to-all-done.2 = bf16[4,2,128,128]{3,2,1,0:T(8,128)(2,1)S(1)} async-done(((bf16[4,2,128,128]{3,2,1,0:T(8,128)(2,1)}), bf16[4,2,128,128]{3,2,1,0:T(8,128)(2,1)S(1)}, u32[]{:S(2)}, u32[]{:S(2)}) %all-to-all-start.2) | async-done | bytes 262176 | tf_op jit(solution)/shard_map/all_to_all | solution.py:199
  118.2 0.0 copy-done.5
  118.2 0.9 convert_multiply_fusion
  (18 shorter events, 0.3 us)
Async XLA Ops:
  0.6 110.7 %copy-start = (f32[8,8]{1,0:T(8,128)S(1)}, f32[8,8]{1,0:T(8,128)}, u32[]{:S(2)}) copy-start(f32[8,8]{1,0:T(8,128)} %param.8) | copy-start | bytes 772
  5.4 5.0 %copy-start.4 = (f32[1,90,128]{2,0,1:T(1,128)S(1)}, f32[1,90,128]{2,0,1:T(1,128)}, u32[]{:S(2)}) copy-start(f32[1,90,128]{2,0,1:T(1,128)} %param.6) | copy-start | bytes 138244
  5.4 48.9 %all-to-all-start = ((bf16[4,16,184,128]{3,2,1,0:T(8,128)(2,1)}), bf16[4,16,184,128]{3,2,1,0:T(8,128)(2,1)S(1)}, u32[]{:S(2)}, u32[]{:S(2)}) async-start(bf16[4,16,184,128]{3,2,1,0:T(8,128)(2,1)} %shard_map.68), calls=%async_computation | async-start | bytes 6029312 | tf_op jit(solution)/shard_map/all_to_all | solution.py:174
  10.4 17.0 %collective-permute-start = (f32[90,128]{1,0:T(8,128)S(1)}, f32[90,128]{1,0:T(8,128)S(1)}, u32[]{:S(2)}, u32[]{:S(2)}) collective-permute-start(f32[90,128]{1,0:T(8,128)S(1)} %bitcast.39), channel_id=1, source_target_pairs={{0,256},{64,320},{128,384},{192,448},{256,0},{320,64},{384,128},{4... | collective-permute-start | bytes 138248 | tf_op jit(solution)/shard_map/ppermute | solution.py:178
  27.4 5.7 %collective-permute-start.1 = (f32[2,90,128]{2,1,0:T(8,128)S(1)}, f32[2,90,128]{2,1,0:T(8,128)S(1)}, u32[]{:S(2)}, u32[]{:S(2)}) collective-permute-start(f32[2,90,128]{2,1,0:T(8,128)S(1)} %pad_maximum_fusion.3), channel_id=1, source_target_pairs={{0,64},{64,0},{128,192},{192,128},{256,320},{320,256},{384,448},{4... | collective-permute-start | bytes 276488 | tf_op jit(solution)/shard_map/ppermute | solution.py:180
  33.1 8.0 %collective-permute-start.2 = (f32[2,2,90,128]{3,2,1,0:T(8,128)S(1)}, f32[2,2,90,128]{3,2,1,0:T(8,128)S(1)}, u32[]{:S(2)}, u32[]{:S(2)}) collective-permute-start(f32[2,2,90,128]{3,2,1,0:T(8,128)S(1)} %pad_maximum_fusion.2), channel_id=1, source_target_pairs={{0,192},{64,128},{128,64},{192,0},{256,448},{320,384},{384,320},{4... | collective-permute-start | bytes 552968 | tf_op jit(solution)/shard_map/ppermute | solution.py:182
  41.2 13.1 %copy-start.1 = (f32[2,4,90,128]{3,2,0,1:T(8,128)}, f32[2,4,90,128]{3,2,0,1:T(8,128)S(1)}, u32[]{:S(2)}) copy-start(f32[2,4,90,128]{3,2,0,1:T(8,128)S(1)} %maximum_bitcast_fusion) | copy-start | bytes 1105924
  41.3 11.6 %collective-permute-start.5 = (f32[2,90,128]{2,1,0:T(8,128)S(1)}, f32[2,90,128]{2,1,0:T(8,128)S(1)}, u32[]{:S(2)}, u32[]{:S(2)}) collective-permute-start(f32[2,90,128]{2,1,0:T(8,128)S(1)} %get-tuple-element.9), channel_id=1, source_target_pairs={{0,16},{16,32},{32,48},{48,0},{1,17},{17,33},{33,49},{49,1},{2,18}... | collective-permute-start | bytes 276488 | tf_op jit(solution)/shard_map/ppermute | solution.py:192
  44.4 8.5 %collective-permute-start.4 = (f32[2,90,128]{2,1,0:T(8,128)S(1)}, f32[2,90,128]{2,1,0:T(8,128)S(1)}, u32[]{:S(2)}, u32[]{:S(2)}) collective-permute-start(f32[2,90,128]{2,1,0:T(8,128)S(1)} %get-tuple-element.10), channel_id=1, source_target_pairs={{0,32},{16,48},{32,0},{48,16},{1,33},{17,49},{33,1},{49,17},{2,34}... | collective-permute-start | bytes 276488 | tf_op jit(solution)/shard_map/ppermute | solution.py:192
  48.9 5.4 %collective-permute-start.3 = (f32[2,90,128]{2,1,0:T(8,128)S(1)}, f32[2,90,128]{2,1,0:T(8,128)S(1)}, u32[]{:S(2)}, u32[]{:S(2)}) collective-permute-start(f32[2,90,128]{2,1,0:T(8,128)S(1)} %get-tuple-element.11), channel_id=1, source_target_pairs={{0,48},{16,0},{32,16},{48,32},{1,49},{17,1},{33,17},{49,33},{2,50}... | collective-permute-start | bytes 276488 | tf_op jit(solution)/shard_map/ppermute | solution.py:192
  57.0 49.0 %all-to-all-start.1 = ((bf16[16,184,128]{2,1,0:T(8,128)(2,1)}), bf16[16,184,128]{2,1,0:T(8,128)(2,1)S(1)}, u32[]{:S(2)}, u32[]{:S(2)}) async-start(bf16[16,184,128]{2,1,0:T(8,128)(2,1)} %shard_map.69), calls=%async_computation.1 | async-start | bytes 1507328 | tf_op jit(solution)/shard_map/all_to_all | solution.py:196
  71.9 39.7 %copy-start.2 = (f32[2,4,90,128]{3,2,0,1:T(8,128)S(1)}, f32[2,4,90,128]{3,2,0,1:T(8,128)}, u32[]{:S(2)}) copy-start(f32[2,4,90,128]{3,2,0,1:T(8,128)} %copy-done.1) | copy-start | bytes 1105924
  73.5 38.3 %copy-start.3 = (f32[8,90,128]{2,0,1:T(8,128)S(1)}, f32[8,90,128]{2,0,1:T(8,128)}, u32[]{:S(2)}) copy-start(f32[8,90,128]{2,0,1:T(8,128)} %param.7) | copy-start | bytes 1105924
  73.5 44.6 %copy-start.5 = (f32[128,128]{1,0:T(8,128)S(1)}, f32[128,128]{1,0:T(8,128)}, u32[]{:S(2)}) copy-start(f32[128,128]{1,0:T(8,128)} %param.9) | copy-start | bytes 196612
  107.7 10.5 %all-to-all-start.2 = ((bf16[4,2,128,128]{3,2,1,0:T(8,128)(2,1)}), bf16[4,2,128,128]{3,2,1,0:T(8,128)(2,1)S(1)}, u32[]{:S(2)}, u32[]{:S(2)}) async-start(bf16[4,2,128,128]{3,2,1,0:T(8,128)(2,1)} %shard_map.70), calls=%async_computation.2 | async-start | bytes 524288 | tf_op jit(solution)/shard_map/all_to_all | solution.py:199

commit v4 on v3

--- a/solution.py
+++ b/solution.py
@@ -98,7 +98,9 @@
     @pl.when(pl.program_id(0) == 0)
     def _():
         for part in range(bands):
-            packed[part] = pack_rows([grads_ref[(part + 4 - x) % 4, place] for place in range(PAIR)], rows)
+            packed[part] = pack_rows(
+                [grads_ref[(part + 4 - x) % 4, place].astype(jnp.float32) for place in range(PAIR)], rows
+            )
 
     for m in range(count):
         product = [
@@ -174,7 +176,7 @@
     parts = lax.all_to_all(sent, "lat", split_axis=0, concat_axis=0, tiled=True)
 
     lat_table = lat_table_make(after(jnp.arange(NLAT, dtype=jnp.int32), sent), NLAT, KLAT)
-    own_grad = grad_field[0]
+    own_grad = grad_field[0].astype(jnp.bfloat16)
     far_grad = lax.ppermute(own_grad, "mem", partners(8, 4))
     mine = jnp.stack([jnp.where(half_z == 0, own_grad, far_grad), jnp.where(half_z == 0, far_grad, own_grad)])
     beside = lax.ppermute(mine, "mem", partners(8, 1))
@@ -200,7 +202,7 @@
     alpha_grad = alpha.reshape(levels, KLON // 4, KLAT).astype(jnp.float32) * loc_weights[None]
 
     mix = after(lax.dynamic_index_in_dim(vert_mix, mem, 1, keepdims=False), sums)
-    static_grad = jnp.sum(mix[:, None, None] * (static_std * grads), axis=0)
+    static_grad = jnp.sum(mix[:, None, None] * (static_std * grads.astype(jnp.float32)), axis=0)
     return (alpha_grad, static_grad[None])
 
 

time: 120 us -> 119 us (level)
  waiting for transfers between devices: 34.3 us -> 32.1 us
  transfers between devices with their start and end apart: 9 -> 9, of which waited for: 6 -> 6; matrix products, arithmetic and copies ran while one was open for 14% -> 15% of each run, Pallas kernels for 0% -> 0%
where the time goes in v4:
time: 119 us; the launch traced here: 117 us
  starting transfers between devices  57.1 us (48%)
  waiting for transfers between devices  32.1 us (27%)
  other arithmetic  16.9 us (14%)
  Pallas kernels  9.11 us (8%)
    all_to_all x1, waiting for transfers between devices, local(): whole = lax.all_to_all(sums, 'lon', split_axis=0, concat_axis=0, tiled=True)  20.2 us
    ppermute x1, starting transfers between devices, local(): far_grad = lax.ppermute(own_grad, 'mem', partners(8, 4))  15.4 us
    all_to_all x1, starting transfers between devices, local(): whole = lax.all_to_all(sums, 'lon', split_axis=0, concat_axis=0, tiled=True)  14.9 us
    convert_element_type x1, other arithmetic, lon_tables_make(): return (main.astype(jnp.bfloat16), jnp.stack(tails).astype(jnp.bfloat16))  12.3 us
    ppermute x3, starting transfers between devices, local(): lax.ppermute(pair(4 - d), 'lat', [(i, (i - d) % 4) for i in range(4)])  10.6 us
    all_to_all x1, waiting for transfers between devices, local(): lax.all_to_all(zonal, 'lat', split_axis=0, concat_axis=0, tiled=True)  5.51 us
    all_to_all x1, starting transfers between devices, local(): parts = lax.all_to_all(sent, 'lat', split_axis=0, concat_axis=0, tiled=True)  4.97 us
    pallas_call x1, Pallas kernels, spread(): pl.pallas_call(spread_kernel, out_shape=jax.ShapeDtypeStruct((levels // P...  4.73 us
  transfers between devices with their start and end apart: 9, of which 6 were waited for; matrix products, arithmetic and copies ran while one was open for 15% of the time, Pallas kernels for 0%

profile of v4, /device:TPU:1, one launch (start us, length us, event | category | flops | bytes accessed | tf_op | source)
XLA Modules:
  0.0 117.4 jit_solution(15221835541773618357)
XLA Ops:
  0.6 0.0 copy-start
  0.6 4.7 %shard_map.68 = bf16[4,16,184,128]{3,2,1,0:T(8,128)(2,1)} custom-call(bf16[16,90,8,128]{3,2,1,0:T(8,128)(2,1)} %bitcast.33), custom_call_target="tpu_custom_call" | custom-call | flops 1474560 | bytes 5898240 | tf_op jit(solution)/shard_map/pallas_call | solution.py:82
  5.4 0.0 copy-start.4
  5.4 5.0 %all-to-all-start = ((bf16[4,16,184,128]{3,2,1,0:T(8,128)(2,1)}), bf16[4,16,184,128]{3,2,1,0:T(8,128)(2,1)S(1)}, u32[]{:S(2)}, u32[]{:S(2)}) async-start(bf16[4,16,184,128]{3,2,1,0:T(8,128)(2,1)} %shard_map.68), calls=%async_computation | async-start | bytes 6029312 | tf_op jit(solution)/shard_map/all_to_all | solution.py:176
  10.4 0.0 copy-done.4
  10.4 15.4 %collective-permute-start = (bf16[90,128]{1,0:T(8,128)(2,1)S(1)}, bf16[90,128]{1,0:T(8,128)(2,1)S(1)}, u32[]{:S(2)}, u32[]{:S(2)}) collective-permute-start(bf16[90,128]{1,0:T(8,128)(2,1)S(1)} %bitcast.39), channel_id=1, source_target_pairs={{0,256},{64,320},{128,384},{192,448},{256,0},{320,64},{384,128},{4... | collective-permute-start | bytes 69128 | tf_op jit(solution)/shard_map/ppermute | solution.py:180
  25.9 1.3 %collective-permute-done = bf16[90,128]{1,0:T(8,128)(2,1)S(1)} collective-permute-done((bf16[90,128]{1,0:T(8,128)(2,1)S(1)}, bf16[90,128]{1,0:T(8,128)(2,1)S(1)}, u32[]{:S(2)}, u32[]{:S(2)}) %collective-permute-start) | collective-permute-done | bytes 23072 | tf_op jit(solution)/shard_map/ppermute | solution.py:180
  27.2 3.2 %collective-permute-start.1 = (bf16[2,90,128]{2,1,0:T(8,128)(2,1)S(1)}, bf16[2,90,128]{2,1,0:T(8,128)(2,1)S(1)}, u32[]{:S(2)}, u32[]{:S(2)}) collective-permute-start(bf16[2,90,128]{2,1,0:T(8,128)(2,1)S(1)} %pad_maximum_fusion.3), channel_id=1, source_target_pairs={{0,64},{64,0},{128,192},{192,128},{256,320},{320,256},{384,448},{4... | collective-permute-start | bytes 138248 | tf_op jit(solution)/shard_map/ppermute | solution.py:182
  30.4 1.9 %collective-permute-done.1 = bf16[2,90,128]{2,1,0:T(8,128)(2,1)S(1)} collective-permute-done((bf16[2,90,128]{2,1,0:T(8,128)(2,1)S(1)}, bf16[2,90,128]{2,1,0:T(8,128)(2,1)S(1)}, u32[]{:S(2)}, u32[]{:S(2)}) %collective-permute-start.1) | collective-permute-done | bytes 46112 | tf_op jit(solution)/shard_map/ppermute | solution.py:182
  32.4 4.3 %collective-permute-start.2 = (bf16[2,2,90,128]{3,2,1,0:T(8,128)(2,1)S(1)}, bf16[2,2,90,128]{3,2,1,0:T(8,128)(2,1)S(1)}, u32[]{:S(2)}, u32[]{:S(2)}) collective-permute-start(bf16[2,2,90,128]{3,2,1,0:T(8,128)(2,1)S(1)} %pad_maximum_fusion.2), channel_id=1, source_target_pairs={{0,192},{64,128},{128,64},{192,0},{256,448},{320,384},{384,320},{4... | collective-permute-start | bytes 276488 | tf_op jit(solution)/shard_map/ppermute | solution.py:184
  36.8 2.4 %collective-permute-done.2 = bf16[2,2,90,128]{3,2,1,0:T(8,128)(2,1)S(1)} collective-permute-done((bf16[2,2,90,128]{3,2,1,0:T(8,128)(2,1)S(1)}, bf16[2,2,90,128]{3,2,1,0:T(8,128)(2,1)S(1)}, u32[]{:S(2)}, u32[]{:S(2)}) %collective-permute-start.2) | collective-permute-done | bytes 92192 | tf_op jit(solution)/shard_map/ppermute | solution.py:184
  39.2 0.8 fusion.36
  40.1 3.2 %collective-permute-start.5 = (bf16[2,90,128]{2,1,0:T(8,128)(2,1)S(1)}, bf16[2,90,128]{2,1,0:T(8,128)(2,1)S(1)}, u32[]{:S(2)}, u32[]{:S(2)}) collective-permute-start(bf16[2,90,128]{2,1,0:T(8,128)(2,1)S(1)} %get-tuple-element.11), channel_id=1, source_target_pairs={{0,16},{16,32},{32,48},{48,0},{1,17},{17,33},{33,49},{49,1},{2,18}... | collective-permute-start | bytes 138248 | tf_op jit(solution)/shard_map/ppermute | solution.py:194
  43.3 4.5 %collective-permute-start.4 = (bf16[2,90,128]{2,1,0:T(8,128)(2,1)S(1)}, bf16[2,90,128]{2,1,0:T(8,128)(2,1)S(1)}, u32[]{:S(2)}, u32[]{:S(2)}) collective-permute-start(bf16[2,90,128]{2,1,0:T(8,128)(2,1)S(1)} %get-tuple-element.12), channel_id=1, source_target_pairs={{0,32},{16,48},{32,0},{48,16},{1,33},{17,49},{33,1},{49,17},{2,34}... | collective-permute-start | bytes 138248 | tf_op jit(solution)/shard_map/ppermute | solution.py:194
  47.8 2.9 %collective-permute-start.3 = (bf16[2,90,128]{2,1,0:T(8,128)(2,1)S(1)}, bf16[2,90,128]{2,1,0:T(8,128)(2,1)S(1)}, u32[]{:S(2)}, u32[]{:S(2)}) collective-permute-start(bf16[2,90,128]{2,1,0:T(8,128)(2,1)S(1)} %get-tuple-element.13), channel_id=1, source_target_pairs={{0,48},{16,0},{32,16},{48,32},{1,49},{17,1},{33,17},{49,33},{2,50}... | collective-permute-start | bytes 138248 | tf_op jit(solution)/shard_map/ppermute | solution.py:194
  50.7 1.0 fusion.13.table_ref
  51.7 0.0 collective-permute-done.5
  51.7 0.0 collective-permute-done.4
  51.8 0.8 collective-permute-done.3
  52.6 0.0 all-to-all-done.parts_ref
  52.6 2.7 %shard_map.69 = bf16[16,184,128]{2,1,0:T(8,128)(2,1)} custom-call(s32[1]{0:T(128)} %bitcast.x_ref, bf16[4,16,184,128]{3,2,1,0:T(8,128)(2,1)S(1)} %all-to-all-done.parts_ref, bf16[4,2,90,128]{3,2,1,0:T(8,128)(2,1)S(1)} %pad_maximum_fusion.1.grads_ref, bf16[512,128]{1,0:T(8,128)(2,1)S(1)} %fusion.13.table_ref), custom_call_target="tpu_custom_call" | custom-call | flops 385875968 | bytes 3014656 | tf_op jit(solution)/shard_map/pallas_call | solution.py:120
  55.3 14.9 %all-to-all-start.1 = ((bf16[16,184,128]{2,1,0:T(8,128)(2,1)}), bf16[16,184,128]{2,1,0:T(8,128)(2,1)S(1)}, u32[]{:S(2)}, u32[]{:S(2)}) async-start(bf16[16,184,128]{2,1,0:T(8,128)(2,1)} %shard_map.69), calls=%async_computation.1 | async-start | bytes 1507328 | tf_op jit(solution)/shard_map/all_to_all | solution.py:198
  70.2 0.0 copy-start.1
  70.3 1.5 %select_convert_fusion.1 = (bf16[1,512,128]{2,1,0:T(8,128)(2,1)S(1)}, bf16[1,512,128]{2,1,0:T(8,128)(2,1)S(1)}) fusion(s32[512]{0:T(512)S(1)} %get-tuple-element.23, s32[128]{0:T(128)S(1)} %fusion.33, s32[512]{0:T(512)S(1)} %get-tuple-element.22, pred[128]{0:T(512)(128)(4,1)S(1)} %get-tuple-element.25, pred[128]{0:T(512)(128)(4,1)S(1)} %get-tuple-element.24), kind=kLoop, calls=%fused_computation.28 | loop fusion | flops 983040 | bytes 267008 | tf_op jit(solution)/shard_map/convert.2
  71.9 0.0 copy-start.2
  71.9 0.0 copy-start.3
  71.9 12.3 %fusion.4.main_ref = bf16[512,1408]{1,0:T(8,128)(2,1)S(1)} fusion(s32[512]{0:T(512)S(1)} %get-tuple-element.23, s32[1408]{0:T(1024)S(1)} %fusion.31, s32[512]{0:T(512)S(1)} %get-tuple-element.22), kind=kLoop, calls=%fused_computation.5 | loop fusion | flops 8650752 | bytes 1451520 | tf_op jit(solution)/shard_map/convert_element_type | solution.py:38
  84.2 20.2 %all-to-all-done.1.rows_ref = bf16[16,184,128]{2,1,0:T(8,128)(2,1)S(1)} async-done(((bf16[16,184,128]{2,1,0:T(8,128)(2,1)}), bf16[16,184,128]{2,1,0:T(8,128)(2,1)S(1)}, u32[]{:S(2)}, u32[]{:S(2)}) %all-to-all-start.1) | async-done | bytes 753696 | tf_op jit(solution)/shard_map/all_to_all | solution.py:198
  104.4 1.7 %shard_map.70 = bf16[4,2,128,128]{3,2,1,0:T(8,128)(2,1)} custom-call(bf16[16,184,128]{2,1,0:T(8,128)(2,1)S(1)} %all-to-all-done.1.rows_ref, bf16[512,1408]{1,0:T(8,128)(2,1)S(1)} %fusion.4.main_ref, bf16[2,512,128]{2,1,0:T(8,128)(2,1)S(1)} %pad_maximum_fusion.tails_ref), custom_call_target="tpu_custom_call" | custom-call | flops 369098752 | bytes 2195456 | tf_op jit(solution)/shard_map/pallas_call | solution.py:156
  106.1 3.7 %all-to-all-start.2 = ((bf16[4,2,128,128]{3,2,1,0:T(8,128)(2,1)}), bf16[4,2,128,128]{3,2,1,0:T(8,128)(2,1)S(1)}, u32[]{:S(2)}, u32[]{:S(2)}) async-start(bf16[4,2,128,128]{3,2,1,0:T(8,128)(2,1)} %shard_map.70), calls=%async_computation.2 | async-start | bytes 524288 | tf_op jit(solution)/shard_map/all_to_all | solution.py:201
  109.7 0.0 copy-done
  109.7 0.2 dynamic-slice_reduce_fusion
  109.9 0.0 copy-done.1
  109.9 0.2 copy.8
  110.2 0.0 copy-done.2
  110.2 0.2 multiply_reduce_fusion
  110.4 0.7 broadcast_in_dim.48
  111.0 5.5 %all-to-all-done.2 = bf16[4,2,128,128]{3,2,1,0:T(8,128)(2,1)S(1)} async-done(((bf16[4,2,128,128]{3,2,1,0:T(8,128)(2,1)}), bf16[4,2,128,128]{3,2,1,0:T(8,128)(2,1)S(1)}, u32[]{:S(2)}, u32[]{:S(2)}) %all-to-all-start.2) | async-done | bytes 262176 | tf_op jit(solution)/shard_map/all_to_all | solution.py:201
  116.5 0.0 copy-done.3
  116.5 0.9 convert_multiply_fusion
  (18 shorter events, 0.2 us)
Async XLA Ops:
  0.6 109.1 %copy-start = (f32[8,8]{1,0:T(8,128)S(1)}, f32[8,8]{1,0:T(8,128)}, u32[]{:S(2)}) copy-start(f32[8,8]{1,0:T(8,128)} %param.8) | copy-start | bytes 772
  5.4 5.0 %copy-start.4 = (f32[1,90,128]{2,0,1:T(1,128)S(1)}, f32[1,90,128]{2,0,1:T(1,128)}, u32[]{:S(2)}) copy-start(f32[1,90,128]{2,0,1:T(1,128)} %param.6) | copy-start | bytes 138244
  5.4 47.2 %all-to-all-start = ((bf16[4,16,184,128]{3,2,1,0:T(8,128)(2,1)}), bf16[4,16,184,128]{3,2,1,0:T(8,128)(2,1)S(1)}, u32[]{:S(2)}, u32[]{:S(2)}) async-start(bf16[4,16,184,128]{3,2,1,0:T(8,128)(2,1)} %shard_map.68), calls=%async_computation | async-start | bytes 6029312 | tf_op jit(solution)/shard_map/all_to_all | solution.py:176
  10.4 16.8 %collective-permute-start = (bf16[90,128]{1,0:T(8,128)(2,1)S(1)}, bf16[90,128]{1,0:T(8,128)(2,1)S(1)}, u32[]{:S(2)}, u32[]{:S(2)}) collective-permute-start(bf16[90,128]{1,0:T(8,128)(2,1)S(1)} %bitcast.39), channel_id=1, source_target_pairs={{0,256},{64,320},{128,384},{192,448},{256,0},{320,64},{384,128},{4... | collective-permute-start | bytes 69128 | tf_op jit(solution)/shard_map/ppermute | solution.py:180
  27.2 5.1 %collective-permute-start.1 = (bf16[2,90,128]{2,1,0:T(8,128)(2,1)S(1)}, bf16[2,90,128]{2,1,0:T(8,128)(2,1)S(1)}, u32[]{:S(2)}, u32[]{:S(2)}) collective-permute-start(bf16[2,90,128]{2,1,0:T(8,128)(2,1)S(1)} %pad_maximum_fusion.3), channel_id=1, source_target_pairs={{0,64},{64,0},{128,192},{192,128},{256,320},{320,256},{384,448},{4... | collective-permute-start | bytes 138248 | tf_op jit(solution)/shard_map/ppermute | solution.py:182
  32.4 6.9 %collective-permute-start.2 = (bf16[2,2,90,128]{3,2,1,0:T(8,128)(2,1)S(1)}, bf16[2,2,90,128]{3,2,1,0:T(8,128)(2,1)S(1)}, u32[]{:S(2)}, u32[]{:S(2)}) collective-permute-start(bf16[2,2,90,128]{3,2,1,0:T(8,128)(2,1)S(1)} %pad_maximum_fusion.2), channel_id=1, source_target_pairs={{0,192},{64,128},{128,64},{192,0},{256,448},{320,384},{384,320},{4... | collective-permute-start | bytes 276488 | tf_op jit(solution)/shard_map/ppermute | solution.py:184
  40.1 11.7 %collective-permute-start.5 = (bf16[2,90,128]{2,1,0:T(8,128)(2,1)S(1)}, bf16[2,90,128]{2,1,0:T(8,128)(2,1)S(1)}, u32[]{:S(2)}, u32[]{:S(2)}) collective-permute-start(bf16[2,90,128]{2,1,0:T(8,128)(2,1)S(1)} %get-tuple-element.11), channel_id=1, source_target_pairs={{0,16},{16,32},{32,48},{48,0},{1,17},{17,33},{33,49},{49,1},{2,18}... | collective-permute-start | bytes 138248 | tf_op jit(solution)/shard_map/ppermute | solution.py:194
  43.3 8.5 %collective-permute-start.4 = (bf16[2,90,128]{2,1,0:T(8,128)(2,1)S(1)}, bf16[2,90,128]{2,1,0:T(8,128)(2,1)S(1)}, u32[]{:S(2)}, u32[]{:S(2)}) collective-permute-start(bf16[2,90,128]{2,1,0:T(8,128)(2,1)S(1)} %get-tuple-element.12), channel_id=1, source_target_pairs={{0,32},{16,48},{32,0},{48,16},{1,33},{17,49},{33,1},{49,17},{2,34}... | collective-permute-start | bytes 138248 | tf_op jit(solution)/shard_map/ppermute | solution.py:194
  47.8 4.8 %collective-permute-start.3 = (bf16[2,90,128]{2,1,0:T(8,128)(2,1)S(1)}, bf16[2,90,128]{2,1,0:T(8,128)(2,1)S(1)}, u32[]{:S(2)}, u32[]{:S(2)}) collective-permute-start(bf16[2,90,128]{2,1,0:T(8,128)(2,1)S(1)} %get-tuple-element.13), channel_id=1, source_target_pairs={{0,48},{16,0},{32,16},{48,32},{1,49},{17,1},{33,17},{49,33},{2,50}... | collective-permute-start | bytes 138248 | tf_op jit(solution)/shard_map/ppermute | solution.py:194
  55.3 49.0 %all-to-all-start.1 = ((bf16[16,184,128]{2,1,0:T(8,128)(2,1)}), bf16[16,184,128]{2,1,0:T(8,128)(2,1)S(1)}, u32[]{:S(2)}, u32[]{:S(2)}) async-start(bf16[16,184,128]{2,1,0:T(8,128)(2,1)} %shard_map.69), calls=%async_computation.1 | async-start | bytes 1507328 | tf_op jit(solution)/shard_map/all_to_all | solution.py:198
  70.2 39.7 %copy-start.1 = (f32[2,4,90,128]{3,2,0,1:T(8,128)S(1)}, f32[2,4,90,128]{3,2,0,1:T(8,128)}, u32[]{:S(2)}) copy-start(f32[2,4,90,128]{3,2,0,1:T(8,128)} %get-tuple-element.8) | copy-start | bytes 1105924
  71.9 38.3 %copy-start.2 = (f32[8,90,128]{2,0,1:T(8,128)S(1)}, f32[8,90,128]{2,0,1:T(8,128)}, u32[]{:S(2)}) copy-start(f32[8,90,128]{2,0,1:T(8,128)} %param.7) | copy-start | bytes 1105924
  71.9 44.6 %copy-start.3 = (f32[128,128]{1,0:T(8,128)S(1)}, f32[128,128]{1,0:T(8,128)}, u32[]{:S(2)}) copy-start(f32[128,128]{1,0:T(8,128)} %param.9) | copy-start | bytes 196612
  106.1 10.5 %all-to-all-start.2 = ((bf16[4,2,128,128]{3,2,1,0:T(8,128)(2,1)}), bf16[4,2,128,128]{3,2,1,0:T(8,128)(2,1)S(1)}, u32[]{:S(2)}, u32[]{:S(2)}) async-start(bf16[4,2,128,128]{3,2,1,0:T(8,128)(2,1)} %shard_map.70), calls=%async_computation.2 | async-start | bytes 524288 | tf_op jit(solution)/shard_map/all_to_all | solution.py:201

commit v5 on v3

--- a/solution.py
+++ b/solution.py
@@ -53,6 +53,18 @@
     return [(i, i ^ flip) for i in range(size)]
 
 
+def to_columns(turn):
+    places = [(half, y, x) for half in range(2) for y in range(4) for x in range(4)]
+    return [(half * 16 + y * 4 + x, half * 16 + (x + turn) % 4 * 4 + y) for half, y, x in places]
+
+
+def gather_y(mine, y):
+    rings = [[(i, i // 4 * 4 + (i - step) % 4) for i in range(8)] for step in (1, 2, 3)]
+    ahead = [lax.ppermute(mine, "mem", pairs) for pairs in rings]
+    turned = jnp.stack([mine, *ahead, mine, *ahead[:2]])
+    return lax.dynamic_slice_in_dim(turned, (4 - y) % 4, 4, 0)
+
+
 def pack_rows(fields, rows):
     lon = fields[0].shape[0]
     whole = lon // TILE * TILE
@@ -67,7 +79,7 @@
     for m in range(count):
         wide[m % 2] = members_ref[m].astype(jnp.float32).reshape(lon * levels, lat)
         for part in range(levels // PAIR):
-            firsts = [part * PAIR + place for place in range(PAIR)]
+            firsts = [part + place * (levels // PAIR) for place in range(PAIR)]
             pieces = [wide[m % 2, pl.ds(first, whole, stride=levels), :] for first in firsts]
             lasts = [
                 wide[m % 2, pl.ds(first + n * levels, 1), :] for first in firsts for n in range(whole, lon)
@@ -91,14 +103,16 @@
     )(members)
 
 
-def lat_sums_kernel(x_ref, parts_ref, grads_ref, table_ref, out_ref, packed):
+def lat_sums_kernel(first_ref, parts_ref, grads_ref, table_ref, out_ref, packed):
     bands, count, rows, _ = parts_ref.shape
-    x = x_ref[0]
+    first = first_ref[0]
 
     @pl.when(pl.program_id(0) == 0)
     def _():
         for part in range(bands):
-            packed[part] = pack_rows([grads_ref[(part + 4 - x) % 4, place] for place in range(PAIR)], rows)
+            packed[part] = pack_rows(
+                [grads_ref[(first + 4 - part) % 4, place].astype(jnp.float32) for place in range(PAIR)], rows
+            )
 
     for m in range(count):
         product = [
@@ -111,7 +125,7 @@
         out_ref[m] = sums.astype(jnp.bfloat16)
 
 
-def lat_sums(x, parts, grads, table):
+def lat_sums(first, parts, grads, table):
     bands, count, rows, lat = parts.shape
     waves = table.shape[1]
     step = min(4, count)
@@ -131,7 +145,7 @@
         cost_estimate=pl.CostEstimate(
             flops=2 * parts.size * waves, bytes_accessed=2 * parts.size, transcendentals=0
         ),
-    )(jnp.reshape(x, (1,)).astype(jnp.int32), parts, grads, table)
+    )(jnp.reshape(first, (1,)).astype(jnp.int32), parts, grads, table)
 
 
 def zonal_kernel(rows_ref, main_ref, tails_ref, out_ref):
@@ -163,11 +177,28 @@
     )(rows, main, tails)
 
 
+def weighted_kernel(values_ref, weights_ref, out_ref):
+    bands = values_ref.shape[0]
+    for place in range(PAIR):
+        for part in range(bands):
+            out_ref[place * bands + part] = values_ref[part, place].astype(jnp.float32) * weights_ref[...]
+
+
+def weighted(values, weights):
+    bands, _, waves, k_lat = values.shape
+    return pl.pallas_call(
+        weighted_kernel,
+        out_shape=jax.ShapeDtypeStruct((bands * PAIR, waves, k_lat), jnp.float32),
+        in_specs=[pl.BlockSpec(memory_space=pltpu.VMEM)] * 2,
+        out_specs=pl.BlockSpec(memory_space=pltpu.VMEM),
+        cost_estimate=pl.CostEstimate(flops=values.size, bytes_accessed=6 * values.size, transcendentals=0),
+    )(values, weights)
+
+
 def local(members, grad_field, static_std, vert_mix, loc_weights):
     mem_local, levels, lon_local, lat_local = members.shape
     mem = lax.axis_index("mem")
     half_z, y = mem // 4, mem % 4
-    x = lax.axis_index("lat")
     rows = -(-PAIR * lon_local // TILE) * TILE
 
     sent = spread(members.transpose(0, 2, 1, 3), rows)
@@ -177,28 +208,17 @@
     own_grad = grad_field[0]
     far_grad = lax.ppermute(own_grad, "mem", partners(8, 4))
     mine = jnp.stack([jnp.where(half_z == 0, own_grad, far_grad), jnp.where(half_z == 0, far_grad, own_grad)])
-    beside = lax.ppermute(mine, "mem", partners(8, 1))
-    two = jnp.stack([jnp.where(y % 2 == 0, mine, beside), jnp.where(y % 2 == 0, beside, mine)])
-    others = lax.ppermute(two, "mem", partners(8, 3))
-    grads = jnp.concatenate([jnp.where(y < 2, two, others), jnp.where(y < 2, others, two)])
-    grads = grads.transpose(1, 0, 2, 3).reshape(levels, lon_local, lat_local)
-    pairs = grads.reshape(4, PAIR, lon_local, lat_local)
-
-    def pair(step):
-        return lax.dynamic_index_in_dim(pairs, (x + step) % 4, 0, keepdims=False)
-
-    met = jnp.stack(
-        [pair(0)]
-        + [lax.ppermute(pair(4 - d), "lat", [(i, (i - d) % 4) for i in range(4)]) for d in (1, 2, 3)]
-    )
-    sums = lat_sums(x, parts, met, lat_table)
+    met = jnp.stack([lax.ppermute(mine.astype(jnp.bfloat16), ("mem", "lat"), to_columns(j)) for j in range(4)])
+    sums = lat_sums(y, parts, met, lat_table)
 
     whole = lax.all_to_all(sums, "lon", split_axis=0, concat_axis=0, tiled=True)
     waves = after(jnp.arange(KLON, dtype=jnp.int32), sums)
-    zonal = zonal_sums(whole, *lon_tables_make(NLON, mem_local, waves))
+    main, tails = lon_tables_make(NLON, mem_local, waves)
+    zonal = zonal_sums(whole, main, tails)
     alpha = lax.all_to_all(zonal, "lat", split_axis=0, concat_axis=0, tiled=True)
-    alpha_grad = alpha.reshape(levels, KLON // 4, KLAT).astype(jnp.float32) * loc_weights[None]
-
+    alpha_grad = weighted(alpha, loc_weights)
+
+    grads = gather_y(after(mine, main), y).transpose(1, 0, 2, 3).reshape(levels, lon_local, lat_local)
     mix = after(lax.dynamic_index_in_dim(vert_mix, mem, 1, keepdims=False), sums)
     static_grad = jnp.sum(mix[:, None, None] * (static_std * grads), axis=0)
     return (alpha_grad, static_grad[None])

time: 120 us -> 123 us (1.025)
  waiting for transfers between devices: 34.3 us -> 28.7 us
  starting transfers between devices: 57.3 us -> 62.3 us
  Pallas kernels: 9.11 us -> 10.9 us
  local copies, waits for them, and re-layouts: 1.19 us -> 2.53 us
    all_to_all x1, waiting for transfers between devices: 20.2 us -> 7.51 us  [local(): whole = lax.all_to_all(sums, 'lon', split_axis=0, concat_axis=0, tiled=True)]
    ppermute x5 -> x7, waiting for transfers between devices: 7.01 us -> 15 us  [the longest x4 12.9 us: local(): lax.ppermute(mine.astype(jnp.bfloat16), ('mem', 'lat'), to_columns(j))]
    ppermute x5 -> x7, starting transfers between devices: 18.4 us -> 23.1 us  [the longest x4 12.9 us: local(): lax.ppermute(mine.astype(jnp.bfloat16), ('mem', 'lat'), to_columns(j))]
    pallas_call x0 -> x1, Pallas kernels: none -> 1.78 us  [weighted(): pl.pallas_call(weighted_kernel, out_shape=jax.ShapeDtypeStruct((bands * P...]
    unnamed x13 -> x19, local copies, waits for them, and re-layouts: 0.04 us -> 1.41 us
    all_to_all x1, starting transfers between devices: 3.66 us -> 5.02 us  [local(): lax.all_to_all(zonal, 'lat', split_axis=0, concat_axis=0, tiled=True)]
  transfers between devices with their start and end apart: 9 -> 11, of which waited for: 6 -> 6; matrix products, arithmetic and copies ran while one was open for 14% -> 15% of each run, Pallas kernels for 0% -> 0%
where the time goes in v5:
time: 123 us; the launch traced here: 122 us
  starting transfers between devices  62.3 us (51%)
  waiting for transfers between devices  28.7 us (23%)
  other arithmetic  16.5 us (13%)
  Pallas kernels  10.9 us (9%)
  local copies, waits for them, and re-layouts  2.53 us (2%)
    ppermute x1, starting transfers between devices, local(): far_grad = lax.ppermute(own_grad, 'mem', partners(8, 4))  15.4 us
    all_to_all x1, starting transfers between devices, local(): whole = lax.all_to_all(sums, 'lon', split_axis=0, concat_axis=0, tiled=True)  13.8 us
    ppermute x4, starting transfers between devices, local(): lax.ppermute(mine.astype(jnp.bfloat16), ('mem', 'lat'), to_columns(j))  12.9 us
    ppermute x4, waiting for transfers between devices, local(): lax.ppermute(mine.astype(jnp.bfloat16), ('mem', 'lat'), to_columns(j))  12.9 us
    convert_element_type x1, other arithmetic, lon_tables_make(): return (main.astype(jnp.bfloat16), jnp.stack(tails).astype(jnp.bfloat16))  12.3 us
    ppermute x3, starting transfers between devices, gather_y(): ahead = [lax.ppermute(mine, 'mem', pairs) for pairs in rings]  10.2 us
    all_to_all x1, waiting for transfers between devices, local(): whole = lax.all_to_all(sums, 'lon', split_axis=0, concat_axis=0, tiled=True)  7.51 us
    all_to_all x1, waiting for transfers between devices, local(): lax.all_to_all(zonal, 'lat', split_axis=0, concat_axis=0, tiled=True)  5.67 us
  transfers between devices with their start and end apart: 11, of which 6 were waited for; matrix products, arithmetic and copies ran while one was open for 15% of the time, Pallas kernels for 0%

profile of v5, /device:TPU:1, one launch (start us, length us, event | category | flops | bytes accessed | tf_op | source)
XLA Modules:
  0.0 122.0 jit_solution(15848717619618611169)
XLA Ops:
  0.6 0.0 copy-start
  0.6 4.7 %shard_map.68 = bf16[4,16,184,128]{3,2,1,0:T(8,128)(2,1)} custom-call(bf16[16,90,8,128]{3,2,1,0:T(8,128)(2,1)} %bitcast.31), custom_call_target="tpu_custom_call" | custom-call | flops 1474560 | bytes 5898240 | tf_op jit(solution)/shard_map/pallas_call | solution.py:94
  5.4 0.0 copy-start.3
  5.4 5.0 %all-to-all-start = ((bf16[4,16,184,128]{3,2,1,0:T(8,128)(2,1)}), bf16[4,16,184,128]{3,2,1,0:T(8,128)(2,1)S(1)}, u32[]{:S(2)}, u32[]{:S(2)}) async-start(bf16[4,16,184,128]{3,2,1,0:T(8,128)(2,1)} %shard_map.68), calls=%async_computation | async-start | bytes 6029312 | tf_op jit(solution)/shard_map/all_to_all | solution.py:205
  10.3 0.0 copy-done.3
  10.4 15.4 %collective-permute-start = (f32[90,128]{1,0:T(8,128)S(1)}, f32[90,128]{1,0:T(8,128)S(1)}, u32[]{:S(2)}, u32[]{:S(2)}) collective-permute-start(f32[90,128]{1,0:T(8,128)S(1)} %bitcast.36), channel_id=1, source_target_pairs={{0,256},{64,320},{128,384},{192,448},{256,0},{320,64},{384,128},{4... | collective-permute-start | bytes 138248 | tf_op jit(solution)/shard_map/ppermute | solution.py:209
  25.8 1.0 fusion.13.table_ref
  26.9 0.5 collective-permute-done
  27.4 4.6 %collective-permute-start.4 = (bf16[2,90,128]{2,1,0:T(8,128)(2,1)S(1)}, bf16[2,90,128]{2,1,0:T(8,128)(2,1)S(1)}, u32[]{:S(2)}, u32[]{:S(2)}) collective-permute-start(bf16[2,90,128]{2,1,0:T(8,128)(2,1)S(1)} %fusion.36), channel_id=1, source_target_pairs={{0,192},{16,0},{32,64},{48,128},{64,208},{80,16},{96,80},{112,144}... | collective-permute-start | bytes 138248 | tf_op jit(solution)/shard_map/ppermute | solution.py:211
  32.1 5.7 %collective-permute-start.3 = (bf16[2,90,128]{2,1,0:T(8,128)(2,1)S(1)}, bf16[2,90,128]{2,1,0:T(8,128)(2,1)S(1)}, u32[]{:S(2)}, u32[]{:S(2)}) collective-permute-start(bf16[2,90,128]{2,1,0:T(8,128)(2,1)S(1)} %fusion.36), channel_id=1, source_target_pairs={{0,128},{16,192},{32,0},{48,64},{64,144},{80,208},{96,16},{112,80}... | collective-permute-start | bytes 138248 | tf_op jit(solution)/shard_map/ppermute | solution.py:211
  37.8 1.9 %collective-permute-start.2 = (bf16[2,90,128]{2,1,0:T(8,128)(2,1)S(1)}, bf16[2,90,128]{2,1,0:T(8,128)(2,1)}, u32[]{:S(2)}, u32[]{:S(2)}) collective-permute-start(bf16[2,90,128]{2,1,0:T(8,128)(2,1)S(1)} %fusion.36), channel_id=1, source_target_pairs={{0,64},{16,128},{32,192},{48,0},{64,80},{80,144},{96,208},{112,16}... | collective-permute-start | bytes 138248 | tf_op jit(solution)/shard_map/ppermute | solution.py:211
  39.7 0.7 collective-permute-start.1
  40.4 0.5 broadcast_compare_fusion
  40.9 0.0 collective-permute-done.4
  40.9 2.1 %collective-permute-done.3 = bf16[2,90,128]{2,1,0:T(8,128)(2,1)S(1)} collective-permute-done((bf16[2,90,128]{2,1,0:T(8,128)(2,1)S(1)}, bf16[2,90,128]{2,1,0:T(8,128)(2,1)S(1)}, u32[]{:S(2)}, u32[]{:S(2)}) %collective-permute-start.3) | collective-permute-done | bytes 46112 | tf_op jit(solution)/shard_map/ppermute | solution.py:211
  43.0 10.8 %collective-permute-done.2 = bf16[2,90,128]{2,1,0:T(8,128)(2,1)} collective-permute-done((bf16[2,90,128]{2,1,0:T(8,128)(2,1)S(1)}, bf16[2,90,128]{2,1,0:T(8,128)(2,1)}, u32[]{:S(2)}, u32[]{:S(2)}) %collective-permute-start.2) | collective-permute-done | bytes 46112 | tf_op jit(solution)/shard_map/ppermute | solution.py:211
  53.8 0.0 collective-permute-done.1
  53.8 0.0 copy-start.4
  53.8 0.6 copy-done.4
  54.4 0.8 pad_maximum_fusion.1.grads_ref
  55.3 0.0 all-to-all-done.parts_ref
  55.3 0.0 copy-start.5
  55.3 2.7 %shard_map.69 = bf16[16,184,128]{2,1,0:T(8,128)(2,1)} custom-call(s32[1]{0:T(128)} %bitcast.first_ref, bf16[4,16,184,128]{3,2,1,0:T(8,128)(2,1)S(1)} %all-to-all-done.parts_ref, bf16[4,2,90,128]{3,2,1,0:T(8,128)(2,1)S(1)} %pad_maximum_fusion.1.grads_ref, bf16[512,128]{1,0:T(8,128)(2,1)S(1)} %fusion.13.table_ref), custom_call_target="tpu_custom_call" | custom-call | flops 385875968 | bytes 3014656 | tf_op jit(solution)/shard_map/pallas_call | solution.py:132
  58.0 13.8 %all-to-all-start.1 = ((bf16[16,184,128]{2,1,0:T(8,128)(2,1)}), bf16[16,184,128]{2,1,0:T(8,128)(2,1)S(1)}, u32[]{:S(2)}, u32[]{:S(2)}) async-start(bf16[16,184,128]{2,1,0:T(8,128)(2,1)} %shard_map.69), calls=%async_computation.1 | async-start | bytes 1507328 | tf_op jit(solution)/shard_map/all_to_all | solution.py:214
  71.8 0.0 copy-done
  71.8 0.2 dynamic-slice_reduce_fusion
  72.1 12.3 %fusion.4.main_ref = bf16[512,1408]{1,0:T(8,128)(2,1)S(1)} fusion(s32[512]{0:T(512)S(1)} %get-tuple-element.15, s32[1408]{0:T(1024)S(1)} %fusion.31, s32[512]{0:T(512)S(1)} %get-tuple-element.14), kind=kLoop, calls=%fused_computation.5 | loop fusion | flops 8650752 | bytes 1451520 | tf_op jit(solution)/shard_map/convert_element_type | solution.py:38
  84.4 2.0 %collective-permute-start.7 = (f32[2,90,128]{2,1,0:T(8,128)S(1)}, f32[2,90,128]{2,1,0:T(8,128)S(1)}, u32[]{:S(2)}, u32[]{:S(2)}) collective-permute-start(f32[2,90,128]{2,1,0:T(8,128)S(1)} %pad_maximum_fusion.2), channel_id=1, source_target_pairs={{0,64},{64,128},{128,192},{192,0},{256,320},{320,384},{384,448},{4... | collective-permute-start | bytes 276488 | tf_op jit(solution)/shard_map/ppermute | solution.py:63
  86.3 6.3 %collective-permute-start.6 = (f32[2,90,128]{2,1,0:T(8,128)S(1)}, f32[2,90,128]{2,1,0:T(8,128)S(1)}, u32[]{:S(2)}, u32[]{:S(2)}) collective-permute-start(f32[2,90,128]{2,1,0:T(8,128)S(1)} %pad_maximum_fusion.2), channel_id=1, source_target_pairs={{0,128},{64,192},{128,0},{192,64},{256,384},{320,448},{384,256},{4... | collective-permute-start | bytes 276488 | tf_op jit(solution)/shard_map/ppermute | solution.py:63
  92.7 1.9 %collective-permute-start.5 = (f32[2,90,128]{2,1,0:T(8,128)S(1)}, f32[2,90,128]{2,1,0:T(8,128)S(1)}, u32[]{:S(2)}, u32[]{:S(2)}) collective-permute-start(f32[2,90,128]{2,1,0:T(8,128)S(1)} %pad_maximum_fusion.2), channel_id=1, source_target_pairs={{0,192},{64,0},{128,64},{192,128},{256,448},{320,256},{384,320},{4... | collective-permute-start | bytes 276488 | tf_op jit(solution)/shard_map/ppermute | solution.py:63
  94.6 0.0 copy-done.5
  94.6 1.5 %select_convert_fusion.1 = (bf16[1,512,128]{2,1,0:T(8,128)(2,1)S(1)}, bf16[1,512,128]{2,1,0:T(8,128)(2,1)S(1)}) fusion(s32[512]{0:T(512)S(1)} %get-tuple-element.15, s32[128]{0:T(128)S(1)} %fusion.33, s32[512]{0:T(512)S(1)} %get-tuple-element.14, pred[128]{0:T(512)(128)(4,1)S(1)} %copy-done.5, pred[128]{0:T(512)(128)(4,1)S(1)} %get-tuple-element.16), kind=kLoop, calls=%fused_computation.28 | loop fusion | flops 983040 | bytes 267008 | tf_op jit(solution)/shard_map/convert
  96.2 2.1 %collective-permute-done.5 = f32[2,90,128]{2,1,0:T(8,128)S(1)} collective-permute-done((f32[2,90,128]{2,1,0:T(8,128)S(1)}, f32[2,90,128]{2,1,0:T(8,128)S(1)}, u32[]{:S(2)}, u32[]{:S(2)}) %collective-permute-start.5) | collective-permute-done | bytes 92192 | tf_op jit(solution)/shard_map/ppermute | solution.py:63
  98.3 0.0 copy-start.2
  98.3 0.0 collective-permute-done.6
  98.4 0.0 collective-permute-done.7
  98.4 7.5 %all-to-all-done.1.rows_ref = bf16[16,184,128]{2,1,0:T(8,128)(2,1)S(1)} async-done(((bf16[16,184,128]{2,1,0:T(8,128)(2,1)}), bf16[16,184,128]{2,1,0:T(8,128)(2,1)S(1)}, u32[]{:S(2)}, u32[]{:S(2)}) %all-to-all-start.1) | async-done | bytes 753696 | tf_op jit(solution)/shard_map/all_to_all | solution.py:214
  106.0 1.7 %shard_map.70 = bf16[4,2,128,128]{3,2,1,0:T(8,128)(2,1)} custom-call(bf16[16,184,128]{2,1,0:T(8,128)(2,1)S(1)} %all-to-all-done.1.rows_ref, bf16[512,1408]{1,0:T(8,128)(2,1)S(1)} %fusion.4.main_ref, bf16[2,512,128]{2,1,0:T(8,128)(2,1)S(1)} %pad_maximum_fusion.tails_ref), custom_call_target="tpu_custom_call" | custom-call | flops 369098752 | bytes 2195456 | tf_op jit(solution)/shard_map/pallas_call | solution.py:168
  107.6 5.0 %all-to-all-start.2 = ((bf16[4,2,128,128]{3,2,1,0:T(8,128)(2,1)}), bf16[4,2,128,128]{3,2,1,0:T(8,128)(2,1)S(1)}, u32[]{:S(2)}, u32[]{:S(2)}) async-start(bf16[4,2,128,128]{3,2,1,0:T(8,128)(2,1)} %shard_map.70), calls=%async_computation.2 | async-start | bytes 524288 | tf_op jit(solution)/shard_map/all_to_all | solution.py:218
  112.7 0.2 copy.7
  112.9 0.0 copy-done.2
  112.9 0.2 multiply_reduce_fusion
  113.2 0.7 broadcast_in_dim.47
  113.8 5.7 %all-to-all-done.2.values_ref = bf16[4,2,128,128]{3,2,1,0:T(8,128)(2,1)S(1)} async-done(((bf16[4,2,128,128]{3,2,1,0:T(8,128)(2,1)}), bf16[4,2,128,128]{3,2,1,0:T(8,128)(2,1)S(1)}, u32[]{:S(2)}, u32[]{:S(2)}) %all-to-all-start.2) | async-done | bytes 262176 | tf_op jit(solution)/shard_map/all_to_all | solution.py:218
  119.5 0.0 copy-start.1
  119.5 0.7 copy-done.1
  120.2 1.8 %shard_map.71 = f32[8,128,128]{2,1,0:T(8,128)} custom-call(bf16[4,2,128,128]{3,2,1,0:T(8,128)(2,1)} %copy-done.1, f32[128,128]{1,0:T(8,128)} %weights_ref.1), custom_call_target="tpu_custom_call" | custom-call | flops 131072 | bytes 786432 | tf_op jit(solution)/shard_map/pallas_call | solution.py:189
  (19 shorter events, 0.2 us)
Async XLA Ops:
  0.6 71.2 %copy-start = (f32[8,8]{1,0:T(8,128)S(1)}, f32[8,8]{1,0:T(8,128)}, u32[]{:S(2)}) copy-start(f32[8,8]{1,0:T(8,128)} %param.8) | copy-start | bytes 772
  5.4 5.0 %copy-start.3 = (f32[1,90,128]{2,0,1:T(1,128)S(1)}, f32[1,90,128]{2,0,1:T(1,128)}, u32[]{:S(2)}) copy-start(f32[1,90,128]{2,0,1:T(1,128)} %param.6) | copy-start | bytes 138244
  5.4 49.9 %all-to-all-start = ((bf16[4,16,184,128]{3,2,1,0:T(8,128)(2,1)}), bf16[4,16,184,128]{3,2,1,0:T(8,128)(2,1)S(1)}, u32[]{:S(2)}, u32[]{:S(2)}) async-start(bf16[4,16,184,128]{3,2,1,0:T(8,128)(2,1)} %shard_map.68), calls=%async_computation | async-start | bytes 6029312 | tf_op jit(solution)/shard_map/all_to_all | solution.py:205
  10.4 17.0 %collective-permute-start = (f32[90,128]{1,0:T(8,128)S(1)}, f32[90,128]{1,0:T(8,128)S(1)}, u32[]{:S(2)}, u32[]{:S(2)}) collective-permute-start(f32[90,128]{1,0:T(8,128)S(1)} %bitcast.36), channel_id=1, source_target_pairs={{0,256},{64,320},{128,384},{192,448},{256,0},{320,64},{384,128},{4... | collective-permute-start | bytes 138248 | tf_op jit(solution)/shard_map/ppermute | solution.py:209
  27.4 13.5 %collective-permute-start.4 = (bf16[2,90,128]{2,1,0:T(8,128)(2,1)S(1)}, bf16[2,90,128]{2,1,0:T(8,128)(2,1)S(1)}, u32[]{:S(2)}, u32[]{:S(2)}) collective-permute-start(bf16[2,90,128]{2,1,0:T(8,128)(2,1)S(1)} %fusion.36), channel_id=1, source_target_pairs={{0,192},{16,0},{32,64},{48,128},{64,208},{80,16},{96,80},{112,144}... | collective-permute-start | bytes 138248 | tf_op jit(solution)/shard_map/ppermute | solution.py:211
  32.1 10.9 %collective-permute-start.3 = (bf16[2,90,128]{2,1,0:T(8,128)(2,1)S(1)}, bf16[2,90,128]{2,1,0:T(8,128)(2,1)S(1)}, u32[]{:S(2)}, u32[]{:S(2)}) collective-permute-start(bf16[2,90,128]{2,1,0:T(8,128)(2,1)S(1)} %fusion.36), channel_id=1, source_target_pairs={{0,128},{16,192},{32,0},{48,64},{64,144},{80,208},{96,16},{112,80}... | collective-permute-start | bytes 138248 | tf_op jit(solution)/shard_map/ppermute | solution.py:211
  37.8 16.0 %collective-permute-start.2 = (bf16[2,90,128]{2,1,0:T(8,128)(2,1)S(1)}, bf16[2,90,128]{2,1,0:T(8,128)(2,1)}, u32[]{:S(2)}, u32[]{:S(2)}) collective-permute-start(bf16[2,90,128]{2,1,0:T(8,128)(2,1)S(1)} %fusion.36), channel_id=1, source_target_pairs={{0,64},{16,128},{32,192},{48,0},{64,80},{80,144},{96,208},{112,16}... | collective-permute-start | bytes 138248 | tf_op jit(solution)/shard_map/ppermute | solution.py:211
  39.7 14.1 %collective-permute-start.1 = (bf16[2,90,128]{2,1,0:T(8,128)(2,1)S(1)}, bf16[2,90,128]{2,1,0:T(8,128)(2,1)S(1)}, u32[]{:S(2)}, u32[]{:S(2)}) collective-permute-start(bf16[2,90,128]{2,1,0:T(8,128)(2,1)S(1)} %fusion.36), channel_id=1, source_target_pairs={{0,0},{16,64},{32,128},{48,192},{64,16},{80,80},{96,144},{112,208}... | collective-permute-start | bytes 138248 | tf_op jit(solution)/shard_map/ppermute | solution.py:211
  53.8 0.6 copy-start.4
  55.3 39.3 %copy-start.5 = (pred[128]{0:T(512)(128)(4,1)S(1)}, pred[128]{0:T(512)(128)(4,1)}, u32[]{:S(2)}) copy-start(pred[128]{0:T(512)(128)(4,1)} %get-tuple-element.17) | copy-start | bytes 388
  58.0 47.9 %all-to-all-start.1 = ((bf16[16,184,128]{2,1,0:T(8,128)(2,1)}), bf16[16,184,128]{2,1,0:T(8,128)(2,1)S(1)}, u32[]{:S(2)}, u32[]{:S(2)}) async-start(bf16[16,184,128]{2,1,0:T(8,128)(2,1)} %shard_map.69), calls=%async_computation.1 | async-start | bytes 1507328 | tf_op jit(solution)/shard_map/all_to_all | solution.py:214
  84.4 14.0 %collective-permute-start.7 = (f32[2,90,128]{2,1,0:T(8,128)S(1)}, f32[2,90,128]{2,1,0:T(8,128)S(1)}, u32[]{:S(2)}, u32[]{:S(2)}) collective-permute-start(f32[2,90,128]{2,1,0:T(8,128)S(1)} %pad_maximum_fusion.2), channel_id=1, source_target_pairs={{0,64},{64,128},{128,192},{192,0},{256,320},{320,384},{384,448},{4... | collective-permute-start | bytes 276488 | tf_op jit(solution)/shard_map/ppermute | solution.py:63
  86.3 12.0 %collective-permute-start.6 = (f32[2,90,128]{2,1,0:T(8,128)S(1)}, f32[2,90,128]{2,1,0:T(8,128)S(1)}, u32[]{:S(2)}, u32[]{:S(2)}) collective-permute-start(f32[2,90,128]{2,1,0:T(8,128)S(1)} %pad_maximum_fusion.2), channel_id=1, source_target_pairs={{0,128},{64,192},{128,0},{192,64},{256,384},{320,448},{384,256},{4... | collective-permute-start | bytes 276488 | tf_op jit(solution)/shard_map/ppermute | solution.py:63
  92.7 5.7 %collective-permute-start.5 = (f32[2,90,128]{2,1,0:T(8,128)S(1)}, f32[2,90,128]{2,1,0:T(8,128)S(1)}, u32[]{:S(2)}, u32[]{:S(2)}) collective-permute-start(f32[2,90,128]{2,1,0:T(8,128)S(1)} %pad_maximum_fusion.2), channel_id=1, source_target_pairs={{0,192},{64,0},{128,64},{192,128},{256,448},{320,256},{384,320},{4... | collective-permute-start | bytes 276488 | tf_op jit(solution)/shard_map/ppermute | solution.py:63
  98.3 14.6 %copy-start.2 = (f32[8,90,128]{2,0,1:T(8,128)S(1)}, f32[8,90,128]{2,0,1:T(8,128)}, u32[]{:S(2)}) copy-start(f32[8,90,128]{2,0,1:T(8,128)} %param.7) | copy-start | bytes 1105924
  107.6 11.8 %all-to-all-start.2 = ((bf16[4,2,128,128]{3,2,1,0:T(8,128)(2,1)}), bf16[4,2,128,128]{3,2,1,0:T(8,128)(2,1)S(1)}, u32[]{:S(2)}, u32[]{:S(2)}) async-start(bf16[4,2,128,128]{3,2,1,0:T(8,128)(2,1)} %shard_map.70), calls=%async_computation.2 | async-start | bytes 524288 | tf_op jit(solution)/shard_map/all_to_all | solution.py:218
  119.5 0.7 copy-start.1

commit v6 on v3

--- a/solution.py
+++ b/solution.py
@@ -91,42 +91,44 @@
     )(members)
 
 
-def lat_sums_kernel(x_ref, parts_ref, grads_ref, table_ref, out_ref, packed):
+def lat_sums_kernel(x_ref, parts_ref, grads_ref, table_ref, out_ref, packed, sums, done):
     bands, count, rows, _ = parts_ref.shape
     x = x_ref[0]
-
-    @pl.when(pl.program_id(0) == 0)
-    def _():
-        for part in range(bands):
-            packed[part] = pack_rows([grads_ref[(part + 4 - x) % 4, place] for place in range(PAIR)], rows)
-
+    group = count // done.shape[0]
+
+    def to_out(i):
+        span = pl.ds(i * group, group)
+        return pltpu.make_async_copy(sums.at[span], out_ref.at[span], done.at[i])
+
+    for part in range(bands):
+        packed[part] = pack_rows([grads_ref[(part + 4 - x) % 4, place] for place in range(PAIR)], rows)
     for m in range(count):
         product = [
             (parts_ref[part, m].astype(jnp.float32) * packed[part]).astype(jnp.bfloat16)
             for part in range(bands)
         ]
-        sums = jnp.dot(
+        sums[m] = jnp.dot(
             jnp.concatenate(product, axis=1), table_ref[...], preferred_element_type=jnp.float32
-        )
-        out_ref[m] = sums.astype(jnp.bfloat16)
+        ).astype(jnp.bfloat16)
+        if m % group == group - 1:
+            to_out(m // group).start()
+    for i in range(done.shape[0]):
+        to_out(i).wait()
 
 
 def lat_sums(x, parts, grads, table):
     bands, count, rows, lat = parts.shape
     waves = table.shape[1]
-    step = min(4, count)
     return pl.pallas_call(
         lat_sums_kernel,
         out_shape=pltpu.HBM((count, rows, waves), jnp.bfloat16),
-        grid=(count // step,),
-        in_specs=[
-            pl.BlockSpec(memory_space=pltpu.SMEM),
-            pl.BlockSpec((bands, step, rows, lat), lambda i: (0, i, 0, 0)),
-            pl.BlockSpec(grads.shape, lambda i: (0, 0, 0, 0)),
-            pl.BlockSpec((bands * lat, waves), lambda i: (0, 0)),
+        in_specs=[pl.BlockSpec(memory_space=pltpu.SMEM)] + [pl.BlockSpec(memory_space=pltpu.VMEM)] * 3,
+        out_specs=pl.BlockSpec(memory_space=pltpu.HBM),
+        scratch_shapes=[
+            pltpu.VMEM((bands, rows, lat), jnp.float32),
+            pltpu.VMEM((count, rows, waves), jnp.bfloat16),
+            pltpu.SemaphoreType.DMA((min(4, count),)),
         ],
-        out_specs=pl.BlockSpec((step, rows, waves), lambda i: (i, 0, 0)),
-        scratch_shapes=[pltpu.VMEM((bands, rows, lat), jnp.float32)],
         compiler_params=pltpu.CompilerParams(vmem_limit_bytes=24 * 2**20),
         cost_estimate=pl.CostEstimate(
             flops=2 * parts.size * waves, bytes_accessed=2 * parts.size, transcendentals=0

time: 120 us -> 119 us (level)
  no operation moved by 1% of the time
where the time goes in v6:
time: 119 us; the launch traced here: 118 us
  starting transfers between devices  57.3 us (48%)
  waiting for transfers between devices  34.3 us (29%)
  other arithmetic  16.1 us (14%)
  Pallas kernels  8.08 us (7%)
  local copies, waits for them, and re-layouts  1.19 us (1%)
    all_to_all x1, waiting for transfers between devices, local(): whole = lax.all_to_all(sums, 'lon', split_axis=0, concat_axis=0, tiled=True)  20.2 us
    ppermute x1, starting transfers between devices, local(): far_grad = lax.ppermute(own_grad, 'mem', partners(8, 4))  15.4 us
    all_to_all x1, starting transfers between devices, local(): whole = lax.all_to_all(sums, 'lon', split_axis=0, concat_axis=0, tiled=True)  14.9 us
    convert_element_type x1, other arithmetic, lon_tables_make(): return (main.astype(jnp.bfloat16), jnp.stack(tails).astype(jnp.bfloat16))  12.3 us
    ppermute x3, starting transfers between devices, local(): lax.ppermute(pair(4 - d), 'lat', [(i, (i - d) % 4) for i in range(4)])  10.5 us
    all_to_all x1, waiting for transfers between devices, local(): lax.all_to_all(zonal, 'lat', split_axis=0, concat_axis=0, tiled=True)  5.51 us
    all_to_all x1, starting transfers between devices, local(): parts = lax.all_to_all(sent, 'lat', split_axis=0, concat_axis=0, tiled=True)  4.97 us
    pallas_call x1, Pallas kernels, spread(): pl.pallas_call(spread_kernel, out_shape=jax.ShapeDtypeStruct((levels // P...  4.73 us
  transfers between devices with their start and end apart: 9, of which 6 were waited for; matrix products, arithmetic and copies ran while one was open for 14% of the time, Pallas kernels for 0%

profile of v6, /device:TPU:1, one launch (start us, length us, event | category | flops | bytes accessed | tf_op | source)
XLA Modules:
  0.0 118.0 jit_solution(3025393273247513030)
XLA Ops:
  0.6 0.0 copy-start
  0.6 4.7 %shard_map.68 = bf16[4,16,184,128]{3,2,1,0:T(8,128)(2,1)} custom-call(bf16[16,90,8,128]{3,2,1,0:T(8,128)(2,1)} %bitcast.33), custom_call_target="tpu_custom_call" | custom-call | flops 1474560 | bytes 5898240 | tf_op jit(solution)/shard_map/pallas_call | solution.py:82
  5.4 0.0 copy-start.4
  5.4 5.0 %all-to-all-start = ((bf16[4,16,184,128]{3,2,1,0:T(8,128)(2,1)}), bf16[4,16,184,128]{3,2,1,0:T(8,128)(2,1)S(1)}, u32[]{:S(2)}, u32[]{:S(2)}) async-start(bf16[4,16,184,128]{3,2,1,0:T(8,128)(2,1)} %shard_map.68), calls=%async_computation | async-start | bytes 6029312 | tf_op jit(solution)/shard_map/all_to_all | solution.py:176
  10.4 0.0 copy-done.4
  10.4 15.4 %collective-permute-start = (f32[90,128]{1,0:T(8,128)S(1)}, f32[90,128]{1,0:T(8,128)S(1)}, u32[]{:S(2)}, u32[]{:S(2)}) collective-permute-start(f32[90,128]{1,0:T(8,128)S(1)} %bitcast.39), channel_id=1, source_target_pairs={{0,256},{64,320},{128,384},{192,448},{256,0},{320,64},{384,128},{4... | collective-permute-start | bytes 138248 | tf_op jit(solution)/shard_map/ppermute | solution.py:180
  25.8 1.6 %collective-permute-done = f32[90,128]{1,0:T(8,128)S(1)} collective-permute-done((f32[90,128]{1,0:T(8,128)S(1)}, f32[90,128]{1,0:T(8,128)S(1)}, u32[]{:S(2)}, u32[]{:S(2)}) %collective-permute-start) | collective-permute-done | bytes 46112 | tf_op jit(solution)/shard_map/ppermute | solution.py:180
  27.4 3.2 %collective-permute-start.1 = (f32[2,90,128]{2,1,0:T(8,128)S(1)}, f32[2,90,128]{2,1,0:T(8,128)S(1)}, u32[]{:S(2)}, u32[]{:S(2)}) collective-permute-start(f32[2,90,128]{2,1,0:T(8,128)S(1)} %pad_maximum_fusion.3), channel_id=1, source_target_pairs={{0,64},{64,0},{128,192},{192,128},{256,320},{320,256},{384,448},{4... | collective-permute-start | bytes 276488 | tf_op jit(solution)/shard_map/ppermute | solution.py:182
  30.8 2.3 %collective-permute-done.1 = f32[2,90,128]{2,1,0:T(8,128)S(1)} collective-permute-done((f32[2,90,128]{2,1,0:T(8,128)S(1)}, f32[2,90,128]{2,1,0:T(8,128)S(1)}, u32[]{:S(2)}, u32[]{:S(2)}) %collective-permute-start.1) | collective-permute-done | bytes 92192 | tf_op jit(solution)/shard_map/ppermute | solution.py:182
  33.1 4.6 %collective-permute-start.2 = (f32[2,2,90,128]{3,2,1,0:T(8,128)S(1)}, f32[2,2,90,128]{3,2,1,0:T(8,128)S(1)}, u32[]{:S(2)}, u32[]{:S(2)}) collective-permute-start(f32[2,2,90,128]{3,2,1,0:T(8,128)S(1)} %pad_maximum_fusion.2), channel_id=1, source_target_pairs={{0,192},{64,128},{128,64},{192,0},{256,448},{320,384},{384,320},{4... | collective-permute-start | bytes 552968 | tf_op jit(solution)/shard_map/ppermute | solution.py:184
  37.8 3.3 %collective-permute-done.2 = f32[2,2,90,128]{3,2,1,0:T(8,128)S(1)} collective-permute-done((f32[2,2,90,128]{3,2,1,0:T(8,128)S(1)}, f32[2,2,90,128]{3,2,1,0:T(8,128)S(1)}, u32[]{:S(2)}, u32[]{:S(2)}) %collective-permute-start.2) | collective-permute-done | bytes 184352 | tf_op jit(solution)/shard_map/ppermute | solution.py:184
  41.2 0.0 copy-start.1
  41.3 3.1 %collective-permute-start.5 = (f32[2,90,128]{2,1,0:T(8,128)S(1)}, f32[2,90,128]{2,1,0:T(8,128)S(1)}, u32[]{:S(2)}, u32[]{:S(2)}) collective-permute-start(f32[2,90,128]{2,1,0:T(8,128)S(1)} %get-tuple-element.9), channel_id=1, source_target_pairs={{0,16},{16,32},{32,48},{48,0},{1,17},{17,33},{33,49},{49,1},{2,18}... | collective-permute-start | bytes 276488 | tf_op jit(solution)/shard_map/ppermute | solution.py:194
  44.4 4.5 %collective-permute-start.4 = (f32[2,90,128]{2,1,0:T(8,128)S(1)}, f32[2,90,128]{2,1,0:T(8,128)S(1)}, u32[]{:S(2)}, u32[]{:S(2)}) collective-permute-start(f32[2,90,128]{2,1,0:T(8,128)S(1)} %get-tuple-element.10), channel_id=1, source_target_pairs={{0,32},{16,48},{32,0},{48,16},{1,33},{17,49},{33,1},{49,17},{2,34}... | collective-permute-start | bytes 276488 | tf_op jit(solution)/shard_map/ppermute | solution.py:194
  48.9 2.9 %collective-permute-start.3 = (f32[2,90,128]{2,1,0:T(8,128)S(1)}, f32[2,90,128]{2,1,0:T(8,128)S(1)}, u32[]{:S(2)}, u32[]{:S(2)}) collective-permute-start(f32[2,90,128]{2,1,0:T(8,128)S(1)} %get-tuple-element.11), channel_id=1, source_target_pairs={{0,48},{16,0},{32,16},{48,32},{1,49},{17,1},{33,17},{49,33},{2,50}... | collective-permute-start | bytes 276488 | tf_op jit(solution)/shard_map/ppermute | solution.py:194
  51.8 1.0 fusion.13.table_ref
  52.9 0.0 collective-permute-done.5
  52.9 0.0 collective-permute-done.4
  52.9 1.4 %collective-permute-done.3 = f32[2,90,128]{2,1,0:T(8,128)S(1)} collective-permute-done((f32[2,90,128]{2,1,0:T(8,128)S(1)}, f32[2,90,128]{2,1,0:T(8,128)S(1)}, u32[]{:S(2)}, u32[]{:S(2)}) %collective-permute-start.3) | collective-permute-done | bytes 92192 | tf_op jit(solution)/shard_map/ppermute | solution.py:194
  54.3 0.0 copy-done.1
  54.3 0.0 all-to-all-done.parts_ref
  54.3 1.7 %shard_map.69 = bf16[16,184,128]{2,1,0:T(8,128)(2,1)} custom-call(s32[1]{0:T(128)} %bitcast.x_ref, bf16[4,16,184,128]{3,2,1,0:T(8,128)(2,1)S(1)} %all-to-all-done.parts_ref, f32[4,2,90,128]{3,2,1,0:T(8,128)S(1)} %pad_maximum_fusion.grads_ref, bf16[512,128]{1,0:T(8,128)(2,1)S(1)} %fusion.13.table_ref), custom_call_target="tpu_custom_call" | custom-call | flops 385875968 | bytes 3014656 | tf_op jit(solution)/shard_map/pallas_call | solution.py:122
  56.0 14.9 %all-to-all-start.1 = ((bf16[16,184,128]{2,1,0:T(8,128)(2,1)}), bf16[16,184,128]{2,1,0:T(8,128)(2,1)S(1)}, u32[]{:S(2)}, u32[]{:S(2)}) async-start(bf16[16,184,128]{2,1,0:T(8,128)(2,1)} %shard_map.69), calls=%async_computation.1 | async-start | bytes 1507328 | tf_op jit(solution)/shard_map/all_to_all | solution.py:198
  70.9 0.0 copy-start.2
  70.9 1.5 %select_convert_fusion.1 = (bf16[1,512,128]{2,1,0:T(8,128)(2,1)S(1)}, bf16[1,512,128]{2,1,0:T(8,128)(2,1)S(1)}) fusion(s32[512]{0:T(512)S(1)} %get-tuple-element.21, s32[128]{0:T(128)S(1)} %fusion.33, s32[512]{0:T(512)S(1)} %get-tuple-element.20, pred[128]{0:T(512)(128)(4,1)S(1)} %get-tuple-element.23, pred[128]{0:T(512)(128)(4,1)S(1)} %get-tuple-element.22), kind=kLoop, calls=%fused_computation.30 | loop fusion | flops 983040 | bytes 267008 | tf_op jit(solution)/shard_map/convert.1
  72.5 0.0 copy-start.3
  72.5 0.0 copy-start.5
  72.5 12.3 %fusion.4.main_ref = bf16[512,1408]{1,0:T(8,128)(2,1)S(1)} fusion(s32[512]{0:T(512)S(1)} %get-tuple-element.21, s32[1408]{0:T(1024)S(1)} %fusion.31, s32[512]{0:T(512)S(1)} %get-tuple-element.20), kind=kLoop, calls=%fused_computation.5 | loop fusion | flops 8650752 | bytes 1451520 | tf_op jit(solution)/shard_map/convert_element_type | solution.py:38
  84.8 20.2 %all-to-all-done.1.rows_ref = bf16[16,184,128]{2,1,0:T(8,128)(2,1)S(1)} async-done(((bf16[16,184,128]{2,1,0:T(8,128)(2,1)}), bf16[16,184,128]{2,1,0:T(8,128)(2,1)S(1)}, u32[]{:S(2)}, u32[]{:S(2)}) %all-to-all-start.1) | async-done | bytes 753696 | tf_op jit(solution)/shard_map/all_to_all | solution.py:198
  105.0 1.7 %shard_map.70 = bf16[4,2,128,128]{3,2,1,0:T(8,128)(2,1)} custom-call(bf16[16,184,128]{2,1,0:T(8,128)(2,1)S(1)} %all-to-all-done.1.rows_ref, bf16[512,1408]{1,0:T(8,128)(2,1)S(1)} %fusion.4.main_ref, bf16[2,512,128]{2,1,0:T(8,128)(2,1)S(1)} %pad_maximum_fusion.1.tails_ref), custom_call_target="tpu_custom_call" | custom-call | flops 369098752 | bytes 2195456 | tf_op jit(solution)/shard_map/pallas_call | solution.py:156
  106.7 3.7 %all-to-all-start.2 = ((bf16[4,2,128,128]{3,2,1,0:T(8,128)(2,1)}), bf16[4,2,128,128]{3,2,1,0:T(8,128)(2,1)S(1)}, u32[]{:S(2)}, u32[]{:S(2)}) async-start(bf16[4,2,128,128]{3,2,1,0:T(8,128)(2,1)} %shard_map.70), calls=%async_computation.2 | async-start | bytes 524288 | tf_op jit(solution)/shard_map/all_to_all | solution.py:201
  110.3 0.0 copy-done
  110.4 0.2 dynamic-slice_reduce_fusion
  110.5 0.0 copy-done.2
  110.5 0.2 copy.8
  110.8 0.0 copy-done.3
  110.8 0.2 multiply_reduce_fusion
  111.0 0.7 broadcast_in_dim.48
  111.7 5.5 %all-to-all-done.2 = bf16[4,2,128,128]{3,2,1,0:T(8,128)(2,1)S(1)} async-done(((bf16[4,2,128,128]{3,2,1,0:T(8,128)(2,1)}), bf16[4,2,128,128]{3,2,1,0:T(8,128)(2,1)S(1)}, u32[]{:S(2)}, u32[]{:S(2)}) %all-to-all-start.2) | async-done | bytes 262176 | tf_op jit(solution)/shard_map/all_to_all | solution.py:201
  117.2 0.0 copy-done.5
  117.2 0.9 convert_multiply_fusion
  (18 shorter events, 0.3 us)
Async XLA Ops:
  0.6 109.7 %copy-start = (f32[8,8]{1,0:T(8,128)S(1)}, f32[8,8]{1,0:T(8,128)}, u32[]{:S(2)}) copy-start(f32[8,8]{1,0:T(8,128)} %param.8) | copy-start | bytes 772
  5.4 5.0 %copy-start.4 = (f32[1,90,128]{2,0,1:T(1,128)S(1)}, f32[1,90,128]{2,0,1:T(1,128)}, u32[]{:S(2)}) copy-start(f32[1,90,128]{2,0,1:T(1,128)} %param.6) | copy-start | bytes 138244
  5.4 48.9 %all-to-all-start = ((bf16[4,16,184,128]{3,2,1,0:T(8,128)(2,1)}), bf16[4,16,184,128]{3,2,1,0:T(8,128)(2,1)S(1)}, u32[]{:S(2)}, u32[]{:S(2)}) async-start(bf16[4,16,184,128]{3,2,1,0:T(8,128)(2,1)} %shard_map.68), calls=%async_computation | async-start | bytes 6029312 | tf_op jit(solution)/shard_map/all_to_all | solution.py:176
  10.4 17.0 %collective-permute-start = (f32[90,128]{1,0:T(8,128)S(1)}, f32[90,128]{1,0:T(8,128)S(1)}, u32[]{:S(2)}, u32[]{:S(2)}) collective-permute-start(f32[90,128]{1,0:T(8,128)S(1)} %bitcast.39), channel_id=1, source_target_pairs={{0,256},{64,320},{128,384},{192,448},{256,0},{320,64},{384,128},{4... | collective-permute-start | bytes 138248 | tf_op jit(solution)/shard_map/ppermute | solution.py:180
  27.4 5.7 %collective-permute-start.1 = (f32[2,90,128]{2,1,0:T(8,128)S(1)}, f32[2,90,128]{2,1,0:T(8,128)S(1)}, u32[]{:S(2)}, u32[]{:S(2)}) collective-permute-start(f32[2,90,128]{2,1,0:T(8,128)S(1)} %pad_maximum_fusion.3), channel_id=1, source_target_pairs={{0,64},{64,0},{128,192},{192,128},{256,320},{320,256},{384,448},{4... | collective-permute-start | bytes 276488 | tf_op jit(solution)/shard_map/ppermute | solution.py:182
  33.1 8.0 %collective-permute-start.2 = (f32[2,2,90,128]{3,2,1,0:T(8,128)S(1)}, f32[2,2,90,128]{3,2,1,0:T(8,128)S(1)}, u32[]{:S(2)}, u32[]{:S(2)}) collective-permute-start(f32[2,2,90,128]{3,2,1,0:T(8,128)S(1)} %pad_maximum_fusion.2), channel_id=1, source_target_pairs={{0,192},{64,128},{128,64},{192,0},{256,448},{320,384},{384,320},{4... | collective-permute-start | bytes 552968 | tf_op jit(solution)/shard_map/ppermute | solution.py:184
  41.2 13.1 %copy-start.1 = (f32[2,4,90,128]{3,2,0,1:T(8,128)}, f32[2,4,90,128]{3,2,0,1:T(8,128)S(1)}, u32[]{:S(2)}) copy-start(f32[2,4,90,128]{3,2,0,1:T(8,128)S(1)} %maximum_bitcast_fusion) | copy-start | bytes 1105924
  41.3 11.6 %collective-permute-start.5 = (f32[2,90,128]{2,1,0:T(8,128)S(1)}, f32[2,90,128]{2,1,0:T(8,128)S(1)}, u32[]{:S(2)}, u32[]{:S(2)}) collective-permute-start(f32[2,90,128]{2,1,0:T(8,128)S(1)} %get-tuple-element.9), channel_id=1, source_target_pairs={{0,16},{16,32},{32,48},{48,0},{1,17},{17,33},{33,49},{49,1},{2,18}... | collective-permute-start | bytes 276488 | tf_op jit(solution)/shard_map/ppermute | solution.py:194
  44.4 8.5 %collective-permute-start.4 = (f32[2,90,128]{2,1,0:T(8,128)S(1)}, f32[2,90,128]{2,1,0:T(8,128)S(1)}, u32[]{:S(2)}, u32[]{:S(2)}) collective-permute-start(f32[2,90,128]{2,1,0:T(8,128)S(1)} %get-tuple-element.10), channel_id=1, source_target_pairs={{0,32},{16,48},{32,0},{48,16},{1,33},{17,49},{33,1},{49,17},{2,34}... | collective-permute-start | bytes 276488 | tf_op jit(solution)/shard_map/ppermute | solution.py:194
  48.9 5.4 %collective-permute-start.3 = (f32[2,90,128]{2,1,0:T(8,128)S(1)}, f32[2,90,128]{2,1,0:T(8,128)S(1)}, u32[]{:S(2)}, u32[]{:S(2)}) collective-permute-start(f32[2,90,128]{2,1,0:T(8,128)S(1)} %get-tuple-element.11), channel_id=1, source_target_pairs={{0,48},{16,0},{32,16},{48,32},{1,49},{17,1},{33,17},{49,33},{2,50}... | collective-permute-start | bytes 276488 | tf_op jit(solution)/shard_map/ppermute | solution.py:194
  56.0 49.0 %all-to-all-start.1 = ((bf16[16,184,128]{2,1,0:T(8,128)(2,1)}), bf16[16,184,128]{2,1,0:T(8,128)(2,1)S(1)}, u32[]{:S(2)}, u32[]{:S(2)}) async-start(bf16[16,184,128]{2,1,0:T(8,128)(2,1)} %shard_map.69), calls=%async_computation.1 | async-start | bytes 1507328 | tf_op jit(solution)/shard_map/all_to_all | solution.py:198
  70.9 39.7 %copy-start.2 = (f32[2,4,90,128]{3,2,0,1:T(8,128)S(1)}, f32[2,4,90,128]{3,2,0,1:T(8,128)}, u32[]{:S(2)}) copy-start(f32[2,4,90,128]{3,2,0,1:T(8,128)} %copy-done.1) | copy-start | bytes 1105924
  72.5 38.3 %copy-start.3 = (f32[8,90,128]{2,0,1:T(8,128)S(1)}, f32[8,90,128]{2,0,1:T(8,128)}, u32[]{:S(2)}) copy-start(f32[8,90,128]{2,0,1:T(8,128)} %param.7) | copy-start | bytes 1105924
  72.5 44.6 %copy-start.5 = (f32[128,128]{1,0:T(8,128)S(1)}, f32[128,128]{1,0:T(8,128)}, u32[]{:S(2)}) copy-start(f32[128,128]{1,0:T(8,128)} %param.9) | copy-start | bytes 196612
  106.7 10.5 %all-to-all-start.2 = ((bf16[4,2,128,128]{3,2,1,0:T(8,128)(2,1)}), bf16[4,2,128,128]{3,2,1,0:T(8,128)(2,1)S(1)}, u32[]{:S(2)}, u32[]{:S(2)}) async-start(bf16[4,2,128,128]{3,2,1,0:T(8,128)(2,1)} %shard_map.70), calls=%async_computation.2 | async-start | bytes 524288 | tf_op jit(solution)/shard_map/all_to_all | solution.py:201

commit v7 on v6

--- a/solution.py
+++ b/solution.py
@@ -60,12 +60,24 @@
     return jnp.concatenate([*[f[:whole] for f in fields], *[f[whole:] for f in fields], empty])
 
 
-def spread_kernel(members_ref, out_ref, wide):
-    count, lon, levels, lat = members_ref.shape
+def spread_kernel(members_ref, out_ref, held, wide, spread_out, arrived, done):
+    count, lon, levels, lat = held.shape
     whole = lon // TILE * TILE
     rows = out_ref.shape[2]
+    group = count // done.shape[0]
+
+    def to_held(m):
+        return pltpu.make_async_copy(members_ref.at[m], held.at[m], arrived.at[m])
+
+    def to_out(i):
+        span = pl.ds(i * group, group)
+        return pltpu.make_async_copy(spread_out.at[:, span], out_ref.at[:, span], done.at[i])
+
     for m in range(count):
-        wide[m % 2] = members_ref[m].astype(jnp.float32).reshape(lon * levels, lat)
+        to_held(m).start()
+    for m in range(count):
+        to_held(m).wait()
+        wide[m % 2] = held[m].astype(jnp.float32).reshape(lon * levels, lat)
         for part in range(levels // PAIR):
             firsts = [part * PAIR + place for place in range(PAIR)]
             pieces = [wide[m % 2, pl.ds(first, whole, stride=levels), :] for first in firsts]
@@ -73,19 +85,28 @@
                 wide[m % 2, pl.ds(first + n * levels, 1), :] for first in firsts for n in range(whole, lon)
             ]
             empty = jnp.zeros((rows - PAIR * lon, lat), jnp.float32)
-            out_ref[part, m] = jnp.concatenate([*pieces, *lasts, empty]).astype(jnp.bfloat16)
+            spread_out[part, m] = jnp.concatenate([*pieces, *lasts, empty]).astype(jnp.bfloat16)
+        if m % group == group - 1:
+            to_out(m // group).start()
+    for i in range(done.shape[0]):
+        to_out(i).wait()
 
 
 def spread(members, rows):
     count, lon, levels, lat = members.shape
-    step = min(4, count)
+    shape = (levels // PAIR, count, rows, lat)
     return pl.pallas_call(
         spread_kernel,
-        out_shape=jax.ShapeDtypeStruct((levels // PAIR, count, rows, lat), members.dtype),
-        grid=(count // step,),
-        in_specs=[pl.BlockSpec((step, lon, levels, lat), lambda i: (i, 0, 0, 0))],
-        out_specs=pl.BlockSpec((levels // PAIR, step, rows, lat), lambda i: (0, i, 0, 0)),
-        scratch_shapes=[pltpu.VMEM((2, lon * levels, lat), jnp.float32)],
+        out_shape=pltpu.HBM(shape, members.dtype),
+        in_specs=[pl.BlockSpec(memory_space=pltpu.HBM)],
+        out_specs=pl.BlockSpec(memory_space=pltpu.HBM),
+        scratch_shapes=[
+            pltpu.VMEM(members.shape, members.dtype),
+            pltpu.VMEM((2, lon * levels, lat), jnp.float32),
+            pltpu.VMEM(shape, members.dtype),
+            pltpu.SemaphoreType.DMA((count,)),
+            pltpu.SemaphoreType.DMA((max(1, count // 2),)),
+        ],
         compiler_params=pltpu.CompilerParams(vmem_limit_bytes=56 * 2**20),
         cost_estimate=pl.CostEstimate(flops=members.size, bytes_accessed=4 * members.size, transcendentals=0),
     )(members)

time: 119 us -> 118 us (level)
  Pallas kernels: 8.08 us -> 6.65 us
    pallas_call x1, Pallas kernels: 4.73 us -> 3.3 us  [spread(): pl.pallas_call(spread_kernel, out_shape=pltpu.HBM(shape, members.dtype),...]
where the time goes in v7:
time: 118 us; the launch traced here: 117 us
  starting transfers between devices  57.3 us (49%)
  waiting for transfers between devices  34.3 us (29%)
  other arithmetic  16.1 us (14%)
  Pallas kernels  6.65 us (6%)
  local copies, waits for them, and re-layouts  1.19 us (1%)
    all_to_all x1, waiting for transfers between devices, local(): whole = lax.all_to_all(sums, 'lon', split_axis=0, concat_axis=0, tiled=True)  20.2 us
    ppermute x1, starting transfers between devices, local(): far_grad = lax.ppermute(own_grad, 'mem', partners(8, 4))  15.4 us
    all_to_all x1, starting transfers between devices, local(): whole = lax.all_to_all(sums, 'lon', split_axis=0, concat_axis=0, tiled=True)  14.9 us
    convert_element_type x1, other arithmetic, lon_tables_make(): return (main.astype(jnp.bfloat16), jnp.stack(tails).astype(jnp.bfloat16))  12.3 us
    ppermute x3, starting transfers between devices, local(): lax.ppermute(pair(4 - d), 'lat', [(i, (i - d) % 4) for i in range(4)])  10.5 us
    all_to_all x1, waiting for transfers between devices, local(): lax.all_to_all(zonal, 'lat', split_axis=0, concat_axis=0, tiled=True)  5.51 us
    all_to_all x1, starting transfers between devices, local(): parts = lax.all_to_all(sent, 'lat', split_axis=0, concat_axis=0, tiled=True)  4.99 us
    ppermute x1, starting transfers between devices, local(): others = lax.ppermute(two, 'mem', partners(8, 3))  4.64 us
  transfers between devices with their start and end apart: 9, of which 6 were waited for; matrix products, arithmetic and copies ran while one was open for 14% of the time, Pallas kernels for 0%

profile of v7, /device:TPU:1, one launch (start us, length us, event | category | flops | bytes accessed | tf_op | source)
XLA Modules:
  0.0 116.6 jit_solution(4827544627223128684)
XLA Ops:
  0.6 0.0 copy-start
  0.6 3.3 %shard_map.68 = bf16[4,16,184,128]{3,2,1,0:T(8,128)(2,1)} custom-call(bf16[16,90,8,128]{3,2,1,0:T(8,128)(2,1)} %bitcast.33), custom_call_target="tpu_custom_call" | custom-call | flops 1474560 | bytes 5898240 | tf_op jit(solution)/shard_map/pallas_call | solution.py:98
  4.0 0.0 copy-start.4
  4.0 5.0 %all-to-all-start = ((bf16[4,16,184,128]{3,2,1,0:T(8,128)(2,1)}), bf16[4,16,184,128]{3,2,1,0:T(8,128)(2,1)S(1)}, u32[]{:S(2)}, u32[]{:S(2)}) async-start(bf16[4,16,184,128]{3,2,1,0:T(8,128)(2,1)} %shard_map.68), calls=%async_computation | async-start | bytes 6029312 | tf_op jit(solution)/shard_map/all_to_all | solution.py:197
  9.0 0.0 copy-done.4
  9.0 15.4 %collective-permute-start = (f32[90,128]{1,0:T(8,128)S(1)}, f32[90,128]{1,0:T(8,128)S(1)}, u32[]{:S(2)}, u32[]{:S(2)}) collective-permute-start(f32[90,128]{1,0:T(8,128)S(1)} %bitcast.39), channel_id=1, source_target_pairs={{0,256},{64,320},{128,384},{192,448},{256,0},{320,64},{384,128},{4... | collective-permute-start | bytes 138248 | tf_op jit(solution)/shard_map/ppermute | solution.py:201
  24.4 1.6 %collective-permute-done = f32[90,128]{1,0:T(8,128)S(1)} collective-permute-done((f32[90,128]{1,0:T(8,128)S(1)}, f32[90,128]{1,0:T(8,128)S(1)}, u32[]{:S(2)}, u32[]{:S(2)}) %collective-permute-start) | collective-permute-done | bytes 46112 | tf_op jit(solution)/shard_map/ppermute | solution.py:201
  26.0 3.2 %collective-permute-start.1 = (f32[2,90,128]{2,1,0:T(8,128)S(1)}, f32[2,90,128]{2,1,0:T(8,128)S(1)}, u32[]{:S(2)}, u32[]{:S(2)}) collective-permute-start(f32[2,90,128]{2,1,0:T(8,128)S(1)} %pad_maximum_fusion.3), channel_id=1, source_target_pairs={{0,64},{64,0},{128,192},{192,128},{256,320},{320,256},{384,448},{4... | collective-permute-start | bytes 276488 | tf_op jit(solution)/shard_map/ppermute | solution.py:203
  29.4 2.3 %collective-permute-done.1 = f32[2,90,128]{2,1,0:T(8,128)S(1)} collective-permute-done((f32[2,90,128]{2,1,0:T(8,128)S(1)}, f32[2,90,128]{2,1,0:T(8,128)S(1)}, u32[]{:S(2)}, u32[]{:S(2)}) %collective-permute-start.1) | collective-permute-done | bytes 92192 | tf_op jit(solution)/shard_map/ppermute | solution.py:203
  31.7 4.6 %collective-permute-start.2 = (f32[2,2,90,128]{3,2,1,0:T(8,128)S(1)}, f32[2,2,90,128]{3,2,1,0:T(8,128)S(1)}, u32[]{:S(2)}, u32[]{:S(2)}) collective-permute-start(f32[2,2,90,128]{3,2,1,0:T(8,128)S(1)} %pad_maximum_fusion.2), channel_id=1, source_target_pairs={{0,192},{64,128},{128,64},{192,0},{256,448},{320,384},{384,320},{4... | collective-permute-start | bytes 552968 | tf_op jit(solution)/shard_map/ppermute | solution.py:205
  36.4 3.3 %collective-permute-done.2 = f32[2,2,90,128]{3,2,1,0:T(8,128)S(1)} collective-permute-done((f32[2,2,90,128]{3,2,1,0:T(8,128)S(1)}, f32[2,2,90,128]{3,2,1,0:T(8,128)S(1)}, u32[]{:S(2)}, u32[]{:S(2)}) %collective-permute-start.2) | collective-permute-done | bytes 184352 | tf_op jit(solution)/shard_map/ppermute | solution.py:205
  39.8 0.0 copy-start.1
  39.9 3.1 %collective-permute-start.5 = (f32[2,90,128]{2,1,0:T(8,128)S(1)}, f32[2,90,128]{2,1,0:T(8,128)S(1)}, u32[]{:S(2)}, u32[]{:S(2)}) collective-permute-start(f32[2,90,128]{2,1,0:T(8,128)S(1)} %get-tuple-element.9), channel_id=1, source_target_pairs={{0,16},{16,32},{32,48},{48,0},{1,17},{17,33},{33,49},{49,1},{2,18}... | collective-permute-start | bytes 276488 | tf_op jit(solution)/shard_map/ppermute | solution.py:215
  43.0 4.5 %collective-permute-start.4 = (f32[2,90,128]{2,1,0:T(8,128)S(1)}, f32[2,90,128]{2,1,0:T(8,128)S(1)}, u32[]{:S(2)}, u32[]{:S(2)}) collective-permute-start(f32[2,90,128]{2,1,0:T(8,128)S(1)} %get-tuple-element.10), channel_id=1, source_target_pairs={{0,32},{16,48},{32,0},{48,16},{1,33},{17,49},{33,1},{49,17},{2,34}... | collective-permute-start | bytes 276488 | tf_op jit(solution)/shard_map/ppermute | solution.py:215
  47.5 2.9 %collective-permute-start.3 = (f32[2,90,128]{2,1,0:T(8,128)S(1)}, f32[2,90,128]{2,1,0:T(8,128)S(1)}, u32[]{:S(2)}, u32[]{:S(2)}) collective-permute-start(f32[2,90,128]{2,1,0:T(8,128)S(1)} %get-tuple-element.11), channel_id=1, source_target_pairs={{0,48},{16,0},{32,16},{48,32},{1,49},{17,1},{33,17},{49,33},{2,50}... | collective-permute-start | bytes 276488 | tf_op jit(solution)/shard_map/ppermute | solution.py:215
  50.4 1.0 fusion.13.table_ref
  51.5 0.0 collective-permute-done.5
  51.5 0.0 collective-permute-done.4
  51.5 1.4 %collective-permute-done.3 = f32[2,90,128]{2,1,0:T(8,128)S(1)} collective-permute-done((f32[2,90,128]{2,1,0:T(8,128)S(1)}, f32[2,90,128]{2,1,0:T(8,128)S(1)}, u32[]{:S(2)}, u32[]{:S(2)}) %collective-permute-start.3) | collective-permute-done | bytes 92192 | tf_op jit(solution)/shard_map/ppermute | solution.py:215
  52.9 0.0 copy-done.1
  52.9 0.0 all-to-all-done.parts_ref
  52.9 1.7 %shard_map.69 = bf16[16,184,128]{2,1,0:T(8,128)(2,1)} custom-call(s32[1]{0:T(128)} %bitcast.x_ref, bf16[4,16,184,128]{3,2,1,0:T(8,128)(2,1)S(1)} %all-to-all-done.parts_ref, f32[4,2,90,128]{3,2,1,0:T(8,128)S(1)} %pad_maximum_fusion.grads_ref, bf16[512,128]{1,0:T(8,128)(2,1)S(1)} %fusion.13.table_ref), custom_call_target="tpu_custom_call" | custom-call | flops 385875968 | bytes 3014656 | tf_op jit(solution)/shard_map/pallas_call | solution.py:143
  54.6 14.9 %all-to-all-start.1 = ((bf16[16,184,128]{2,1,0:T(8,128)(2,1)}), bf16[16,184,128]{2,1,0:T(8,128)(2,1)S(1)}, u32[]{:S(2)}, u32[]{:S(2)}) async-start(bf16[16,184,128]{2,1,0:T(8,128)(2,1)} %shard_map.69), calls=%async_computation.1 | async-start | bytes 1507328 | tf_op jit(solution)/shard_map/all_to_all | solution.py:219
  69.5 0.0 copy-start.2
  69.5 1.5 %select_convert_fusion.1 = (bf16[1,512,128]{2,1,0:T(8,128)(2,1)S(1)}, bf16[1,512,128]{2,1,0:T(8,128)(2,1)S(1)}) fusion(s32[512]{0:T(512)S(1)} %get-tuple-element.21, s32[128]{0:T(128)S(1)} %fusion.33, s32[512]{0:T(512)S(1)} %get-tuple-element.20, pred[128]{0:T(512)(128)(4,1)S(1)} %get-tuple-element.23, pred[128]{0:T(512)(128)(4,1)S(1)} %get-tuple-element.22), kind=kLoop, calls=%fused_computation.30 | loop fusion | flops 983040 | bytes 267008 | tf_op jit(solution)/shard_map/convert.1
  71.1 0.0 copy-start.3
  71.1 0.0 copy-start.5
  71.1 12.3 %fusion.4.main_ref = bf16[512,1408]{1,0:T(8,128)(2,1)S(1)} fusion(s32[512]{0:T(512)S(1)} %get-tuple-element.21, s32[1408]{0:T(1024)S(1)} %fusion.31, s32[512]{0:T(512)S(1)} %get-tuple-element.20), kind=kLoop, calls=%fused_computation.5 | loop fusion | flops 8650752 | bytes 1451520 | tf_op jit(solution)/shard_map/convert_element_type | solution.py:38
  83.5 20.2 %all-to-all-done.1.rows_ref = bf16[16,184,128]{2,1,0:T(8,128)(2,1)S(1)} async-done(((bf16[16,184,128]{2,1,0:T(8,128)(2,1)}), bf16[16,184,128]{2,1,0:T(8,128)(2,1)S(1)}, u32[]{:S(2)}, u32[]{:S(2)}) %all-to-all-start.1) | async-done | bytes 753696 | tf_op jit(solution)/shard_map/all_to_all | solution.py:219
  103.6 1.7 %shard_map.70 = bf16[4,2,128,128]{3,2,1,0:T(8,128)(2,1)} custom-call(bf16[16,184,128]{2,1,0:T(8,128)(2,1)S(1)} %all-to-all-done.1.rows_ref, bf16[512,1408]{1,0:T(8,128)(2,1)S(1)} %fusion.4.main_ref, bf16[2,512,128]{2,1,0:T(8,128)(2,1)S(1)} %pad_maximum_fusion.1.tails_ref), custom_call_target="tpu_custom_call" | custom-call | flops 369098752 | bytes 2195456 | tf_op jit(solution)/shard_map/pallas_call | solution.py:177
  105.3 3.7 %all-to-all-start.2 = ((bf16[4,2,128,128]{3,2,1,0:T(8,128)(2,1)}), bf16[4,2,128,128]{3,2,1,0:T(8,128)(2,1)S(1)}, u32[]{:S(2)}, u32[]{:S(2)}) async-start(bf16[4,2,128,128]{3,2,1,0:T(8,128)(2,1)} %shard_map.70), calls=%async_computation.2 | async-start | bytes 524288 | tf_op jit(solution)/shard_map/all_to_all | solution.py:222
  109.0 0.0 copy-done
  109.0 0.2 dynamic-slice_reduce_fusion
  109.1 0.0 copy-done.2
  109.1 0.2 copy.8
  109.4 0.0 copy-done.3
  109.4 0.2 multiply_reduce_fusion
  109.6 0.7 broadcast_in_dim.48
  110.3 5.5 %all-to-all-done.2 = bf16[4,2,128,128]{3,2,1,0:T(8,128)(2,1)S(1)} async-done(((bf16[4,2,128,128]{3,2,1,0:T(8,128)(2,1)}), bf16[4,2,128,128]{3,2,1,0:T(8,128)(2,1)S(1)}, u32[]{:S(2)}, u32[]{:S(2)}) %all-to-all-start.2) | async-done | bytes 262176 | tf_op jit(solution)/shard_map/all_to_all | solution.py:222
  115.8 0.0 copy-done.5
  115.8 0.9 convert_multiply_fusion
  (18 shorter events, 0.3 us)
Async XLA Ops:
  0.6 108.3 %copy-start = (f32[8,8]{1,0:T(8,128)S(1)}, f32[8,8]{1,0:T(8,128)}, u32[]{:S(2)}) copy-start(f32[8,8]{1,0:T(8,128)} %param.8) | copy-start | bytes 772
  4.0 5.0 %copy-start.4 = (f32[1,90,128]{2,0,1:T(1,128)S(1)}, f32[1,90,128]{2,0,1:T(1,128)}, u32[]{:S(2)}) copy-start(f32[1,90,128]{2,0,1:T(1,128)} %param.6) | copy-start | bytes 138244
  4.0 48.9 %all-to-all-start = ((bf16[4,16,184,128]{3,2,1,0:T(8,128)(2,1)}), bf16[4,16,184,128]{3,2,1,0:T(8,128)(2,1)S(1)}, u32[]{:S(2)}, u32[]{:S(2)}) async-start(bf16[4,16,184,128]{3,2,1,0:T(8,128)(2,1)} %shard_map.68), calls=%async_computation | async-start | bytes 6029312 | tf_op jit(solution)/shard_map/all_to_all | solution.py:197
  9.0 17.0 %collective-permute-start = (f32[90,128]{1,0:T(8,128)S(1)}, f32[90,128]{1,0:T(8,128)S(1)}, u32[]{:S(2)}, u32[]{:S(2)}) collective-permute-start(f32[90,128]{1,0:T(8,128)S(1)} %bitcast.39), channel_id=1, source_target_pairs={{0,256},{64,320},{128,384},{192,448},{256,0},{320,64},{384,128},{4... | collective-permute-start | bytes 138248 | tf_op jit(solution)/shard_map/ppermute | solution.py:201
  26.0 5.7 %collective-permute-start.1 = (f32[2,90,128]{2,1,0:T(8,128)S(1)}, f32[2,90,128]{2,1,0:T(8,128)S(1)}, u32[]{:S(2)}, u32[]{:S(2)}) collective-permute-start(f32[2,90,128]{2,1,0:T(8,128)S(1)} %pad_maximum_fusion.3), channel_id=1, source_target_pairs={{0,64},{64,0},{128,192},{192,128},{256,320},{320,256},{384,448},{4... | collective-permute-start | bytes 276488 | tf_op jit(solution)/shard_map/ppermute | solution.py:203
  31.7 8.0 %collective-permute-start.2 = (f32[2,2,90,128]{3,2,1,0:T(8,128)S(1)}, f32[2,2,90,128]{3,2,1,0:T(8,128)S(1)}, u32[]{:S(2)}, u32[]{:S(2)}) collective-permute-start(f32[2,2,90,128]{3,2,1,0:T(8,128)S(1)} %pad_maximum_fusion.2), channel_id=1, source_target_pairs={{0,192},{64,128},{128,64},{192,0},{256,448},{320,384},{384,320},{4... | collective-permute-start | bytes 552968 | tf_op jit(solution)/shard_map/ppermute | solution.py:205
  39.8 13.1 %copy-start.1 = (f32[2,4,90,128]{3,2,0,1:T(8,128)}, f32[2,4,90,128]{3,2,0,1:T(8,128)S(1)}, u32[]{:S(2)}) copy-start(f32[2,4,90,128]{3,2,0,1:T(8,128)S(1)} %maximum_bitcast_fusion) | copy-start | bytes 1105924
  39.9 11.6 %collective-permute-start.5 = (f32[2,90,128]{2,1,0:T(8,128)S(1)}, f32[2,90,128]{2,1,0:T(8,128)S(1)}, u32[]{:S(2)}, u32[]{:S(2)}) collective-permute-start(f32[2,90,128]{2,1,0:T(8,128)S(1)} %get-tuple-element.9), channel_id=1, source_target_pairs={{0,16},{16,32},{32,48},{48,0},{1,17},{17,33},{33,49},{49,1},{2,18}... | collective-permute-start | bytes 276488 | tf_op jit(solution)/shard_map/ppermute | solution.py:215
  43.0 8.5 %collective-permute-start.4 = (f32[2,90,128]{2,1,0:T(8,128)S(1)}, f32[2,90,128]{2,1,0:T(8,128)S(1)}, u32[]{:S(2)}, u32[]{:S(2)}) collective-permute-start(f32[2,90,128]{2,1,0:T(8,128)S(1)} %get-tuple-element.10), channel_id=1, source_target_pairs={{0,32},{16,48},{32,0},{48,16},{1,33},{17,49},{33,1},{49,17},{2,34}... | collective-permute-start | bytes 276488 | tf_op jit(solution)/shard_map/ppermute | solution.py:215
  47.5 5.4 %collective-permute-start.3 = (f32[2,90,128]{2,1,0:T(8,128)S(1)}, f32[2,90,128]{2,1,0:T(8,128)S(1)}, u32[]{:S(2)}, u32[]{:S(2)}) collective-permute-start(f32[2,90,128]{2,1,0:T(8,128)S(1)} %get-tuple-element.11), channel_id=1, source_target_pairs={{0,48},{16,0},{32,16},{48,32},{1,49},{17,1},{33,17},{49,33},{2,50}... | collective-permute-start | bytes 276488 | tf_op jit(solution)/shard_map/ppermute | solution.py:215
  54.6 49.0 %all-to-all-start.1 = ((bf16[16,184,128]{2,1,0:T(8,128)(2,1)}), bf16[16,184,128]{2,1,0:T(8,128)(2,1)S(1)}, u32[]{:S(2)}, u32[]{:S(2)}) async-start(bf16[16,184,128]{2,1,0:T(8,128)(2,1)} %shard_map.69), calls=%async_computation.1 | async-start | bytes 1507328 | tf_op jit(solution)/shard_map/all_to_all | solution.py:219
  69.5 39.7 %copy-start.2 = (f32[2,4,90,128]{3,2,0,1:T(8,128)S(1)}, f32[2,4,90,128]{3,2,0,1:T(8,128)}, u32[]{:S(2)}) copy-start(f32[2,4,90,128]{3,2,0,1:T(8,128)} %copy-done.1) | copy-start | bytes 1105924
  71.1 38.3 %copy-start.3 = (f32[8,90,128]{2,0,1:T(8,128)S(1)}, f32[8,90,128]{2,0,1:T(8,128)}, u32[]{:S(2)}) copy-start(f32[8,90,128]{2,0,1:T(8,128)} %param.7) | copy-start | bytes 1105924
  71.1 44.6 %copy-start.5 = (f32[128,128]{1,0:T(8,128)S(1)}, f32[128,128]{1,0:T(8,128)}, u32[]{:S(2)}) copy-start(f32[128,128]{1,0:T(8,128)} %param.9) | copy-start | bytes 196612
  105.3 10.5 %all-to-all-start.2 = ((bf16[4,2,128,128]{3,2,1,0:T(8,128)(2,1)}), bf16[4,2,128,128]{3,2,1,0:T(8,128)(2,1)S(1)}, u32[]{:S(2)}, u32[]{:S(2)}) async-start(bf16[4,2,128,128]{3,2,1,0:T(8,128)(2,1)} %shard_map.70), calls=%async_computation.2 | async-start | bytes 524288 | tf_op jit(solution)/shard_map/all_to_all | solution.py:222

commit v8 on v7

--- a/solution.py
+++ b/solution.py
@@ -77,12 +77,12 @@
         to_held(m).start()
     for m in range(count):
         to_held(m).wait()
-        wide[m % 2] = held[m].astype(jnp.float32).reshape(lon * levels, lat)
+        wide[m % 2, : lon * levels] = held[m].astype(jnp.float32).reshape(lon * levels, lat)
         for part in range(levels // PAIR):
             firsts = [part * PAIR + place for place in range(PAIR)]
             pieces = [wide[m % 2, pl.ds(first, whole, stride=levels), :] for first in firsts]
             lasts = [
-                wide[m % 2, pl.ds(first + n * levels, 1), :] for first in firsts for n in range(whole, lon)
+                wide[m % 2, pl.ds(first + whole * levels, lon - whole, stride=levels), :] for first in firsts
             ]
             empty = jnp.zeros((rows - PAIR * lon, lat), jnp.float32)
             spread_out[part, m] = jnp.concatenate([*pieces, *lasts, empty]).astype(jnp.bfloat16)
@@ -102,7 +102,7 @@
         out_specs=pl.BlockSpec(memory_space=pltpu.HBM),
         scratch_shapes=[
             pltpu.VMEM(members.shape, members.dtype),
-            pltpu.VMEM((2, lon * levels, lat), jnp.float32),
+            pltpu.VMEM((2, (lon + TILE) * levels, lat), jnp.float32),
             pltpu.VMEM(shape, members.dtype),
             pltpu.SemaphoreType.DMA((count,)),
             pltpu.SemaphoreType.DMA((max(1, count // 2),)),
@@ -157,10 +157,14 @@
     )(jnp.reshape(x, (1,)).astype(jnp.int32), parts, grads, table)
 
 
-def zonal_kernel(rows_ref, main_ref, tails_ref, out_ref):
+def zonal_kernel(rows_ref, main_ref, tails_ref, out_ref, sums_ref, done):
     blocks = rows_ref.shape[0]
     whole = main_ref.shape[1] // blocks
     bands = [rows_ref[block].astype(jnp.float32) for block in range(blocks)]
+
+    def to_out(level):
+        return pltpu.make_async_copy(sums_ref.at[:, level], out_ref.at[:, level], done.at[level])
+
     last = jnp.concatenate([band[PAIR * whole :] for band in bands]).astype(jnp.bfloat16)
     for level in range(PAIR):
         first = [band[level * whole : (level + 1) * whole] for band in bands]
@@ -169,7 +173,10 @@
         ) + jnp.dot(tails_ref[level], last, preferred_element_type=jnp.float32)
         quarter = sums.shape[0] // 4
         for part in range(4):
-            out_ref[part, level] = sums[part * quarter : (part + 1) * quarter].astype(jnp.bfloat16)
+            sums_ref[part, level] = sums[part * quarter : (part + 1) * quarter].astype(jnp.bfloat16)
+        to_out(level).start()
+    for level in range(PAIR):
+        to_out(level).wait()
 
 
 def zonal_sums(rows, main, tails):
@@ -178,7 +185,11 @@
         zonal_kernel,
         out_shape=pltpu.HBM((4, PAIR, waves // 4, k_lat), jnp.bfloat16),
         in_specs=[pl.BlockSpec(memory_space=pltpu.VMEM)] * 3,
-        out_specs=pl.BlockSpec(memory_space=pltpu.VMEM),
+        out_specs=pl.BlockSpec(memory_space=pltpu.HBM),
+        scratch_shapes=[
+            pltpu.VMEM((4, PAIR, waves // 4, k_lat), jnp.bfloat16),
+            pltpu.SemaphoreType.DMA((PAIR,)),
+        ],
         compiler_params=pltpu.CompilerParams(vmem_limit_bytes=24 * 2**20),
         cost_estimate=pl.CostEstimate(
             flops=2 * PAIR * main.size * k_lat, bytes_accessed=2 * (main.size + rows.size), transcendentals=0

time: 118 us -> 118 us (level)
  no operation moved by 1% of the time
where the time goes in v8:
time: 118 us; the launch traced here: 117 us
  starting transfers between devices  57.3 us (49%)
  waiting for transfers between devices  34.3 us (29%)
  other arithmetic  16.1 us (14%)
  Pallas kernels  6.67 us (6%)
  local copies, waits for them, and re-layouts  1.19 us (1%)
    all_to_all x1, waiting for transfers between devices, local(): whole = lax.all_to_all(sums, 'lon', split_axis=0, concat_axis=0, tiled=True)  20.2 us
    ppermute x1, starting transfers between devices, local(): far_grad = lax.ppermute(own_grad, 'mem', partners(8, 4))  15.4 us
    all_to_all x1, starting transfers between devices, local(): whole = lax.all_to_all(sums, 'lon', split_axis=0, concat_axis=0, tiled=True)  14.9 us
    convert_element_type x1, other arithmetic, lon_tables_make(): return (main.astype(jnp.bfloat16), jnp.stack(tails).astype(jnp.bfloat16))  12.3 us
    ppermute x3, starting transfers between devices, local(): lax.ppermute(pair(4 - d), 'lat', [(i, (i - d) % 4) for i in range(4)])  10.5 us
    all_to_all x1, waiting for transfers between devices, local(): lax.all_to_all(zonal, 'lat', split_axis=0, concat_axis=0, tiled=True)  5.51 us
    all_to_all x1, starting transfers between devices, local(): parts = lax.all_to_all(sent, 'lat', split_axis=0, concat_axis=0, tiled=True)  4.99 us
    ppermute x1, starting transfers between devices, local(): others = lax.ppermute(two, 'mem', partners(8, 3))  4.64 us
  transfers between devices with their start and end apart: 9, of which 6 were waited for; matrix products, arithmetic and copies ran while one was open for 14% of the time, Pallas kernels for 0%

profile of v8, /device:TPU:1, one launch (start us, length us, event | category | flops | bytes accessed | tf_op | source)
XLA Modules:
  0.0 116.7 jit_solution(5871400108520579295)
XLA Ops:
  0.6 0.0 copy-start
  0.6 3.3 %shard_map.68 = bf16[4,16,184,128]{3,2,1,0:T(8,128)(2,1)} custom-call(bf16[16,90,8,128]{3,2,1,0:T(8,128)(2,1)} %bitcast.33), custom_call_target="tpu_custom_call" | custom-call | flops 1474560 | bytes 5898240 | tf_op jit(solution)/shard_map/pallas_call | solution.py:98
  4.0 0.0 copy-start.4
  4.0 5.0 %all-to-all-start = ((bf16[4,16,184,128]{3,2,1,0:T(8,128)(2,1)}), bf16[4,16,184,128]{3,2,1,0:T(8,128)(2,1)S(1)}, u32[]{:S(2)}, u32[]{:S(2)}) async-start(bf16[4,16,184,128]{3,2,1,0:T(8,128)(2,1)} %shard_map.68), calls=%async_computation | async-start | bytes 6029312 | tf_op jit(solution)/shard_map/all_to_all | solution.py:208
  9.0 0.0 copy-done.4
  9.0 15.4 %collective-permute-start = (f32[90,128]{1,0:T(8,128)S(1)}, f32[90,128]{1,0:T(8,128)S(1)}, u32[]{:S(2)}, u32[]{:S(2)}) collective-permute-start(f32[90,128]{1,0:T(8,128)S(1)} %bitcast.39), channel_id=1, source_target_pairs={{0,256},{64,320},{128,384},{192,448},{256,0},{320,64},{384,128},{4... | collective-permute-start | bytes 138248 | tf_op jit(solution)/shard_map/ppermute | solution.py:212
  24.5 1.6 %collective-permute-done = f32[90,128]{1,0:T(8,128)S(1)} collective-permute-done((f32[90,128]{1,0:T(8,128)S(1)}, f32[90,128]{1,0:T(8,128)S(1)}, u32[]{:S(2)}, u32[]{:S(2)}) %collective-permute-start) | collective-permute-done | bytes 46112 | tf_op jit(solution)/shard_map/ppermute | solution.py:212
  26.1 3.2 %collective-permute-start.1 = (f32[2,90,128]{2,1,0:T(8,128)S(1)}, f32[2,90,128]{2,1,0:T(8,128)S(1)}, u32[]{:S(2)}, u32[]{:S(2)}) collective-permute-start(f32[2,90,128]{2,1,0:T(8,128)S(1)} %pad_maximum_fusion.3), channel_id=1, source_target_pairs={{0,64},{64,0},{128,192},{192,128},{256,320},{320,256},{384,448},{4... | collective-permute-start | bytes 276488 | tf_op jit(solution)/shard_map/ppermute | solution.py:214
  29.4 2.3 %collective-permute-done.1 = f32[2,90,128]{2,1,0:T(8,128)S(1)} collective-permute-done((f32[2,90,128]{2,1,0:T(8,128)S(1)}, f32[2,90,128]{2,1,0:T(8,128)S(1)}, u32[]{:S(2)}, u32[]{:S(2)}) %collective-permute-start.1) | collective-permute-done | bytes 92192 | tf_op jit(solution)/shard_map/ppermute | solution.py:214
  31.8 4.6 %collective-permute-start.2 = (f32[2,2,90,128]{3,2,1,0:T(8,128)S(1)}, f32[2,2,90,128]{3,2,1,0:T(8,128)S(1)}, u32[]{:S(2)}, u32[]{:S(2)}) collective-permute-start(f32[2,2,90,128]{3,2,1,0:T(8,128)S(1)} %pad_maximum_fusion.2), channel_id=1, source_target_pairs={{0,192},{64,128},{128,64},{192,0},{256,448},{320,384},{384,320},{4... | collective-permute-start | bytes 552968 | tf_op jit(solution)/shard_map/ppermute | solution.py:216
  36.4 3.3 %collective-permute-done.2 = f32[2,2,90,128]{3,2,1,0:T(8,128)S(1)} collective-permute-done((f32[2,2,90,128]{3,2,1,0:T(8,128)S(1)}, f32[2,2,90,128]{3,2,1,0:T(8,128)S(1)}, u32[]{:S(2)}, u32[]{:S(2)}) %collective-permute-start.2) | collective-permute-done | bytes 184352 | tf_op jit(solution)/shard_map/ppermute | solution.py:216
  39.8 0.0 copy-start.1
  39.9 3.1 %collective-permute-start.5 = (f32[2,90,128]{2,1,0:T(8,128)S(1)}, f32[2,90,128]{2,1,0:T(8,128)S(1)}, u32[]{:S(2)}, u32[]{:S(2)}) collective-permute-start(f32[2,90,128]{2,1,0:T(8,128)S(1)} %get-tuple-element.9), channel_id=1, source_target_pairs={{0,16},{16,32},{32,48},{48,0},{1,17},{17,33},{33,49},{49,1},{2,18}... | collective-permute-start | bytes 276488 | tf_op jit(solution)/shard_map/ppermute | solution.py:226
  43.1 4.5 %collective-permute-start.4 = (f32[2,90,128]{2,1,0:T(8,128)S(1)}, f32[2,90,128]{2,1,0:T(8,128)S(1)}, u32[]{:S(2)}, u32[]{:S(2)}) collective-permute-start(f32[2,90,128]{2,1,0:T(8,128)S(1)} %get-tuple-element.10), channel_id=1, source_target_pairs={{0,32},{16,48},{32,0},{48,16},{1,33},{17,49},{33,1},{49,17},{2,34}... | collective-permute-start | bytes 276488 | tf_op jit(solution)/shard_map/ppermute | solution.py:226
  47.5 2.9 %collective-permute-start.3 = (f32[2,90,128]{2,1,0:T(8,128)S(1)}, f32[2,90,128]{2,1,0:T(8,128)S(1)}, u32[]{:S(2)}, u32[]{:S(2)}) collective-permute-start(f32[2,90,128]{2,1,0:T(8,128)S(1)} %get-tuple-element.11), channel_id=1, source_target_pairs={{0,48},{16,0},{32,16},{48,32},{1,49},{17,1},{33,17},{49,33},{2,50}... | collective-permute-start | bytes 276488 | tf_op jit(solution)/shard_map/ppermute | solution.py:226
  50.5 1.0 fusion.13.table_ref
  51.5 0.0 collective-permute-done.5
  51.5 0.0 collective-permute-done.4
  51.5 1.4 %collective-permute-done.3 = f32[2,90,128]{2,1,0:T(8,128)S(1)} collective-permute-done((f32[2,90,128]{2,1,0:T(8,128)S(1)}, f32[2,90,128]{2,1,0:T(8,128)S(1)}, u32[]{:S(2)}, u32[]{:S(2)}) %collective-permute-start.3) | collective-permute-done | bytes 92192 | tf_op jit(solution)/shard_map/ppermute | solution.py:226
  52.9 0.0 copy-done.1
  52.9 0.0 all-to-all-done.parts_ref
  52.9 1.7 %shard_map.69 = bf16[16,184,128]{2,1,0:T(8,128)(2,1)} custom-call(s32[1]{0:T(128)} %bitcast.x_ref, bf16[4,16,184,128]{3,2,1,0:T(8,128)(2,1)S(1)} %all-to-all-done.parts_ref, f32[4,2,90,128]{3,2,1,0:T(8,128)S(1)} %pad_maximum_fusion.grads_ref, bf16[512,128]{1,0:T(8,128)(2,1)S(1)} %fusion.13.table_ref), custom_call_target="tpu_custom_call" | custom-call | flops 385875968 | bytes 3014656 | tf_op jit(solution)/shard_map/pallas_call | solution.py:143
  54.6 14.9 %all-to-all-start.1 = ((bf16[16,184,128]{2,1,0:T(8,128)(2,1)}), bf16[16,184,128]{2,1,0:T(8,128)(2,1)S(1)}, u32[]{:S(2)}, u32[]{:S(2)}) async-start(bf16[16,184,128]{2,1,0:T(8,128)(2,1)} %shard_map.69), calls=%async_computation.1 | async-start | bytes 1507328 | tf_op jit(solution)/shard_map/all_to_all | solution.py:230
  69.5 0.0 copy-start.2
  69.6 1.5 %select_convert_fusion.1 = (bf16[1,512,128]{2,1,0:T(8,128)(2,1)S(1)}, bf16[1,512,128]{2,1,0:T(8,128)(2,1)S(1)}) fusion(s32[512]{0:T(512)S(1)} %get-tuple-element.21, s32[128]{0:T(128)S(1)} %fusion.33, s32[512]{0:T(512)S(1)} %get-tuple-element.20, pred[128]{0:T(512)(128)(4,1)S(1)} %get-tuple-element.23, pred[128]{0:T(512)(128)(4,1)S(1)} %get-tuple-element.22), kind=kLoop, calls=%fused_computation.30 | loop fusion | flops 983040 | bytes 267008 | tf_op jit(solution)/shard_map/convert.1
  71.1 0.0 copy-start.3
  71.2 0.0 copy-start.5
  71.2 12.3 %fusion.4.main_ref = bf16[512,1408]{1,0:T(8,128)(2,1)S(1)} fusion(s32[512]{0:T(512)S(1)} %get-tuple-element.21, s32[1408]{0:T(1024)S(1)} %fusion.31, s32[512]{0:T(512)S(1)} %get-tuple-element.20), kind=kLoop, calls=%fused_computation.5 | loop fusion | flops 8650752 | bytes 1451520 | tf_op jit(solution)/shard_map/convert_element_type | solution.py:38
  83.5 20.2 %all-to-all-done.1.rows_ref = bf16[16,184,128]{2,1,0:T(8,128)(2,1)S(1)} async-done(((bf16[16,184,128]{2,1,0:T(8,128)(2,1)}), bf16[16,184,128]{2,1,0:T(8,128)(2,1)S(1)}, u32[]{:S(2)}, u32[]{:S(2)}) %all-to-all-start.1) | async-done | bytes 753696 | tf_op jit(solution)/shard_map/all_to_all | solution.py:230
  103.6 1.7 %shard_map.70 = bf16[4,2,128,128]{3,2,1,0:T(8,128)(2,1)} custom-call(bf16[16,184,128]{2,1,0:T(8,128)(2,1)S(1)} %all-to-all-done.1.rows_ref, bf16[512,1408]{1,0:T(8,128)(2,1)S(1)} %fusion.4.main_ref, bf16[2,512,128]{2,1,0:T(8,128)(2,1)S(1)} %pad_maximum_fusion.1.tails_ref), custom_call_target="tpu_custom_call" | custom-call | flops 369098752 | bytes 2195456 | tf_op jit(solution)/shard_map/pallas_call | solution.py:184
  105.3 3.7 %all-to-all-start.2 = ((bf16[4,2,128,128]{3,2,1,0:T(8,128)(2,1)}), bf16[4,2,128,128]{3,2,1,0:T(8,128)(2,1)S(1)}, u32[]{:S(2)}, u32[]{:S(2)}) async-start(bf16[4,2,128,128]{3,2,1,0:T(8,128)(2,1)} %shard_map.70), calls=%async_computation.2 | async-start | bytes 524288 | tf_op jit(solution)/shard_map/all_to_all | solution.py:233
  109.0 0.0 copy-done
  109.0 0.2 dynamic-slice_reduce_fusion
  109.2 0.0 copy-done.2
  109.2 0.2 copy.8
  109.4 0.0 copy-done.3
  109.4 0.2 multiply_reduce_fusion
  109.6 0.7 broadcast_in_dim.48
  110.3 5.5 %all-to-all-done.2 = bf16[4,2,128,128]{3,2,1,0:T(8,128)(2,1)S(1)} async-done(((bf16[4,2,128,128]{3,2,1,0:T(8,128)(2,1)}), bf16[4,2,128,128]{3,2,1,0:T(8,128)(2,1)S(1)}, u32[]{:S(2)}, u32[]{:S(2)}) %all-to-all-start.2) | async-done | bytes 262176 | tf_op jit(solution)/shard_map/all_to_all | solution.py:233
  115.8 0.0 copy-done.5
  115.8 0.9 convert_multiply_fusion
  (18 shorter events, 0.3 us)
Async XLA Ops:
  0.6 108.4 %copy-start = (f32[8,8]{1,0:T(8,128)S(1)}, f32[8,8]{1,0:T(8,128)}, u32[]{:S(2)}) copy-start(f32[8,8]{1,0:T(8,128)} %param.8) | copy-start | bytes 772
  4.0 5.0 %copy-start.4 = (f32[1,90,128]{2,0,1:T(1,128)S(1)}, f32[1,90,128]{2,0,1:T(1,128)}, u32[]{:S(2)}) copy-start(f32[1,90,128]{2,0,1:T(1,128)} %param.6) | copy-start | bytes 138244
  4.0 48.9 %all-to-all-start = ((bf16[4,16,184,128]{3,2,1,0:T(8,128)(2,1)}), bf16[4,16,184,128]{3,2,1,0:T(8,128)(2,1)S(1)}, u32[]{:S(2)}, u32[]{:S(2)}) async-start(bf16[4,16,184,128]{3,2,1,0:T(8,128)(2,1)} %shard_map.68), calls=%async_computation | async-start | bytes 6029312 | tf_op jit(solution)/shard_map/all_to_all | solution.py:208
  9.0 17.0 %collective-permute-start = (f32[90,128]{1,0:T(8,128)S(1)}, f32[90,128]{1,0:T(8,128)S(1)}, u32[]{:S(2)}, u32[]{:S(2)}) collective-permute-start(f32[90,128]{1,0:T(8,128)S(1)} %bitcast.39), channel_id=1, source_target_pairs={{0,256},{64,320},{128,384},{192,448},{256,0},{320,64},{384,128},{4... | collective-permute-start | bytes 138248 | tf_op jit(solution)/shard_map/ppermute | solution.py:212
  26.1 5.7 %collective-permute-start.1 = (f32[2,90,128]{2,1,0:T(8,128)S(1)}, f32[2,90,128]{2,1,0:T(8,128)S(1)}, u32[]{:S(2)}, u32[]{:S(2)}) collective-permute-start(f32[2,90,128]{2,1,0:T(8,128)S(1)} %pad_maximum_fusion.3), channel_id=1, source_target_pairs={{0,64},{64,0},{128,192},{192,128},{256,320},{320,256},{384,448},{4... | collective-permute-start | bytes 276488 | tf_op jit(solution)/shard_map/ppermute | solution.py:214
  31.8 8.0 %collective-permute-start.2 = (f32[2,2,90,128]{3,2,1,0:T(8,128)S(1)}, f32[2,2,90,128]{3,2,1,0:T(8,128)S(1)}, u32[]{:S(2)}, u32[]{:S(2)}) collective-permute-start(f32[2,2,90,128]{3,2,1,0:T(8,128)S(1)} %pad_maximum_fusion.2), channel_id=1, source_target_pairs={{0,192},{64,128},{128,64},{192,0},{256,448},{320,384},{384,320},{4... | collective-permute-start | bytes 552968 | tf_op jit(solution)/shard_map/ppermute | solution.py:216
  39.8 13.1 %copy-start.1 = (f32[2,4,90,128]{3,2,0,1:T(8,128)}, f32[2,4,90,128]{3,2,0,1:T(8,128)S(1)}, u32[]{:S(2)}) copy-start(f32[2,4,90,128]{3,2,0,1:T(8,128)S(1)} %maximum_bitcast_fusion) | copy-start | bytes 1105924
  39.9 11.6 %collective-permute-start.5 = (f32[2,90,128]{2,1,0:T(8,128)S(1)}, f32[2,90,128]{2,1,0:T(8,128)S(1)}, u32[]{:S(2)}, u32[]{:S(2)}) collective-permute-start(f32[2,90,128]{2,1,0:T(8,128)S(1)} %get-tuple-element.9), channel_id=1, source_target_pairs={{0,16},{16,32},{32,48},{48,0},{1,17},{17,33},{33,49},{49,1},{2,18}... | collective-permute-start | bytes 276488 | tf_op jit(solution)/shard_map/ppermute | solution.py:226
  43.1 8.5 %collective-permute-start.4 = (f32[2,90,128]{2,1,0:T(8,128)S(1)}, f32[2,90,128]{2,1,0:T(8,128)S(1)}, u32[]{:S(2)}, u32[]{:S(2)}) collective-permute-start(f32[2,90,128]{2,1,0:T(8,128)S(1)} %get-tuple-element.10), channel_id=1, source_target_pairs={{0,32},{16,48},{32,0},{48,16},{1,33},{17,49},{33,1},{49,17},{2,34}... | collective-permute-start | bytes 276488 | tf_op jit(solution)/shard_map/ppermute | solution.py:226
  47.5 5.4 %collective-permute-start.3 = (f32[2,90,128]{2,1,0:T(8,128)S(1)}, f32[2,90,128]{2,1,0:T(8,128)S(1)}, u32[]{:S(2)}, u32[]{:S(2)}) collective-permute-start(f32[2,90,128]{2,1,0:T(8,128)S(1)} %get-tuple-element.11), channel_id=1, source_target_pairs={{0,48},{16,0},{32,16},{48,32},{1,49},{17,1},{33,17},{49,33},{2,50}... | collective-permute-start | bytes 276488 | tf_op jit(solution)/shard_map/ppermute | solution.py:226
  54.6 49.0 %all-to-all-start.1 = ((bf16[16,184,128]{2,1,0:T(8,128)(2,1)}), bf16[16,184,128]{2,1,0:T(8,128)(2,1)S(1)}, u32[]{:S(2)}, u32[]{:S(2)}) async-start(bf16[16,184,128]{2,1,0:T(8,128)(2,1)} %shard_map.69), calls=%async_computation.1 | async-start | bytes 1507328 | tf_op jit(solution)/shard_map/all_to_all | solution.py:230
  69.5 39.7 %copy-start.2 = (f32[2,4,90,128]{3,2,0,1:T(8,128)S(1)}, f32[2,4,90,128]{3,2,0,1:T(8,128)}, u32[]{:S(2)}) copy-start(f32[2,4,90,128]{3,2,0,1:T(8,128)} %copy-done.1) | copy-start | bytes 1105924
  71.1 38.3 %copy-start.3 = (f32[8,90,128]{2,0,1:T(8,128)S(1)}, f32[8,90,128]{2,0,1:T(8,128)}, u32[]{:S(2)}) copy-start(f32[8,90,128]{2,0,1:T(8,128)} %param.7) | copy-start | bytes 1105924
  71.2 44.7 %copy-start.5 = (f32[128,128]{1,0:T(8,128)S(1)}, f32[128,128]{1,0:T(8,128)}, u32[]{:S(2)}) copy-start(f32[128,128]{1,0:T(8,128)} %param.9) | copy-start | bytes 196612
  105.3 10.5 %all-to-all-start.2 = ((bf16[4,2,128,128]{3,2,1,0:T(8,128)(2,1)}), bf16[4,2,128,128]{3,2,1,0:T(8,128)(2,1)S(1)}, u32[]{:S(2)}, u32[]{:S(2)}) async-start(bf16[4,2,128,128]{3,2,1,0:T(8,128)(2,1)} %shard_map.70), calls=%async_computation.2 | async-start | bytes 524288 | tf_op jit(solution)/shard_map/all_to_all | solution.py:233
